TPU v7x, 32 devices: a whole 2x2x4 slice. The times are simulated.
32 devices in a mesh: grp: 2 (over y), res: 4 (over z), br: 2 (over core), aux: 2 (over x).
Axes of the slice: x: 2, y: 2, z: 4, core: 2. Of those that a mesh axis runs over, the one named last changes fastest.
Arguments:
- homolog_features: bfloat16 [32, 128, 256], P(('grp', 'br', 'aux'), 'res'), parts along dimension 0, may hold values from -6 to 6
- couple_features: bfloat16 [256, 128, 128], P(('grp', 'res'), ('br', 'aux')), parts along dimension 0, may hold values from -6 to 6
- symbol_ids: int32 [32, 128], P(('grp', 'br', 'aux'), 'res'), parts along dimension 0, may hold values from 0 to 22
- entry_present: int32 [32, 128], P(('grp', 'br', 'aux'), 'res'), parts along dimension 0, may hold values 0 or 1
- amino_present: int32 [256], P('grp'), parts along dimension 0, may hold values 0 or 1
- symbol_lookup_matrix: bfloat16 [23, 256], replicated, may hold values from -3 to 3
- horizontal_entry_matrix: bfloat16 [256, 1024], replicated, may hold values from -0.375 to 0.375
- couple_logit_matrix: bfloat16 [128, 8], replicated, may hold values from -40 to 40, as said below
- horizontal_exit_matrix: bfloat16 [256, 256], replicated, may hold values from -0.375 to 0.375
- vertical_entry_matrix: bfloat16 [256, 1024], replicated, may hold values from -0.375 to 0.375
- vertical_exit_matrix: bfloat16 [256, 256], replicated, may hold values from -0.375 to 0.375
- feedforward_first_matrix: bfloat16 [256, 1024], replicated, may hold values from -0.375 to 0.375
- feedforward_second_matrix: bfloat16 [1024, 256], replicated, may hold values from -0.1875 to 0.1875
- trimul_entry_matrix: bfloat16 [128, 640], replicated, may hold values from -0.5 to 0.5
- trimul_exit_matrix: bfloat16 [128, 128], replicated, may hold values from -0.5 to 0.5
Outputs:
- alignment_output: bfloat16 [32, 128, 256], P(('grp', 'br', 'aux'), 'res'), parts along dimension 0
- pair_output: bfloat16 [256, 128, 128], P(('grp', 'res'), ('br', 'aux')), parts along dimension 0
There are 2 independent parts, one for each index of `grp`. A program takes and returns all parts, laid end to end along the dimension named above; an argument that names none is the same for every part. Nothing has to cross between parts.
Inputs may be any that keep to these rules, and one draw needn't show every extreme that they name: `couple_logit_matrix`: a projection of the 128 pair channels onto the 8 heads.
All inputs are finite; a program needn't handle non-finite values. No bound on the sum of `entry_present` on one device may be relied on, other than what follows from the above.
Results may differ from a plain program's by a relative error of at most 0.008.
Values may be sent and summed in bfloat16 or wider, within the bound.
No kernel may reach another device: no remote copies, remote signals or barrier semaphores. Data moves between devices by JAX's collectives and lax.ppermute only.
A program may use at most 64 MiB of HBM per device.

v0:
```python
import jax
import jax.numpy as jnp
from jax import lax
from jax.sharding import PartitionSpec as P

epsilon = 1e-05
masked_fill_value = 1000000000.0


def normalize(inputs):
    values = inputs.astype(jnp.float32)
    average = jnp.mean(values, axis=-1, keepdims=True)
    centred = values - average
    variance = jnp.mean(centred * centred, axis=-1, keepdims=True)
    return centred * lax.rsqrt(variance + epsilon)


def apply_projection(row_block, weight):
    flattened = row_block.reshape(-1, row_block.shape[-1])
    result = jnp.dot(flattened, weight, preferred_element_type=jnp.float32)
    return result.reshape(row_block.shape[:-1] + (weight.shape[1],))


def merge_block(partial_state, scores, value_rows, value_form):
    running_max, running_sum, weighted = partial_state
    new_max = jnp.maximum(running_max, jnp.max(scores, axis=-1))
    powers = jnp.exp(scores - new_max[..., None])
    running_sum = jnp.sum(powers, axis=-1)
    update = jnp.einsum(
        value_form, powers.astype(jnp.bfloat16), value_rows, preferred_element_type=jnp.float32
    )
    weighted = update
    return (new_max, running_sum, weighted)


def finish_block(partial_state, axes_order):
    running_max, running_sum, weighted = partial_state
    return weighted / jnp.transpose(running_sum, axes_order)[..., None]


def on_device(
    homolog_features,
    couple_features,
    symbol_ids,
    entry_present,
    amino_present,
    symbol_lookup_matrix,
    horizontal_entry_matrix,
    couple_logit_matrix,
    horizontal_exit_matrix,
    vertical_entry_matrix,
    vertical_exit_matrix,
    feedforward_first_matrix,
    feedforward_second_matrix,
    trimul_entry_matrix,
    trimul_exit_matrix,
):
    homolog_lines, amino_positions, feature_extent = homolog_features.shape
    heads_number = couple_logit_matrix.shape[1]
    head_width = feature_extent // heads_number
    head_scale = head_width ** (-0.5)
    pair_width = couple_features.shape[2]
    token_class_count = symbol_lookup_matrix.shape[0]
    indicator_symbols = (
        symbol_ids[..., None] == jnp.arange(token_class_count, dtype=jnp.int32)[None, None, :]
    ).astype(jnp.bfloat16)
    symbol_vectors = homolog_features.astype(jnp.float32) + jnp.einsum(
        "zas,sv->zav", indicator_symbols, symbol_lookup_matrix, preferred_element_type=jnp.float32
    )
    valid_bfloat = entry_present.astype(jnp.bfloat16)
    normed_first = normalize(symbol_vectors).astype(jnp.bfloat16)
    horizontal_combined = apply_projection(normed_first, horizontal_entry_matrix)
    horizontal_queries = (
        horizontal_combined[..., :feature_extent]
        .astype(jnp.bfloat16)
        .reshape(homolog_lines, amino_positions, heads_number, head_width)
    )
    horizontal_sigmoid = jax.nn.sigmoid(horizontal_combined[..., 3 * feature_extent :])
    pair_norm = normalize(couple_features).astype(jnp.bfloat16)
    bias_tile = jnp.einsum(
        "ijc,ch->hij", pair_norm, couple_logit_matrix, preferred_element_type=jnp.float32
    )
    pair_bias = lax.all_gather(bias_tile, ("br", "aux"), axis=2, tiled=True)
    row_init = (
        jnp.full((homolog_lines, heads_number, amino_positions), -1e30, jnp.float32),
        jnp.zeros((homolog_lines, heads_number, amino_positions), jnp.float32),
        jnp.zeros((homolog_lines, amino_positions, heads_number, head_width), jnp.float32),
    )
    partial_rows = lax.all_gather(normed_first, "res", axis=1, tiled=True)
    valid_part = lax.all_gather(valid_bfloat, "res", axis=1, tiled=True)
    key_count = partial_rows.shape[1]
    key_value_rows = apply_projection(
        partial_rows, horizontal_entry_matrix[:, feature_extent : 3 * feature_extent]
    )
    key_rows = (
        key_value_rows[..., :feature_extent]
        .astype(jnp.bfloat16)
        .reshape(homolog_lines, key_count, heads_number, head_width)
    )
    value_rows = (
        key_value_rows[..., feature_extent:]
        .astype(jnp.bfloat16)
        .reshape(homolog_lines, key_count, heads_number, head_width)
    )
    scores = (
        jnp.einsum(
            "sihd,sjhd->shij", horizontal_queries, key_rows, preferred_element_type=jnp.float32
        )
        * head_scale
    )
    scores = (
        scores
        + pair_bias[None]
        + (masked_fill_value * (valid_part.astype(jnp.float32) - 1.0))[:, None, None, :]
    )
    row_state = merge_block(row_init, scores, value_rows, "shij,sjhd->sihd")
    horizontal_context = finish_block(row_state, (0, 2, 1))
    horizontal_result = (
        horizontal_sigmoid
        * horizontal_context.reshape(homolog_lines, amino_positions, feature_extent)
    ).astype(jnp.bfloat16)
    after_row = symbol_vectors + apply_projection(horizontal_result, horizontal_exit_matrix)
    normed_second = normalize(after_row).astype(jnp.bfloat16)
    vertical_combined = apply_projection(normed_second, vertical_entry_matrix)
    vertical_queries = (
        vertical_combined[..., :feature_extent]
        .astype(jnp.bfloat16)
        .reshape(homolog_lines, amino_positions, heads_number, head_width)
    )
    column_key_rows = vertical_combined[..., feature_extent : 2 * feature_extent].astype(
        jnp.bfloat16
    )
    column_value_rows = vertical_combined[..., 2 * feature_extent : 3 * feature_extent].astype(
        jnp.bfloat16
    )
    vertical_sigmoid = jax.nn.sigmoid(vertical_combined[..., 3 * feature_extent :])
    col_init = (
        jnp.full((amino_positions, heads_number, homolog_lines), -1e30, jnp.float32),
        jnp.zeros((amino_positions, heads_number, homolog_lines), jnp.float32),
        jnp.zeros((homolog_lines, amino_positions, heads_number, head_width), jnp.float32),
    )
    key_part = lax.all_gather(column_key_rows, ("br", "aux"), axis=0, tiled=True)
    value_part = lax.all_gather(column_value_rows, ("br", "aux"), axis=0, tiled=True)
    valid_part = lax.all_gather(valid_bfloat, ("br", "aux"), axis=0, tiled=True)
    key_count = key_part.shape[0]
    key_rows = key_part.reshape(key_count, amino_positions, heads_number, head_width)
    value_rows = value_part.reshape(key_count, amino_positions, heads_number, head_width)
    scores = (
        jnp.einsum(
            "srhd,trhd->rhst", vertical_queries, key_rows, preferred_element_type=jnp.float32
        )
        * head_scale
    )
    scores = (
        scores + (masked_fill_value * (valid_part.astype(jnp.float32) - 1.0)).T[:, None, None, :]
    )
    col_state = merge_block(col_init, scores, value_rows, "rhst,trhd->srhd")
    vertical_context = finish_block(col_state, (2, 0, 1))
    vertical_result = (
        vertical_sigmoid * vertical_context.reshape(homolog_lines, amino_positions, feature_extent)
    ).astype(jnp.bfloat16)
    after_column_update = after_row + apply_projection(vertical_result, vertical_exit_matrix)
    normed_third = normalize(after_column_update).astype(jnp.bfloat16)
    hidden_units = jax.nn.relu(apply_projection(normed_third, feedforward_first_matrix)).astype(
        jnp.bfloat16
    )
    alignment_output = (
        after_column_update + apply_projection(hidden_units, feedforward_second_matrix)
    ).astype(jnp.bfloat16)
    pair_rows_dev = couple_features.shape[0]
    pair_cols_dev = couple_features.shape[1]
    valid_res = amino_present.astype(jnp.float32)
    row_valid = lax.dynamic_slice_in_dim(
        valid_res, lax.axis_index("res") * pair_rows_dev, pair_rows_dev
    )
    col_valid = lax.dynamic_slice_in_dim(
        valid_res, lax.axis_index(("br", "aux")) * pair_cols_dev, pair_cols_dev
    )
    pair_valid = row_valid[:, None] * col_valid[None, :]
    projected = jnp.einsum(
        "ijc,cd->dij",
        pair_norm,
        trimul_entry_matrix[:, : 4 * pair_width],
        preferred_element_type=jnp.float32,
    )
    left_side = (
        jax.nn.sigmoid(projected[pair_width : 2 * pair_width]) * projected[:pair_width] * pair_valid
    ).astype(jnp.bfloat16)
    right_side = (
        jax.nn.sigmoid(projected[3 * pair_width :])
        * projected[2 * pair_width : 3 * pair_width]
        * pair_valid
    ).astype(jnp.bfloat16)
    out_gate = jax.nn.sigmoid(apply_projection(pair_norm, trimul_entry_matrix[:, 4 * pair_width :]))
    left_chan, right_chan = (
        lax.all_to_all(left_side, "res", split_axis=0, concat_axis=1, tiled=True),
        lax.all_to_all(right_side, "res", split_axis=0, concat_axis=1, tiled=True),
    )
    product = jnp.einsum(
        "cki,ckj->cij",
        lax.all_gather(left_chan, ("br", "aux"), axis=2, tiled=True),
        right_chan,
        preferred_element_type=jnp.float32,
    ).astype(jnp.bfloat16)
    swapped_back = lax.all_to_all(product, "res", split_axis=1, concat_axis=0, tiled=True)
    normed_final = normalize(swapped_back.transpose(1, 2, 0)).astype(jnp.bfloat16)
    pair_output = (
        couple_features.astype(jnp.float32)
        + out_gate * apply_projection(normed_final, trimul_exit_matrix)
    ).astype(jnp.bfloat16)
    return (alignment_output, pair_output)


def solution(mesh):
    return jax.shard_map(
        on_device,
        mesh=mesh,
        in_specs=(
            P(("grp", "br", "aux"), "res", None),
            P(("grp", "res"), ("br", "aux"), None),
            P(("grp", "br", "aux"), "res"),
            P(("grp", "br", "aux"), "res"),
            P("grp"),
            P(),
            P(),
            P(),
            P(),
            P(),
            P(),
            P(),
            P(),
            P(),
            P(),
        ),
        out_specs=(P(("grp", "br", "aux"), "res", None), P(("grp", "res"), ("br", "aux"), None)),
        check_vma=False,
    )
```

profile of v0, /device:TPU:0, one launch (start us, length us, event | category | flops | bytes accessed | tf_op | source)
XLA Modules:
  0.0 149.0 jit_solution(16225407068456731938)
XLA Ops:
  9.1 1.3 fusion.18
  10.6 1.5 convolution_bitcast_fusion
  12.4 1.4 copy.72
  13.9 1.7 %reshape.203 = bf16[4,2,16384]{2,1,0:T(2,128)(2,1)} reshape(bf16[128,32,32]{2,1,0:T(8,128)(2,1)S(1)} %copy.72) | data formatting | bytes 524288
  15.5 6.4 %all-to-all-start = ((bf16[4,2,16384]{2,1,0:T(2,128)(2,1)}), bf16[4,2,16384]{2,1,0:T(2,128)(2,1)S(1)}, u32[]{:S(2)}, u32[]{:S(2)}) async-start(bf16[4,2,16384]{2,1,0:T(2,128)(2,1)} %reshape.203), calls=%async_computation | async-start | bytes 524288 | tf_op jit(solution)/shard_map/all_to_all | solution.py:196
  22.0 1.4 copy.74
  23.4 1.7 %reshape.205 = bf16[4,2,16384]{2,1,0:T(2,128)(2,1)} reshape(bf16[128,32,32]{2,1,0:T(8,128)(2,1)S(1)} %copy.74) | data formatting | bytes 524288
  25.7 14.5 %all_gather.21 = bf16[4,128,256]{2,1,0:T(8,128)(2,1)S(1)} all-gather(bf16[4,32,256]{2,1,0:T(8,128)(2,1)S(1)} %multiply_convert_fusion.4), channel_id=1, replica_groups=mesh['grp'=2,'res'=4,'br'=2,'aux'=2] {'res'}, dimensions={1}, use_global_device_ids=true | all-gather | bytes 327680 | tf_op jit(solution)/shard_map/all_gather | solution.py:89
  41.9 13.0 %all_gather.22 = f32[8,32,128]{1,0,2:T(8,128)S(1)} all-gather(f32[8,32,32]{1,0,2:T(8,128)S(1)} %copy.63), channel_id=1, replica_groups=mesh['grp'=2,'res'=4,'br'=2,'aux'=2] {'br','aux'}, dimensions={2}, use_global_device_ids=true | all-gather | bytes 163840 | tf_op jit(solution)/shard_map/all_gather | solution.py:83
  55.7 11.0 %all-gather = bf16[4,32,4]{1,2,0:T(4,128)(2,1)S(1)} all-gather(bf16[1,32,4]{1,2,0:T(4,128)(2,1)S(1)} %get-tuple-element.10), channel_id=1, replica_groups=mesh['grp'=2,'res'=4,'br'=2,'aux'=2] {'res'}, dimensions={0}, use_global_device_ids=true | all-gather | bytes 1280 | tf_op jit(solution)/shard_map/all_gather | solution.py:90
  69.9 10.6 %all_gather.25 = bf16[16,32,256]{2,1,0:T(8,128)(2,1)S(1)} all-gather(bf16[4,32,256]{2,1,0:T(8,128)(2,1)S(1)} %get-tuple-element.7), channel_id=1, replica_groups=mesh['grp'=2,'res'=4,'br'=2,'aux'=2] {'br','aux'}, dimensions={0}, use_global_device_ids=true | all-gather | bytes 327680 | tf_op jit(solution)/shard_map/all_gather | solution.py:142
  81.1 6.1 %all-gather.1 = bf16[4,4,32]{2,1,0:T(4,128)(2,1)S(1)} all-gather(bf16[1,4,32]{2,1,0:T(4,128)(2,1)S(1)} %copy-done.13), channel_id=1, replica_groups=mesh['grp'=2,'res'=4,'br'=2,'aux'=2] {'br','aux'}, dimensions={0}, use_global_device_ids=true | all-gather | bytes 1280 | tf_op jit(solution)/shard_map/all_gather | solution.py:144
  87.2 2.4 %fusion.95 = (f32[32,8,4]{2,1,0:T(8,128)}, f32[32,8,4,16]{3,2,1,0:T(4,128)}) fusion(f32[32,16]{1,0:T(8,128)S(1)} %bitcast.117, bf16[16,32,8,32]{3,2,1,0:T(8,128)(2,1)S(1)} %reshape.173, bf16[4,32,8,32]{3,2,1,0:T(8,128)(2,1)S(1)} %reshape.172), kind=kOutput, calls=%fused_computation.139 | convolution fusion | flops 1096704 | bytes 399360 | tf_op jit(solution)/shard_map/srhd,trhd->rhst/dot_general | solution.py:149
  89.7 3.4 %all-to-all-start.1 = ((bf16[4,2,16384]{2,1,0:T(2,128)(2,1)}), bf16[4,2,16384]{2,1,0:T(2,128)(2,1)S(1)}, u32[]{:S(2)}, u32[]{:S(2)}) async-start(bf16[4,2,16384]{2,1,0:T(2,128)(2,1)} %reshape.205), calls=%async_computation.1 | async-start | bytes 524288 | tf_op jit(solution)/shard_map/all_to_all | solution.py:197
  95.8 11.0 %all_gather.24 = bf16[16,32,256]{2,1,0:T(8,128)(2,1)S(1)} all-gather(bf16[4,32,256]{2,1,0:T(8,128)(2,1)S(1)} %get-tuple-element.8), channel_id=1, replica_groups=mesh['grp'=2,'res'=4,'br'=2,'aux'=2] {'br','aux'}, dimensions={0}, use_global_device_ids=true | all-gather | bytes 327680 | tf_op jit(solution)/shard_map/all_gather | solution.py:143
  111.5 2.0 %fusion.3 = f32[32,32,128]{2,1,0:T(8,128)} fusion(bf16[32,32,128]{2,1,0:T(8,128)(2,1)S(1)} %copy-done.1, f32[32,32]{1,0:T(8,128)S(1)} %copy-done.9, f32[32,32]{1,0:T(8,128)S(1)} %broadcast_multiply_fusion.2, bf16[128,640]{1,0:T(8,128)(2,1)} %param.28), kind=kOutput, calls=%fused_computation.9 | convolution fusion | flops 34471936 | bytes 827392 | tf_op jit(solution)/shard_map/dot_general | solution.py:20
  115.4 1.9 %convolution_convert_fusion.1 = bf16[32,128,32]{1,2,0:T(8,128)(2,1)S(1)} fusion(bf16[32,128,128]{1,2,0:T(8,128)(2,1)} %all-gather.4.cloned.1.call-done, bf16[32,128,32]{1,2,0:T(8,128)(2,1)S(1)} %all_to_all.40), kind=kOutput, calls=%fused_computation.20 | convolution fusion | flops 33685504 | bytes 1572864 | tf_op jit(solution)/shard_map/cki,ckj->cij/dot_general | solution.py:199
  117.3 1.5 copy.76
  118.8 1.7 %reshape.207 = bf16[4,2,16384]{2,1,0:T(2,128)(2,1)} reshape(bf16[128,32,32]{2,1,0:T(8,128)(2,1)S(1)} %bitcast.106) | data formatting | bytes 524288
  120.5 4.8 %all-to-all-start.2 = ((bf16[4,2,16384]{2,1,0:T(2,128)(2,1)}), bf16[4,2,16384]{2,1,0:T(2,128)(2,1)S(1)}, u32[]{:S(2)}, u32[]{:S(2)}) async-start(bf16[4,2,16384]{2,1,0:T(2,128)(2,1)} %reshape.207), calls=%async_computation.2 | async-start | bytes 524288 | tf_op jit(solution)/shard_map/all_to_all | solution.py:205
  126.4 7.8 %all-to-all-done.2 = bf16[4,2,16384]{2,1,0:T(2,128)(2,1)S(1)} async-done(((bf16[4,2,16384]{2,1,0:T(2,128)(2,1)}), bf16[4,2,16384]{2,1,0:T(2,128)(2,1)S(1)}, u32[]{:S(2)}, u32[]{:S(2)}) %all-to-all-start.2) | async-done | bytes 262176 | tf_op jit(solution)/shard_map/all_to_all | solution.py:205
  134.7 1.6 %convert_bitcast_fusion = f32[4,32,32,32]{3,1,2,0:T(8,128)} fusion(bf16[32,4,32,32]{3,0,2,1:T(8,128)(2,1)S(1)} %bitcast.105), kind=kLoop, calls=%fused_computation | loop fusion | flops 131072 | bytes 786432 | tf_op jit(solution)/shard_map/convert_element_type | solution.py:11
  136.3 2.1 %copy.77 = f32[4,32,32,32]{1,0,3,2:T(4,128)S(1)} copy(f32[4,32,32,32]{3,1,2,0:T(8,128)} %convert_bitcast_fusion) | data formatting | bytes 1048576 | tf_op jit(solution)/shard_map/convert_element_type | solution.py:11
  139.9 2.2 %fusion.9 = bf16[32,32,128]{2,1,0:T(8,128)(2,1)} fusion(f32[32,32,128]{2,1,0:T(8,128)} %fusion.3, bf16[32,32,128]{2,1,0:T(8,128)(2,1)S(1)} %copy-done.1, f32[128,32,32]{0,2,1:T(8,128)S(1)} %reshape.175, f32[32,32]{1,0:T(8,128)S(1)} %add_rsqrt_fusion, f32[32,32]{1,0:T(8,128)S(1)} %broadcast_multiply_fusion.1, bf16[128,128]{1,0:T(8,128)(2,1)S(1)} %copy-done.11), kind=kOutput, calls=%fused_computation.19 | convolution fusion | flops 34471936 | bytes 1613824 | tf_op jit(solution)/shard_map/dot_general | solution.py:20
  (107 shorter events, 21.3 us)
Async XLA Ops:
  7.2 61.6 %copy-start = (bf16[256,1024]{1,0:T(8,128)(2,1)S(1)}, bf16[256,1024]{1,0:T(8,128)(2,1)}, u32[]{:S(2)}) copy-start(bf16[256,1024]{1,0:T(8,128)(2,1)} %param.24) | copy-start | bytes 1572868
  10.4 30.7 %copy-start.8 = (f32[32,32]{1,0:T(8,128)}, f32[32,32]{1,0:T(8,128)S(1)}, u32[]{:S(2)}) copy-start(f32[32,32]{1,0:T(8,128)S(1)} %add_rsqrt_fusion.1) | copy-start | bytes 12292
  13.8 11.3 %copy-start.10 = (bf16[4,32,256]{2,1,0:T(8,128)(2,1)S(1)}, bf16[4,32,256]{2,1,0:T(8,128)(2,1)}, u32[]{:S(2)}) copy-start(bf16[4,32,256]{2,1,0:T(8,128)(2,1)} %param.15) | copy-start | bytes 196612
  13.8 11.3 %copy-start.12 = (bf16[23,256]{1,0:T(8,128)(2,1)S(1)}, bf16[23,256]{1,0:T(8,128)(2,1)}, u32[]{:S(2)}) copy-start(bf16[23,256]{1,0:T(8,128)(2,1)} %param.20) | copy-start | bytes 35332
  13.9 11.2 %copy-start.15 = (s32[4,32]{1,0:T(4,128)S(1)}, s32[4,32]{1,0:T(4,128)}, u32[]{:S(2)}) copy-start(s32[4,32]{1,0:T(4,128)} %param.17) | copy-start | bytes 1540
  15.5 24.7 %copy-start.2 = (bf16[256,1024]{1,0:T(8,128)(2,1)S(1)}, bf16[256,1024]{1,0:T(8,128)(2,1)}, u32[]{:S(2)}) copy-start(bf16[256,1024]{1,0:T(8,128)(2,1)} %param.21) | copy-start | bytes 1572868
  15.5 74.1 %all-to-all-start = ((bf16[4,2,16384]{2,1,0:T(2,128)(2,1)}), bf16[4,2,16384]{2,1,0:T(2,128)(2,1)S(1)}, u32[]{:S(2)}, u32[]{:S(2)}) async-start(bf16[4,2,16384]{2,1,0:T(2,128)(2,1)} %reshape.203), calls=%async_computation | async-start | bytes 524288 | tf_op jit(solution)/shard_map/all_to_all | solution.py:196
  40.2 1.0 copy-start.1
  40.2 1.0 copy-start.18
  40.7 14.3 %copy-start.14 = (s32[4,32]{1,0:T(4,128)S(1)}, s32[4,32]{1,0:T(4,128)}, u32[]{:S(2)}) copy-start(s32[4,32]{1,0:T(4,128)} %param.18) | copy-start | bytes 1540
  67.2 1.1 copy-start.16
  68.6 1.3 copy-start.6
  68.6 12.5 %copy-start.13 = (bf16[1,4,32]{2,1,0:T(4,128)(2,1)S(1)}, bf16[1,4,32]{2,1,0:T(4,128)(2,1)}, u32[]{:S(2)}) copy-start(bf16[1,4,32]{2,1,0:T(4,128)(2,1)} %get-tuple-element.9) | copy-start | bytes 772
  89.7 23.9 %all-to-all-start.1 = ((bf16[4,2,16384]{2,1,0:T(2,128)(2,1)}), bf16[4,2,16384]{2,1,0:T(2,128)(2,1)S(1)}, u32[]{:S(2)}, u32[]{:S(2)}) async-start(bf16[4,2,16384]{2,1,0:T(2,128)(2,1)} %reshape.205), calls=%async_computation.1 | async-start | bytes 524288 | tf_op jit(solution)/shard_map/all_to_all | solution.py:197
  93.1 22.3 %all-gather.4.cloned.1.call-start = ((), (), s32[]{:S(2)}) async-start(), calls=%async_computation.3 | async-start | bytes 1310720 | tf_op jit(solution)/shard_map/all_gather | solution.py:201
  95.8 12.4 %copy-start.3 = (f32[32,8,4,16]{3,2,1,0:T(4,128)S(1)}, f32[32,8,4,16]{3,2,1,0:T(4,128)}, u32[]{:S(2)}) copy-start(f32[32,8,4,16]{3,2,1,0:T(4,128)} %get-tuple-element.22) | copy-start | bytes 196612
  108.8 1.3 copy-start.7
  108.8 1.3 copy-start.17
  109.9 1.6 %copy-start.9 = (f32[32,32]{1,0:T(8,128)S(1)}, f32[32,32]{1,0:T(8,128)}, u32[]{:S(2)}) copy-start(f32[32,32]{1,0:T(8,128)} %copy-done.8) | copy-start | bytes 12292
  115.3 10.0 %copy-start.4 = (bf16[1024,256]{1,0:T(8,128)(2,1)S(1)}, bf16[1024,256]{1,0:T(8,128)(2,1)}, u32[]{:S(2)}) copy-start(bf16[1024,256]{1,0:T(8,128)(2,1)} %param.27) | copy-start | bytes 1572868
  115.4 9.9 %copy-start.5 = (bf16[256,1024]{1,0:T(8,128)(2,1)S(1)}, bf16[256,1024]{1,0:T(8,128)(2,1)}, u32[]{:S(2)}) copy-start(bf16[256,1024]{1,0:T(8,128)(2,1)} %param.26) | copy-start | bytes 1572868
  120.5 13.7 %all-to-all-start.2 = ((bf16[4,2,16384]{2,1,0:T(2,128)(2,1)}), bf16[4,2,16384]{2,1,0:T(2,128)(2,1)S(1)}, u32[]{:S(2)}, u32[]{:S(2)}) async-start(bf16[4,2,16384]{2,1,0:T(2,128)(2,1)} %reshape.207), calls=%async_computation.2 | async-start | bytes 524288 | tf_op jit(solution)/shard_map/all_to_all | solution.py:205
  138.4 1.5 %copy-start.11 = (bf16[128,128]{1,0:T(8,128)(2,1)S(1)}, bf16[128,128]{1,0:T(8,128)(2,1)}, u32[]{:S(2)}) copy-start(bf16[128,128]{1,0:T(8,128)(2,1)} %param.29) | copy-start | bytes 98308
Sparse Core Ops, SparseCore 0:
  96.1 18.3 all-gather.3
where the time goes:
time: 150 us; the launch traced here: 149 us
  blocking collectives  66.1 us (44%)
  local copies, waits for them, and re-layouts  19.6 us (13%)
  matrix products  16.8 us (11%)
  starting transfers between devices  14.9 us (10%)
  between operations  14.6 us (10%)
  other arithmetic  9.09 us (6%)
  waiting for transfers between devices  7.83 us (5%)
    all_gather x1, blocking collectives, on_device(): partial_rows = lax.all_gather(normed_first, 'res', axis=1, tiled=True)  14.5 us
    all_gather x1, blocking collectives, on_device(): pair_bias = lax.all_gather(bias_tile, ('br', 'aux'), axis=2, tiled=True)  13 us
    all_gather x1, blocking collectives, on_device(): valid_part = lax.all_gather(valid_bfloat, 'res', axis=1, tiled=True)  11 us
    all_gather x1, blocking collectives, on_device(): lax.all_gather(column_value_rows, ('br', 'aux'), axis=0, tiled=True)  11 us
    all_gather x1, blocking collectives, on_device(): lax.all_gather(column_key_rows, ('br', 'aux'), axis=0, tiled=True)  10.6 us
    dot_general x8, matrix products, apply_projection(): result = jnp.dot(flattened, weight, preferred_element_type=jnp.float32)  8.37 us
    all_to_all x1, waiting for transfers between devices, on_device(): lax.all_to_all(product, 'res', split_axis=1, concat_axis=0, tiled=True)  7.79 us
    unnamed x44, local copies, waits for them, and re-layouts  6.59 us
  transfers between devices with their start and end apart: 4, of which 1 were waited for; matrix products, arithmetic and copies ran while one was open for 15% of the time, Pallas kernels for 0%

commit v1 on v0

v1 whole, which is shorter than its diff:
```python
import functools

import jax
import jax.numpy as jnp
from jax import lax
from jax.experimental import pallas as pl
from jax.experimental.pallas import tpu as pltpu
from jax.sharding import PartitionSpec as P

epsilon = 1e-05
masked_fill_value = 1000000000.0
bf16 = jnp.bfloat16
f32 = jnp.float32
SIDE = ("br", "aux")
ALL = ("res", "br", "aux")
NT = (((1,), (1,)), ((), ()))
TN = (((0,), (0,)), ((), ()))


def normalize(values):
    average = jnp.mean(values, axis=-1, keepdims=True)
    centred = values - average
    variance = jnp.mean(centred * centred, axis=-1, keepdims=True)
    return centred * lax.rsqrt(variance + epsilon)


def sigmoid(values):
    return 1.0 / (1.0 + jnp.exp(-values))


def dot(left, right):
    return jnp.dot(left, right, preferred_element_type=f32)


def iota(shape, dim):
    return lax.broadcasted_iota(jnp.int32, shape, dim)


def round_up(count, step):
    return -(-count // step) * step


def side_index():
    return lax.axis_index("br") * lax.axis_size("aux") + lax.axis_index("aux")


def embed_kernel(features, ids, present, table, embedded, payload, tail):
    lines, positions, depth = features.shape
    kinds = table.shape[0]
    rows = lines * positions
    for line in range(lines):
        onehot = (iota((kinds, positions), 0) == ids[line : line + 1, :]).astype(bf16)
        token = lax.dot_general(onehot, table[...], TN, preferred_element_type=f32)
        values = features[line].astype(f32) + token
        span = slice(line * positions, (line + 1) * positions)
        embedded[span, :] = values
        payload[span, :] = normalize(values).astype(bf16)
    tail[...] = jnp.zeros_like(tail)
    tail[:lines, :positions] = present[...].astype(f32)
    payload[rows:, :] = tail[...].astype(bf16)


def attend(queries, keys, values, bias, heads):
    count, depth = queries.shape
    width = depth // heads
    own = (iota((heads, depth), 1) // width == iota((heads, depth), 0)).astype(f32)
    spread = (queries[:, None, :] * own[None]).reshape(count * heads, depth).astype(bf16)
    scores = lax.dot_general(spread, keys, NT, preferred_element_type=f32) * width ** (-0.5)
    scores = bias(scores)
    powers = jnp.exp(scores - jnp.max(scores, axis=-1, keepdims=True))
    weights = (powers * (1.0 / jnp.sum(powers, axis=-1, keepdims=True))).astype(bf16)
    mixed = dot(weights, values).reshape(count, heads, depth)
    return jnp.sum(mixed * own[None], axis=1)


def row_kernel(relative, side_relative, sides, lines, positions, *refs):
    terms, refs = refs[:sides], refs[sides:]
    blocks = refs[: len(refs) - 10]
    own, embedded, entry, leave, after, payload, bias, keys, values, mix = refs[len(refs) - 10 :]
    depth = leave.shape[0]
    heads = bias.shape[0] // positions
    rows = lines * positions
    key_count = bias.shape[1]
    me = lax.axis_index("res")
    lanes = terms[0].shape[1]
    per = lanes // positions
    side = side_index()
    sums = []
    for term in terms:
        held = positions * heads // per
        base = term.shape[0] - 3 * held
        sums.append(
            term[base : base + held, :].astype(f32)
            + term[base + held : base + 2 * held, :].astype(f32)
            + term[base + 2 * held :, :].astype(f32)
        )
    place = iota((heads, key_count), 1) // positions
    for line in range(positions):
        total = jnp.zeros((heads, key_count), f32)
        for slot, values_of in enumerate(sums):
            source = (side ^ slot) if side_relative else slot
            part = values_of[(line // per) * heads : (line // per + 1) * heads]
            part = pltpu.roll(part, ((source - line % per + lanes) % per) * positions, 1)
            part = jnp.concatenate([part] * (key_count // lanes), axis=1)
            total = jnp.where(place == source, part, total)
        bias[line * heads : (line + 1) * heads, :] = total
    penalty = jnp.zeros((payload.shape[0] - rows, key_count), f32)
    for slot, block in enumerate(blocks):
        source = (me ^ slot) if relative else slot
        block = rows_of(block, payload.shape[0], depth)
        place = iota((depth, key_count), 0)
        place = (place < positions) & (iota((depth, key_count), 1) == place + source * positions)
        penalty += dot(block[rows:, :], place.astype(bf16))
        projected = dot(block[:rows, :], entry[:, depth : 3 * depth]).astype(bf16)
        for line in range(lines):
            span = pl.ds(pl.multiple_of(source * positions, positions), positions)
            part = projected[line * positions : (line + 1) * positions]
            keys[line, span, :] = part[:, :depth]
            values[line, span, :] = part[:, depth:]
    penalty = masked_fill_value * (penalty - 1.0)
    normed = own[:rows, :]
    queries = dot(normed, entry[:, :depth]).astype(bf16).astype(f32)
    gate = sigmoid(dot(normed, entry[:, 3 * depth :]))
    for line in range(lines):
        span = slice(line * positions, (line + 1) * positions)
        fixed = lambda scores, line=line: scores + bias[...] + penalty[line : line + 1, :]
        mixed = attend(queries[span], keys[line], values[line], fixed, heads)
        mix[span, :] = (gate[span] * mixed).astype(bf16)
    result = embedded[...] + dot(mix[...], leave[...])
    after[...] = result
    payload[:rows, :] = normalize(result).astype(bf16)
    payload[rows:, :] = own[rows:, :]


def column_kernel(lines, positions, group, heads, *refs):
    blocks = refs[: len(refs) - 10]
    own, after, entry, leave, first, second, output, keys, values, mix = refs[len(refs) - 10 :]
    depth = leave.shape[0]
    rows = lines * positions
    presence = []
    for slot, block in enumerate(blocks):
        projected = dot(block[:rows, :], entry[:, depth : 3 * depth])
        span = slice(slot * lines, (slot + 1) * lines)
        keys[span] = projected[:, :depth].reshape(lines, positions, depth)
        values[span] = projected[:, depth:].reshape(lines, positions, depth)
        presence.append(block[rows:, :])
    tail = presence[0].shape[0]
    presence = jnp.concatenate(presence, axis=0)
    normed = own[:rows, :]
    queries = dot(normed, entry[:, :depth]).astype(bf16).astype(f32)
    queries = queries.reshape(lines, positions, depth)
    gate = sigmoid(dot(normed, entry[:, 3 * depth :])).reshape(lines, positions, depth)
    key_count = len(blocks) * lines * group
    row = iota((presence.shape[0], key_count), 0)
    lane = iota((presence.shape[0], key_count), 1)
    chosen = (row % tail < lines) & ((row // tail) * lines + row % tail == lane // group)
    shape = (lines * group * heads, key_count)
    same = (iota(shape, 0) // heads) % group == iota(shape, 1) % group
    for start in range(0, positions, group):
        span = slice(start, start + group)
        pick = (iota((depth, key_count), 0) == start + iota((depth, key_count), 1) % group)
        held = dot(presence, pick.astype(bf16))
        held = jnp.sum(jnp.where(chosen, held, 0.0), axis=0, keepdims=True)
        penalty = masked_fill_value * (held - 1.0)
        fixed = lambda scores: jnp.where(same, scores + penalty, -jnp.inf)
        mixed = attend(
            queries[:, span].reshape(lines * group, depth),
            keys[:, span].reshape(key_count, depth).astype(bf16),
            values[:, span].reshape(key_count, depth).astype(bf16),
            fixed,
            heads,
        )
        mix[:, span] = gate[:, span] * mixed.reshape(lines, group, depth)
    mixed = mix[...].reshape(rows, depth).astype(bf16)
    result = after[...] + dot(mixed, leave[...])
    hidden = jnp.maximum(dot(normalize(result).astype(bf16), first[...]), 0.0).astype(bf16)
    result = result + dot(hidden, second[...])
    output[...] = result.astype(bf16).reshape(output.shape)


def fetch(sources, buffers, semaphores):
    copies = [
        pltpu.make_async_copy(source, buffer, semaphores.at[index])
        for index, (source, buffer) in enumerate(zip(sources, buffers))
    ]
    for copy in copies:
        copy.start()
    for copy in copies:
        copy.wait()


def split(values):
    high = values.astype(bf16)
    rest = values - high.astype(f32)
    middle = rest.astype(bf16)
    return high, middle, (rest - middle.astype(f32)).astype(bf16)


def start_kernel(count, present, *refs):
    sources, outputs, rest = refs[:count], refs[count : count + 6], refs[count + 6 :]
    buffers, semaphores, tail = rest[:count], rest[count], rest[count + 1]
    fetch(sources, buffers, semaphores)
    embedded, payload, bundle, gate, terms, near = outputs
    embed_kernel(*buffers[:4], embedded, payload, tail)
    present_row, pairs, entry, logits = buffers[4:]
    lines, positions, width = pairs.shape
    heads = logits.shape[0]
    normed = normalize(pairs[...].astype(f32).reshape(lines * positions, width)).astype(bf16)
    logit = lax.dot_general(logits[...], normed, NT, preferred_element_type=f32)
    held = terms.shape[0] // 3
    for index, term in enumerate(split(logit)):
        for part in range(held // heads):
            base = index * held + part * heads
            terms[base : base + heads, :] = term[:, part * width : (part + 1) * width]
    projected = dot(normed, entry[:, 2 * width :])
    gate[...] = sigmoid(projected[:, 2 * width :])
    operand = (sigmoid(projected[:, width : 2 * width]) * projected[:, :width]).astype(bf16)
    mask_right(lax.axis_index("res"), operand, present, present_row, near)
    base = lines * positions
    bundle[:base, :] = pairs[...].reshape(base, width)
    for part in range(payload.shape[1] // width):
        span = slice(base + part * payload.shape[0], base + (part + 1) * payload.shape[0])
        bundle[span, :] = payload[:, part * width : (part + 1) * width]


def rows_of(block, count, depth):
    if block.shape == (count, depth):
        return block[...]
    parts = depth // block.shape[1]
    base = block.shape[0] - parts * count
    return jnp.concatenate(
        [block[base + part * count : base + (part + 1) * count, :] for part in range(parts)], axis=1
    )


def turn_kernel(pairs, entry, terms, out):
    width = pairs.shape[2]
    operand = gated(pairs, entry[:, : 2 * width])
    out[: operand.shape[0], :] = operand
    out[operand.shape[0] :, :] = terms[...]


def gated(pairs, weight):
    lines, positions, width = pairs.shape
    normed = normalize(pairs[...].astype(f32).reshape(lines * positions, width)).astype(bf16)
    projected = dot(normed, weight)
    return (sigmoid(projected[:, width:]) * projected[:, :width]).astype(bf16)


def left_kernel(pairs, entry, left):
    width = pairs.shape[2]
    left[...] = gated(pairs, entry[:, : 2 * width])


def mask_right(source, operand, present, present_row, right):
    lines, positions, width = right.shape
    lane = iota((positions, present_row.shape[1]), 1)
    lane = lane == iota((positions, present_row.shape[1]), 0) + side_index() * positions
    valid = jnp.where(lane, present_row[...].astype(f32), 0.0)
    valid = jnp.sum(valid, axis=1, keepdims=True)
    operand = operand.astype(f32)
    for line in range(lines):
        both = valid * present[source * lines + line].astype(f32)
        right[line] = (operand[line * positions : (line + 1) * positions] * both).astype(
            right.dtype
        )


def right_operand(relative, slot, present, present_row, pairs, entry, right):
    width = pairs.shape[2]
    source = (lax.axis_index("res") ^ slot) if relative else slot
    operand = gated(pairs, entry[:, 2 * width : 4 * width])
    mask_right(source, operand, present, present_row, right)


def pick_left(relative, slot, lefts, left):
    source = (lax.axis_index("res") ^ slot) if relative[0] else slot
    side = side_index()
    for place, block in enumerate(lefts):
        held = (side ^ place) if relative[1] else place

        @pl.when(held == source)
        def _():
            left[...] = block[...].astype(f32).reshape(left.shape)


def accumulate(left, right, total_in, total):
    step = 4
    depth, positions, width = right.shape

    def body(index, carry):
        base = index * step
        sums = [None if total_in is None else total_in[base + t] for t in range(step)]
        for line in range(depth):
            line_right = right[line].astype(f32)
            for t in range(step):
                term = left[line, pl.ds(base + t, 1), :] * line_right
                sums[t] = term if sums[t] is None else sums[t] + term
        for t in range(step):
            total[base + t] = sums[t]
        return carry

    lax.fori_loop(0, total.shape[0] // step, body, 0)


def middle_kernel(relative, slots, *refs):
    rights, lefts = refs[: len(slots)], refs[len(slots) : -2]
    total, left = refs[-2:]
    for index, slot in enumerate(slots):
        pick_left(relative, slot, lefts, left)
        accumulate(left, rights[index], total if index else None, total)


def last_kernel(relative, slot, *refs):
    present, present_row, pairs, entry, total_in, own, gate, leave = refs[:8]
    lefts, (out, left, right, total) = refs[8:-4], refs[-4:]
    lines, positions, width = out.shape
    pick_left(relative, slot, lefts, left)
    right_operand(relative[0], slot, present, present_row, pairs, entry, right)
    accumulate(left, right, total_in, total)
    me = lax.axis_index("res")
    for line in range(lines):
        total[line] = total[line] * present[me * lines + line].astype(f32)
    product = total[...].reshape(lines * positions, width).astype(bf16).astype(f32)
    update = gate[...] * dot(normalize(product).astype(bf16), leave[...])
    out[...] = (own[...].astype(f32) + update.reshape(out.shape)).astype(bf16)


def far_kernel(lines, present, present_row, bundle, entry, right):
    width = bundle.shape[1]
    pairs = bundle[: lines * right.shape[1], :].reshape(right.shape)
    operand = gated(pairs, entry[:, 2 * width : 4 * width])
    mask_right(lax.axis_index("res") ^ 1, operand, present, present_row, right)


def partial_kernel(other_half, own, beside, other, other_beside, near, far, total, left):
    half = lax.axis_index("res") // 2
    wanted = (1 - half) if other_half else half
    mine = lax.axis_index("br") == wanted
    straight = lax.axis_index("res") % 2 == lax.axis_index("aux")
    count = total.shape[0]
    lines = near.shape[0]

    def load(first, second):
        for slot, block in enumerate((first, second)):
            for line in range(lines):
                base = line * count
                left[slot * lines + line] = block[base : base + count, :].astype(f32)

    other_core = jnp.logical_not(mine)
    crossed = jnp.logical_not(straight)
    pl.when(mine & straight)(lambda: load(own, beside))
    pl.when(mine & crossed)(lambda: load(beside, own))
    pl.when(other_core & straight)(lambda: load(other, other_beside))
    pl.when(other_core & crossed)(lambda: load(other_beside, other))
    step = 8

    def body(index, carry):
        base = index * step
        sums = [None] * step
        for line in range(2 * lines):
            right = near[line] if line < lines else far[line - lines]
            for t in range(step):
                term = left[line, pl.ds(base + t, 1), :] * right
                sums[t] = term if sums[t] is None else sums[t] + term
        for t in range(step):
            total[base + t] = sums[t].astype(total.dtype)
        return carry

    lax.fori_loop(0, count // step, body, 0)


def finish_kernel(present, kept, own, gate, leave, *refs):
    received, (out, total) = refs[:-2], refs[-2:]
    lines, positions, width = out.shape
    me = lax.axis_index("res")
    each = lines // len(received)
    for line in range(lines):
        sums = kept[line] + received[line // each][line % each].astype(f32)
        total[line] = sums * present[me * lines + line].astype(f32)
    product = total[...].reshape(lines * positions, width).astype(bf16).astype(f32)
    update = gate[...] * dot(normalize(product).astype(bf16), leave[...])
    out[...] = (own[...].astype(f32) + update.reshape(out.shape)).astype(bf16)


def gather(block, axis):
    size = lax.axis_size(axis)
    if size in (1, 2, 4):
        return [block] + [flip(block, axis, d) for d in range(1, size)], True
    whole = lax.all_gather(block, axis)
    return [whole[i] for i in range(size)], False


def flip(block, axis, bit=1):
    return lax.ppermute(block, axis, [(i, i ^ bit) for i in range(lax.axis_size(axis))])


def gather_side(block, ahead=()):
    if lax.axis_size("br") == 2 and lax.axis_size("aux") == 2:
        near = flip(block, "br")
        far = flip(block, "aux")
        far = lax.optimization_barrier((far, *ahead))[0]
        return [block, far, near, flip(far, "br")], True
    whole = lax.all_gather(block, SIDE)
    return [whole[i] for i in range(whole.shape[0])], False


def shape(dims, kind):
    return jax.ShapeDtypeStruct(dims, kind)


def call(kernel, out_shape, scratch=(), smem=0, after=(), hbm=False):
    def run(*args):
        count, unread = len(args), len(after)

        def ordered(*refs):
            kernel(*refs[:count], *refs[count + unread :])

        return pl.pallas_call(
            ordered,
            out_shape=out_shape,
            in_specs=[pl.BlockSpec(memory_space=pltpu.SMEM)] * smem
            + [pl.BlockSpec(memory_space=pltpu.HBM if hbm else pltpu.VMEM)] * (count - smem)
            + [pl.BlockSpec(memory_space=pl.ANY)] * unread,
            out_specs=jax.tree.map(lambda _: pl.BlockSpec(memory_space=pltpu.VMEM), out_shape),
            scratch_shapes=list(scratch),
            compiler_params=pltpu.CompilerParams(vmem_limit_bytes=(62 if hbm else 48) * 1024 * 1024),
            cost_estimate=pl.CostEstimate(flops=1, bytes_accessed=1, transcendentals=0),
        )(*args, *after)

    return run


def triangle_by_gather(pairs, presence, entry, leave, gate):
    res = lax.axis_size("res")
    side = lax.axis_size("br") * lax.axis_size("aux")
    rows, cols, width = pairs.shape
    cube = pltpu.VMEM((rows, cols, width), f32)
    turned = lax.ppermute(
        pairs, ALL, [(r * side + b, b * side + r) for r in range(res) for b in range(side)]
    )
    left = call(left_kernel, shape((rows * cols, width), bf16))(turned, entry)
    lefts, left_relative = gather_side(left)
    blocks, pair_relative = gather(pairs, "res")
    relative = (pair_relative, left_relative)
    slots = list(range(res - 1))
    rights = [
        call(
            functools.partial(right_operand, pair_relative, slot), shape(pairs.shape, bf16), smem=1
        )(*presence, blocks[slot], entry)
        for slot in slots
    ]
    total = call(
        functools.partial(middle_kernel, relative, slots), shape(pairs.shape, f32), [cube]
    )(*rights, *lefts)
    return call(
        functools.partial(last_kernel, relative, res - 1),
        shape(pairs.shape, bf16),
        [cube, cube, cube],
        smem=1,
    )(*presence, blocks[-1], entry, total, pairs, gate, leave, *lefts)


def turn_pairs(pairs):
    index = lambda half, low, br, aux: ((half * 2 + low) * 2 + br) * 2 + aux
    every = [(h, low, br, aux) for h in (0, 1) for low in (0, 1) for br in (0, 1) for aux in (0, 1)]
    return lax.ppermute(
        pairs, ALL, [(index(h, l, br, a), index(h, a, br, l)) for h, l, br, a in every]
    )


def on_device(
    homolog_features,
    couple_features,
    symbol_ids,
    entry_present,
    amino_present,
    symbol_lookup_matrix,
    horizontal_entry_matrix,
    couple_logit_matrix,
    horizontal_exit_matrix,
    vertical_entry_matrix,
    vertical_exit_matrix,
    feedforward_first_matrix,
    feedforward_second_matrix,
    trimul_entry_matrix,
    trimul_exit_matrix,
):
    lines, positions, depth = homolog_features.shape
    pair_rows, pair_cols, width = couple_features.shape
    heads = couple_logit_matrix.shape[1]
    res = lax.axis_size("res")
    side = lax.axis_size("br") * lax.axis_size("aux")
    rows = lines * positions
    tail = round_up(lines, 16)
    residues = positions * res
    area = pair_rows * pair_cols
    held = pair_rows * pair_cols * heads // width
    presence = [amino_present, amino_present[None, :]]
    halves = (res, lax.axis_size("br"), lax.axis_size("aux")) == (4, 2, 2)

    args = (
        homolog_features,
        symbol_ids,
        entry_present,
        symbol_lookup_matrix,
        amino_present[None, :],
        couple_features,
        trimul_entry_matrix,
        couple_logit_matrix.T,
    )
    embedded, payload, bundle, gate, terms, near = call(
        functools.partial(start_kernel, len(args)),
        (
            shape((rows, depth), f32),
            shape((rows + tail, depth), bf16),
            shape((area + (rows + tail) * (depth // width), width), bf16),
            shape((area, width), f32),
            shape((3 * held, width), bf16),
            shape(couple_features.shape, f32),
        ),
        [pltpu.VMEM(x.shape, x.dtype) for x in args]
        + [pltpu.SemaphoreType.DMA((len(args),)), pltpu.VMEM((tail, depth), f32)],
        smem=1,
        hbm=True,
    )(amino_present, *args)
    pending = ()
    if halves:
        beside = flip(bundle, "res")
        row_blocks = [payload, beside, flip(payload, "res", 2), flip(payload, "res", 3)]
        row_relative = True
        turned = call(turn_kernel, shape((area + 3 * held, width), bf16))(
            turn_pairs(couple_features), trimul_entry_matrix, terms
        )
        terms, side_relative = gather_side(turned, (beside, *row_blocks[2:]))
        far = call(
            functools.partial(far_kernel, pair_rows),
            shape(couple_features.shape, f32),
            smem=1,
            after=(turned,),
        )(*presence, beside, trimul_entry_matrix)

        def sums(other_half, kind, after):
            return call(
                functools.partial(partial_kernel, other_half),
                shape(couple_features.shape, kind),
                [pltpu.VMEM((2 * pair_rows, pair_cols, width), f32)],
                after=after,
            )(*terms, near, far)

        sent = sums(True, bf16, ())
        received = flip(sent, "res", 2)
        pending = (sent,)
    else:
        row_blocks, row_relative = gather(payload, "res")
        terms, side_relative = gather_side(terms)

    after, payload = call(
        functools.partial(row_kernel, row_relative, side_relative, side, lines, positions),
        (shape((rows, depth), f32), shape((rows + tail, depth), bf16)),
        [
            pltpu.VMEM((pair_rows * heads, residues), f32),
            pltpu.VMEM((lines, residues, depth), bf16),
            pltpu.VMEM((lines, residues, depth), bf16),
            pltpu.VMEM((rows, depth), bf16),
        ],
        after=pending,
    )(*terms, *row_blocks, payload, embedded, horizontal_entry_matrix, horizontal_exit_matrix)
    column_blocks, _ = gather_side(payload)
    if halves:
        kept = sums(False, f32, (payload,))
        pending = (kept,)
    group = 8
    alignment_output = call(
        functools.partial(column_kernel, lines, positions, group, heads),
        shape((lines, positions, depth), bf16),
        [
            pltpu.VMEM((side * lines, positions, depth), f32),
            pltpu.VMEM((side * lines, positions, depth), f32),
            pltpu.VMEM((lines, positions, depth), f32),
        ],
        after=pending,
    )(
        *column_blocks,
        payload,
        after,
        vertical_entry_matrix,
        vertical_exit_matrix,
        feedforward_first_matrix,
        feedforward_second_matrix,
    )
    if halves:
        pair_output = call(
            finish_kernel,
            shape(couple_features.shape, bf16),
            [pltpu.VMEM(couple_features.shape, f32)],
            smem=1,
        )(amino_present, kept, couple_features, gate, trimul_exit_matrix, received)
    else:
        pair_output = triangle_by_gather(
            couple_features, presence, trimul_entry_matrix, trimul_exit_matrix, gate
        )
    return (alignment_output, pair_output)


def solution(mesh):
    return jax.shard_map(
        on_device,
        mesh=mesh,
        in_specs=(
            P(("grp", "br", "aux"), "res", None),
            P(("grp", "res"), ("br", "aux"), None),
            P(("grp", "br", "aux"), "res"),
            P(("grp", "br", "aux"), "res"),
            P("grp"),
            P(),
            P(),
            P(),
            P(),
            P(),
            P(),
            P(),
            P(),
            P(),
            P(),
        ),
        out_specs=(P(("grp", "br", "aux"), "res", None), P(("grp", "res"), ("br", "aux"), None)),
        check_vma=False,
    )
```

time: 150 us -> 47.1 us (0.31)
  blocking collectives: 66.1 us -> 0 us
  local copies, waits for them, and re-layouts: 19.6 us -> 0.86 us
  Pallas kernels: 0 us -> 18.5 us
  matrix products: 16.8 us -> 0 us
  between operations: 14.6 us -> 0.84 us
  other arithmetic: 9.09 us -> 0 us
  waiting for transfers between devices: 7.83 us -> 11.4 us
    all_gather x6 -> x0, blocking collectives: 66.1 us -> none  [the longest x1 14.5 us: on_device(): partial_rows = lax.all_gather(normed_first, 'res', axis=1, tiled=True)]
    pallas_call x0 -> x8, Pallas kernels: none -> 18.5 us  [run(): pl.pallas_call(ordered, out_shape=out_shape, in_specs=[pl.BlockSpec(memor...]
    dot_general x16 -> x0, matrix products: 16.8 us -> none  [the longest x8 8.37 us: apply_projection(): result = jnp.dot(flattened, weight, preferred_element_type=jnp.float32)]
    ppermute x0 -> x11, starting transfers between devices: none -> 15.2 us  [the longest x10 13.6 us: flip(): lax.ppermute(block, axis, [(i, i ^ bit) for i in range(lax.axis_size(axis...]
    all_to_all x3 -> x0, starting transfers between devices: 14.7 us -> none  [the longest x1 6.44 us: on_device(): lax.all_to_all(left_side, 'res', split_axis=0, concat_axis=1, tiled=True)]
    ppermute x0 -> x11, waiting for transfers between devices: none -> 11.4 us  [the longest x10 11.4 us: flip(): lax.ppermute(block, axis, [(i, i ^ bit) for i in range(lax.axis_size(axis...]
    all_to_all x3 -> x0, waiting for transfers between devices: 7.79 us -> none  [the longest x1 7.79 us: on_device(): lax.all_to_all(product, 'res', split_axis=1, concat_axis=0, tiled=True)]
    convert_element_type x5 -> x0, local copies, waits for them, and re-layouts: 7.32 us -> none  [the longest x2 2.95 us: normalize(): values = inputs.astype(jnp.float32)]
  transfers between devices with their start and end apart: 4 -> 11, of which waited for: 1 -> 5; matrix products, arithmetic and copies ran while one was open for 15% -> 0% of each run, Pallas kernels for 0% -> 30%
where the time goes in v1:
time: 47.1 us; the launch traced here: 46.8 us
  Pallas kernels  18.5 us (39%)
  starting transfers between devices  15.2 us (32%)
  waiting for transfers between devices  11.4 us (24%)
  local copies, waits for them, and re-layouts  0.86 us (2%)
  between operations  0.84 us (2%)
    pallas_call x8, Pallas kernels, run(): pl.pallas_call(ordered, out_shape=out_shape, in_specs=[pl.BlockSpec(memor...  18.5 us
    ppermute x10, starting transfers between devices, flip(): lax.ppermute(block, axis, [(i, i ^ bit) for i in range(lax.axis_size(axis...  13.6 us
    ppermute x10, waiting for transfers between devices, flip(): lax.ppermute(block, axis, [(i, i ^ bit) for i in range(lax.axis_size(axis...  11.4 us
    ppermute x1, starting transfers between devices, turn_pairs(): lax.ppermute(pairs, ALL, [(index(h, l, br, a), index(h, a, br, l)) for h,...  1.61 us
  transfers between devices with their start and end apart: 11, of which 5 were waited for; matrix products, arithmetic and copies ran while one was open for 0% of the time, Pallas kernels for 30%

profile of v1, /device:TPU:0, one launch (start us, length us, event | category | flops | bytes accessed | tf_op | source)
XLA Modules:
  0.0 46.8 jit_solution(12468210703163555732)
XLA Ops:
  0.6 1.6 %collective-permute-start = (bf16[32,32,128]{2,1,0:T(8,128)(2,1)}, bf16[32,32,128]{2,1,0:T(8,128)(2,1)S(1)}, u32[]{:S(2)}, u32[]{:S(2)}) collective-permute-start(bf16[32,32,128]{2,1,0:T(8,128)(2,1)} %refs_2_.3), channel_id=1, source_target_pairs={{0,0},{1,4},{2,2},{3,6},{4,1},{5,5},{6,3},{7,7},{8,8},{9,12},{10,1... | collective-permute-start | bytes 786440 | tf_op jit(solution)/shard_map/ppermute | solution.py:467
  2.2 3.9 %shard_map.158 = (f32[128,256]{1,0:T(8,128)}, bf16[144,256]{1,0:T(8,128)(2,1)}, bf16[1312,128]{1,0:T(8,128)(2,1)}, f32[1024,128]{1,0:T(8,128)}, bf16[192,128]{1,0:T(8,128)(2,1)}, /*index=5*/f32[32,32,128]{2,1,0:T(8,128)}) custom-call(s32[128]{0:T(128)} %refs_0_.5, bf16[4,32,256]{2,1,0:T(8,128)(2,1)} %refs_1_.2, s32[4,32]{1,0:T(4,128)} %refs_2_.2, ...), custom_call_target="tpu_custom_call" | custom-call | flops 1 | bytes 1 | tf_op jit(solution)/shard_map/pallas_call | solution.py:419
  6.1 4.8 %collective-permute-start.2 = (bf16[1312,128]{1,0:T(8,128)(2,1)}, bf16[1312,128]{1,0:T(8,128)(2,1)S(1)}, u32[]{:S(2)}, u32[]{:S(2)}) collective-permute-start(bf16[1312,128]{1,0:T(8,128)(2,1)} %get-tuple-element.12), channel_id=1, source_target_pairs={{0,4},{4,0},{8,12},{12,8},{1,5},{5,1},{9,13},{13,9},{2,6},{6,2},{1... | collective-permute-start | bytes 1007624 | tf_op jit(solution)/shard_map/ppermute | solution.py:395
  10.9 0.8 %copy-done.12 = bf16[192,128]{1,0:T(8,128)(2,1)S(1)} copy-done((bf16[192,128]{1,0:T(8,128)(2,1)S(1)}, bf16[192,128]{1,0:T(8,128)(2,1)}, u32[]{:S(2)}) %copy-start.12) | copy-done | bytes 49176
  11.7 0.6 %shard_map.159.refs_4_.refs_0_ = bf16[1216,128]{1,0:T(8,128)(2,1)S(1)} custom-call(bf16[32,32,128]{2,1,0:T(8,128)(2,1)S(1)} %collective-permute-done.refs_0_, bf16[128,640]{1,0:T(8,128)(2,1)S(1)} %copy-done.1, bf16[192,128]{1,0:T(8,128)(2,1)S(1)} %copy-done.12), custom_call_target="tpu_custom_call" | custom-call | flops 1 | bytes 1 | tf_op jit(solution)/shard_map/pallas_call | solution.py:419
  12.3 0.0 copy-start.14
  12.3 4.9 %collective-permute-start.1 = (bf16[1216,128]{1,0:T(8,128)(2,1)S(1)}, bf16[1216,128]{1,0:T(8,128)(2,1)S(1)}, u32[]{:S(2)}, u32[]{:S(2)}) collective-permute-start(bf16[1216,128]{1,0:T(8,128)(2,1)S(1)} %shard_map.159.refs_4_.refs_0_), channel_id=1, source_target_pairs={{0,1},{1,0},{2,3},{3,2},{4,5},{5,4},{6,7},{7,6},{8,9},{9,8},{10,11... | collective-permute-start | bytes 933896 | tf_op jit(solution)/shard_map/ppermute | solution.py:395
  17.2 2.4 %collective-permute-start.4 = (bf16[144,256]{1,0:T(8,128)(2,1)S(1)}, bf16[144,256]{1,0:T(8,128)(2,1)S(1)}, u32[]{:S(2)}, u32[]{:S(2)}) collective-permute-start(bf16[144,256]{1,0:T(8,128)(2,1)S(1)} %copy-done.8), channel_id=1, source_target_pairs={{0,12},{4,8},{8,4},{12,0},{1,13},{5,9},{9,5},{13,1},{2,14},{6,10},... | collective-permute-start | bytes 221192 | tf_op jit(solution)/shard_map/ppermute | solution.py:395
  19.6 0.3 collective-permute-start.3
  19.9 5.0 %collective-permute-done.4.refs_7_ = bf16[144,256]{1,0:T(8,128)(2,1)S(1)} collective-permute-done((bf16[144,256]{1,0:T(8,128)(2,1)S(1)}, bf16[144,256]{1,0:T(8,128)(2,1)S(1)}, u32[]{:S(2)}, u32[]{:S(2)}) %collective-permute-start.4) | collective-permute-done | bytes 73760 | tf_op jit(solution)/shard_map/ppermute | solution.py:395
  24.8 1.5 %collective-permute-done.3.refs_6_ = bf16[144,256]{1,0:T(8,128)(2,1)S(1)} collective-permute-done((bf16[144,256]{1,0:T(8,128)(2,1)S(1)}, bf16[144,256]{1,0:T(8,128)(2,1)S(1)}, u32[]{:S(2)}, u32[]{:S(2)}) %collective-permute-start.3) | collective-permute-done | bytes 73760 | tf_op jit(solution)/shard_map/ppermute | solution.py:395
  26.4 1.1 %shard_map.160.refs_5_ = f32[32,32,128]{2,1,0:T(8,128)S(1)} custom-call(s32[128]{0:T(128)S(1)} %copy-done.14, s32[1,128]{1,0:T(1,128)S(1)} %bitcast.3, bf16[1312,128]{1,0:T(8,128)(2,1)S(1)} %collective-permute-done.2.refs_2_.refs_5_, bf16[128,640]{1,0:T(8,128)(2,1)S(1)} %copy-done.1, bf16[1216,128]{1,0:T(8,128)(2,1)S(1)} %shard_map.159.refs_4_.refs_0_), custom_call_target="tpu_custom_call" | custom-call | flops 1 | bytes 1 | tf_op jit(solution)/shard_map/pallas_call | solution.py:419
  27.5 0.4 collective-permute-done.6.refs_3_
  28.0 2.9 %shard_map.161.refs_12_ = bf16[32,32,128]{2,1,0:T(8,128)(2,1)S(1)} custom-call(bf16[1216,128]{1,0:T(8,128)(2,1)S(1)} %shard_map.159.refs_4_.refs_0_, bf16[1216,128]{1,0:T(8,128)(2,1)S(1)} %collective-permute-done.1.refs_1_, bf16[1216,128]{1,0:T(8,128)(2,1)S(1)} %collective-permute-done.5.refs_2_, bf16[1216,128]{1,0:T(8,128)(2,1)S(1)} %collective-permute-done.6.refs_3_, ...), custom_call_target="tpu_custom_call" | custom-call | flops 1 | bytes 1 | tf_op jit(solution)/shard_map/pallas_call | solution.py:419
  30.9 0.1 collective-permute-start.10
  31.0 1.6 %shard_map.162 = (f32[128,256]{1,0:T(8,128)S(1)}, bf16[144,256]{1,0:T(8,128)(2,1)S(1)}) custom-call(bf16[1216,128]{1,0:T(8,128)(2,1)S(1)} %shard_map.159.refs_4_.refs_0_, bf16[1216,128]{1,0:T(8,128)(2,1)S(1)} %collective-permute-done.1.refs_1_, bf16[1216,128]{1,0:T(8,128)(2,1)S(1)} %collective-permute-done.5.refs_2_, ...), custom_call_target="tpu_custom_call" | custom-call | flops 1 | bytes 1 | tf_op jit(solution)/shard_map/pallas_call | solution.py:419
  32.5 0.0 copy-start.6
  32.6 1.2 %collective-permute-start.7 = (bf16[144,256]{1,0:T(8,128)(2,1)S(1)}, bf16[144,256]{1,0:T(8,128)(2,1)S(1)}, u32[]{:S(2)}, u32[]{:S(2)}) collective-permute-start(bf16[144,256]{1,0:T(8,128)(2,1)S(1)} %get-tuple-element.17.refs_6_.refs_0_.refs_4_), channel_id=1, source_target_pairs={{0,1},{1,0},{2,3},{3,2},{4,5},{5,4},{6,7},{7,6},{8,9},{9,8},{10,11... | collective-permute-start | bytes 221192 | tf_op jit(solution)/shard_map/ppermute | solution.py:395
  33.8 3.2 %collective-permute-done.7.refs_1_ = bf16[144,256]{1,0:T(8,128)(2,1)S(1)} collective-permute-done((bf16[144,256]{1,0:T(8,128)(2,1)S(1)}, bf16[144,256]{1,0:T(8,128)(2,1)S(1)}, u32[]{:S(2)}, u32[]{:S(2)}) %collective-permute-start.7) | collective-permute-done | bytes 73760 | tf_op jit(solution)/shard_map/ppermute | solution.py:395
  37.0 3.4 %shard_map.163.refs_10_.refs_1_ = f32[32,32,128]{2,1,0:T(8,128)S(1)} custom-call(bf16[1216,128]{1,0:T(8,128)(2,1)S(1)} %shard_map.159.refs_4_.refs_0_, bf16[1216,128]{1,0:T(8,128)(2,1)S(1)} %collective-permute-done.1.refs_1_, bf16[1216,128]{1,0:T(8,128)(2,1)S(1)} %collective-permute-done.5.refs_2_, bf16[1216,128]{1,0:T(8,128)(2,1)S(1)} %collective-permute-done.6.refs_3_, ...), custom_call_target="tpu_custom_call" | custom-call | flops 1 | bytes 1 | tf_op jit(solution)/shard_map/pallas_call | solution.py:419
  40.5 0.0 copy-start.13
  40.5 3.3 %shard_map.164 = bf16[4,32,256]{2,1,0:T(8,128)(2,1)} custom-call(bf16[144,256]{1,0:T(8,128)(2,1)S(1)} %get-tuple-element.17.refs_6_.refs_0_.refs_4_, bf16[144,256]{1,0:T(8,128)(2,1)S(1)} %collective-permute-done.7.refs_1_, bf16[144,256]{1,0:T(8,128)(2,1)S(1)} %collective-permute-done.8.refs_2_, bf16[144,256]{1,0:T(8,128)(2,1)S(1)} %collective-permute-done.9.refs_3_, ...), custom_call_target="tpu_custom_call" | custom-call | flops 1 | bytes 1 | tf_op jit(solution)/shard_map/pallas_call | solution.py:419
  43.8 1.3 %collective-permute-done.10.refs_5_ = bf16[32,32,128]{2,1,0:T(8,128)(2,1)S(1)} collective-permute-done((bf16[32,32,128]{2,1,0:T(8,128)(2,1)S(1)}, bf16[32,32,128]{2,1,0:T(8,128)(2,1)S(1)}, u32[]{:S(2)}, u32[]{:S(2)}) %collective-permute-start.10) | collective-permute-done | bytes 262176 | tf_op jit(solution)/shard_map/ppermute | solution.py:395
  45.1 1.7 %shard_map.165 = bf16[32,32,128]{2,1,0:T(8,128)(2,1)} custom-call(s32[128]{0:T(128)S(1)} %copy-done.14, f32[32,32,128]{2,1,0:T(8,128)S(1)} %shard_map.163.refs_10_.refs_1_, bf16[32,32,128]{2,1,0:T(8,128)(2,1)S(1)} %copy-done.2, f32[1024,128]{1,0:T(8,128)S(1)} %copy-done.7, bf16[128,128]{1,0:T(8,128)(2,1)S(1)} %copy-done.13, ...), custom_call_target="tpu_custom_call" | custom-call | flops 1 | bytes 1 | tf_op jit(solution)/shard_map/pallas_call | solution.py:419
  (36 shorter events, 0.1 us)
Async XLA Ops:
  0.6 10.3 %collective-permute-start = (bf16[32,32,128]{2,1,0:T(8,128)(2,1)}, bf16[32,32,128]{2,1,0:T(8,128)(2,1)S(1)}, u32[]{:S(2)}, u32[]{:S(2)}) collective-permute-start(bf16[32,32,128]{2,1,0:T(8,128)(2,1)} %refs_2_.3), channel_id=1, source_target_pairs={{0,0},{1,4},{2,2},{3,6},{4,1},{5,5},{6,3},{7,7},{8,8},{9,12},{10,1... | collective-permute-start | bytes 786440 | tf_op jit(solution)/shard_map/ppermute | solution.py:467
  2.2 8.7 %copy-start.1 = (bf16[128,640]{1,0:T(8,128)(2,1)S(1)}, bf16[128,640]{1,0:T(8,128)(2,1)}, u32[]{:S(2)}) copy-start(bf16[128,640]{1,0:T(8,128)(2,1)} %refs_3_.3) | copy-start | bytes 491524
  6.1 20.2 %collective-permute-start.2 = (bf16[1312,128]{1,0:T(8,128)(2,1)}, bf16[1312,128]{1,0:T(8,128)(2,1)S(1)}, u32[]{:S(2)}, u32[]{:S(2)}) collective-permute-start(bf16[1312,128]{1,0:T(8,128)(2,1)} %get-tuple-element.12), channel_id=1, source_target_pairs={{0,4},{4,0},{8,12},{12,8},{1,5},{5,1},{9,13},{13,9},{2,6},{6,2},{1... | collective-permute-start | bytes 1007624 | tf_op jit(solution)/shard_map/ppermute | solution.py:395
  11.7 5.5 %copy-start.8 = (bf16[144,256]{1,0:T(8,128)(2,1)S(1)}, bf16[144,256]{1,0:T(8,128)(2,1)}, u32[]{:S(2)}) copy-start(bf16[144,256]{1,0:T(8,128)(2,1)} %get-tuple-element.13.refs_4_.refs_8_) | copy-start | bytes 221188
  12.3 14.0 %copy-start.14 = (s32[128]{0:T(128)S(1)}, s32[128]{0:T(128)}, u32[]{:S(2)}) copy-start(s32[128]{0:T(128)} %refs_0_.5) | copy-start | bytes 1540
  12.3 14.0 %collective-permute-start.1 = (bf16[1216,128]{1,0:T(8,128)(2,1)S(1)}, bf16[1216,128]{1,0:T(8,128)(2,1)S(1)}, u32[]{:S(2)}, u32[]{:S(2)}) collective-permute-start(bf16[1216,128]{1,0:T(8,128)(2,1)S(1)} %shard_map.159.refs_4_.refs_0_), channel_id=1, source_target_pairs={{0,1},{1,0},{2,3},{3,2},{4,5},{5,4},{6,7},{7,6},{8,9},{9,8},{10,11... | collective-permute-start | bytes 933896 | tf_op jit(solution)/shard_map/ppermute | solution.py:395
  17.2 10.7 %copy-start = (f32[32,32,128]{2,1,0:T(8,128)S(1)}, f32[32,32,128]{2,1,0:T(8,128)}, u32[]{:S(2)}) copy-start(f32[32,32,128]{2,1,0:T(8,128)} %get-tuple-element.16.refs_4_) | copy-start | bytes 1572868
  17.2 7.6 %collective-permute-start.4 = (bf16[144,256]{1,0:T(8,128)(2,1)S(1)}, bf16[144,256]{1,0:T(8,128)(2,1)S(1)}, u32[]{:S(2)}, u32[]{:S(2)}) collective-permute-start(bf16[144,256]{1,0:T(8,128)(2,1)S(1)} %copy-done.8), channel_id=1, source_target_pairs={{0,12},{4,8},{8,4},{12,0},{1,13},{5,9},{9,5},{13,1},{2,14},{6,10},... | collective-permute-start | bytes 221192 | tf_op jit(solution)/shard_map/ppermute | solution.py:395
  19.6 6.8 %collective-permute-start.3 = (bf16[144,256]{1,0:T(8,128)(2,1)S(1)}, bf16[144,256]{1,0:T(8,128)(2,1)S(1)}, u32[]{:S(2)}, u32[]{:S(2)}) collective-permute-start(bf16[144,256]{1,0:T(8,128)(2,1)S(1)} %copy-done.8), channel_id=1, source_target_pairs={{0,8},{4,12},{8,0},{12,4},{1,9},{5,13},{9,1},{13,5},{2,10},{6,14},... | collective-permute-start | bytes 221192 | tf_op jit(solution)/shard_map/ppermute | solution.py:395
  19.9 7.6 %collective-permute-start.5 = (bf16[1216,128]{1,0:T(8,128)(2,1)S(1)}, bf16[1216,128]{1,0:T(8,128)(2,1)S(1)}, u32[]{:S(2)}, u32[]{:S(2)}) collective-permute-start(bf16[1216,128]{1,0:T(8,128)(2,1)S(1)} %shard_map.159.refs_4_.refs_0_), channel_id=1, source_target_pairs={{0,2},{2,0},{1,3},{3,1},{4,6},{6,4},{5,7},{7,5},{8,10},{10,8},{9,1... | collective-permute-start | bytes 933896 | tf_op jit(solution)/shard_map/ppermute | solution.py:395
  26.3 1.6 %collective-permute-start.6 = (bf16[1216,128]{1,0:T(8,128)(2,1)S(1)}, bf16[1216,128]{1,0:T(8,128)(2,1)S(1)}, u32[]{:S(2)}, u32[]{:S(2)}) collective-permute-start(bf16[1216,128]{1,0:T(8,128)(2,1)S(1)} %collective-permute-done.1.refs_1_), channel_id=1, source_target_pairs={{0,2},{2,0},{1,3},{3,1},{4,6},{6,4},{5,7},{7,5},{8,10},{10,8},{9,1... | collective-permute-start | bytes 933896 | tf_op jit(solution)/shard_map/ppermute | solution.py:395
  28.0 3.0 %copy-start.9 = (bf16[256,256]{1,0:T(8,128)(2,1)S(1)}, bf16[256,256]{1,0:T(8,128)(2,1)}, u32[]{:S(2)}) copy-start(bf16[256,256]{1,0:T(8,128)(2,1)} %refs_11_.1) | copy-start | bytes 393220
  28.0 3.0 %copy-start.11 = (f32[128,256]{1,0:T(8,128)S(1)}, f32[128,256]{1,0:T(8,128)}, u32[]{:S(2)}) copy-start(f32[128,256]{1,0:T(8,128)} %get-tuple-element.15.refs_9_) | copy-start | bytes 393220
  30.9 14.2 %collective-permute-start.10 = (bf16[32,32,128]{2,1,0:T(8,128)(2,1)S(1)}, bf16[32,32,128]{2,1,0:T(8,128)(2,1)S(1)}, u32[]{:S(2)}, u32[]{:S(2)}) collective-permute-start(bf16[32,32,128]{2,1,0:T(8,128)(2,1)S(1)} %shard_map.161.refs_12_), channel_id=1, source_target_pairs={{0,8},{4,12},{8,0},{12,4},{1,9},{5,13},{9,1},{13,5},{2,10},{6,14},... | collective-permute-start | bytes 786440 | tf_op jit(solution)/shard_map/ppermute | solution.py:395
  32.5 7.9 %copy-start.4 = (bf16[256,1024]{1,0:T(8,128)(2,1)S(1)}, bf16[256,1024]{1,0:T(8,128)(2,1)}, u32[]{:S(2)}) copy-start(bf16[256,1024]{1,0:T(8,128)(2,1)} %refs_6_.3) | copy-start | bytes 1572868
  32.5 7.9 %copy-start.5 = (bf16[256,1024]{1,0:T(8,128)(2,1)S(1)}, bf16[256,1024]{1,0:T(8,128)(2,1)}, u32[]{:S(2)}) copy-start(bf16[256,1024]{1,0:T(8,128)(2,1)} %refs_8_.1) | copy-start | bytes 1572868
  32.5 7.9 %copy-start.6 = (bf16[1024,256]{1,0:T(8,128)(2,1)S(1)}, bf16[1024,256]{1,0:T(8,128)(2,1)}, u32[]{:S(2)}) copy-start(bf16[1024,256]{1,0:T(8,128)(2,1)} %refs_9_.1) | copy-start | bytes 1572868
  32.6 7.9 %copy-start.10 = (bf16[256,256]{1,0:T(8,128)(2,1)S(1)}, bf16[256,256]{1,0:T(8,128)(2,1)}, u32[]{:S(2)}) copy-start(bf16[256,256]{1,0:T(8,128)(2,1)} %refs_7_.3) | copy-start | bytes 393220
  32.6 4.4 %collective-permute-start.7 = (bf16[144,256]{1,0:T(8,128)(2,1)S(1)}, bf16[144,256]{1,0:T(8,128)(2,1)S(1)}, u32[]{:S(2)}, u32[]{:S(2)}) collective-permute-start(bf16[144,256]{1,0:T(8,128)(2,1)S(1)} %get-tuple-element.17.refs_6_.refs_0_.refs_4_), channel_id=1, source_target_pairs={{0,1},{1,0},{2,3},{3,2},{4,5},{5,4},{6,7},{7,6},{8,9},{9,8},{10,11... | collective-permute-start | bytes 221192 | tf_op jit(solution)/shard_map/ppermute | solution.py:395
  33.8 6.6 %collective-permute-start.8 = (bf16[144,256]{1,0:T(8,128)(2,1)S(1)}, bf16[144,256]{1,0:T(8,128)(2,1)S(1)}, u32[]{:S(2)}, u32[]{:S(2)}) collective-permute-start(bf16[144,256]{1,0:T(8,128)(2,1)S(1)} %get-tuple-element.17.refs_6_.refs_0_.refs_4_), channel_id=1, source_target_pairs={{0,2},{2,0},{1,3},{3,1},{4,6},{6,4},{5,7},{7,5},{8,10},{10,8},{9,1... | collective-permute-start | bytes 221192 | tf_op jit(solution)/shard_map/ppermute | solution.py:395
  37.0 3.4 %collective-permute-start.9 = (bf16[144,256]{1,0:T(8,128)(2,1)S(1)}, bf16[144,256]{1,0:T(8,128)(2,1)S(1)}, u32[]{:S(2)}, u32[]{:S(2)}) collective-permute-start(bf16[144,256]{1,0:T(8,128)(2,1)S(1)} %collective-permute-done.7.refs_1_), channel_id=1, source_target_pairs={{0,2},{2,0},{1,3},{3,1},{4,6},{6,4},{5,7},{7,5},{8,10},{10,8},{9,1... | collective-permute-start | bytes 221192 | tf_op jit(solution)/shard_map/ppermute | solution.py:395
  40.4 4.7 %copy-start.2 = (bf16[32,32,128]{2,1,0:T(8,128)(2,1)S(1)}, bf16[32,32,128]{2,1,0:T(8,128)(2,1)}, u32[]{:S(2)}) copy-start(bf16[32,32,128]{2,1,0:T(8,128)(2,1)} %refs_2_.3) | copy-start | bytes 786436
  40.5 4.6 %copy-start.7 = (f32[1024,128]{1,0:T(8,128)S(1)}, f32[1024,128]{1,0:T(8,128)}, u32[]{:S(2)}) copy-start(f32[1024,128]{1,0:T(8,128)} %get-tuple-element.19.refs_3_) | copy-start | bytes 1572868
  40.5 4.6 %copy-start.13 = (bf16[128,128]{1,0:T(8,128)(2,1)S(1)}, bf16[128,128]{1,0:T(8,128)(2,1)}, u32[]{:S(2)}) copy-start(bf16[128,128]{1,0:T(8,128)(2,1)} %refs_4_.3) | copy-start | bytes 98308
  (2 other events, 3.8 us)

commit v2 on v1

--- a/solution.py
+++ b/solution.py
@@ -107,7 +107,6 @@
     penalty = jnp.zeros((payload.shape[0] - rows, key_count), f32)
     for slot, block in enumerate(blocks):
         source = (me ^ slot) if relative else slot
-        block = rows_of(block, payload.shape[0], depth)
         place = iota((depth, key_count), 0)
         place = (place < positions) & (iota((depth, key_count), 1) == place + source * positions)
         penalty += dot(block[rows:, :], place.astype(bf16))
@@ -138,6 +137,11 @@
     depth = leave.shape[0]
     rows = lines * positions
     presence = []
+    blocks = [
+        block.at[part] if len(block.shape) == 3 else block
+        for block in blocks
+        for part in range(block.shape[0] if len(block.shape) == 3 else 1)
+    ]
     for slot, block in enumerate(blocks):
         projected = dot(block[:rows, :], entry[:, depth : 3 * depth])
         span = slice(slot * lines, (slot + 1) * lines)
@@ -200,7 +204,7 @@
     sources, outputs, rest = refs[:count], refs[count : count + 6], refs[count + 6 :]
     buffers, semaphores, tail = rest[:count], rest[count], rest[count + 1]
     fetch(sources, buffers, semaphores)
-    embedded, payload, bundle, gate, terms, near = outputs
+    embedded, payload, gate, terms, near, left = outputs
     embed_kernel(*buffers[:4], embedded, payload, tail)
     present_row, pairs, entry, logits = buffers[4:]
     lines, positions, width = pairs.shape
@@ -212,32 +216,34 @@
         for part in range(held // heads):
             base = index * held + part * heads
             terms[base : base + heads, :] = term[:, part * width : (part + 1) * width]
-    projected = dot(normed, entry[:, 2 * width :])
-    gate[...] = sigmoid(projected[:, 2 * width :])
-    operand = (sigmoid(projected[:, width : 2 * width]) * projected[:, :width]).astype(bf16)
+    projected = dot(normed, entry[...])
+    gate[...] = sigmoid(projected[:, 4 * width :])
+    left[...] = (sigmoid(projected[:, width : 2 * width]) * projected[:, :width]).astype(bf16)
+    operand = sigmoid(projected[:, 3 * width : 4 * width]) * projected[:, 2 * width : 3 * width]
+    operand = operand.astype(bf16)
     mask_right(lax.axis_index("res"), operand, present, present_row, near)
-    base = lines * positions
-    bundle[:base, :] = pairs[...].reshape(base, width)
-    for part in range(payload.shape[1] // width):
-        span = slice(base + part * payload.shape[0], base + (part + 1) * payload.shape[0])
-        bundle[span, :] = payload[:, part * width : (part + 1) * width]
-
-
-def rows_of(block, count, depth):
-    if block.shape == (count, depth):
-        return block[...]
-    parts = depth // block.shape[1]
-    base = block.shape[0] - parts * count
-    return jnp.concatenate(
-        [block[base + part * count : base + (part + 1) * count, :] for part in range(parts)], axis=1
-    )
-
-
-def turn_kernel(pairs, entry, terms, out):
+
+
+def hold_kernel(left, terms, out):
+    out[: left.shape[0], :] = left[...]
+    out[left.shape[0] :, :] = terms[...]
+
+
+def on_turn():
+    return lax.axis_index("res") % 2 == lax.axis_index("aux")
+
+
+def turn_kernel(pairs, entry, own, both, out):
     width = pairs.shape[2]
     operand = gated(pairs, entry[:, : 2 * width])
-    out[: operand.shape[0], :] = operand
-    out[operand.shape[0] :, :] = terms[...]
+    area = operand.shape[0]
+    both[:area, :] = jnp.where(on_turn(), own[:area, :].astype(f32), operand.astype(f32)).astype(
+        bf16
+    )
+    both[area : 2 * area, :] = operand
+    both[2 * area :, :] = own[area:, :]
+    out[:area, :] = operand
+    out[area:, :] = own[area:, :]
 
 
 def gated(pairs, weight):
@@ -326,48 +332,57 @@
     out[...] = (own[...].astype(f32) + update.reshape(out.shape)).astype(bf16)
 
 
-def far_kernel(lines, present, present_row, bundle, entry, right):
-    width = bundle.shape[1]
-    pairs = bundle[: lines * right.shape[1], :].reshape(right.shape)
+def far_kernel(present, present_row, turned, crossed, entry, right):
+    width = turned.shape[2]
+    pairs = jnp.where(on_turn(), turned[...].astype(f32), crossed[...].astype(f32))
     operand = gated(pairs, entry[:, 2 * width : 4 * width])
     mask_right(lax.axis_index("res") ^ 1, operand, present, present_row, right)
 
 
-def partial_kernel(other_half, own, beside, other, other_beside, near, far, total, left):
-    half = lax.axis_index("res") // 2
-    wanted = (1 - half) if other_half else half
-    mine = lax.axis_index("br") == wanted
-    straight = lax.axis_index("res") % 2 == lax.axis_index("aux")
-    count = total.shape[0]
-    lines = near.shape[0]
-
-    def load(first, second):
-        for slot, block in enumerate((first, second)):
-            for line in range(lines):
-                base = line * count
-                left[slot * lines + line] = block[base : base + count, :].astype(f32)
-
-    other_core = jnp.logical_not(mine)
-    crossed = jnp.logical_not(straight)
-    pl.when(mine & straight)(lambda: load(own, beside))
-    pl.when(mine & crossed)(lambda: load(beside, own))
-    pl.when(other_core & straight)(lambda: load(other, other_beside))
-    pl.when(other_core & crossed)(lambda: load(other_beside, other))
+def accumulate_rows(left, right, total_in, total):
     step = 8
 
     def body(index, carry):
         base = index * step
-        sums = [None] * step
-        for line in range(2 * lines):
-            right = near[line] if line < lines else far[line - lines]
+        sums = [None if total_in is None else total_in[base + t] for t in range(step)]
+        for line in range(right.shape[0]):
+            line_right = right[line]
             for t in range(step):
-                term = left[line, pl.ds(base + t, 1), :] * right
+                term = left[line, pl.ds(base + t, 1), :] * line_right
                 sums[t] = term if sums[t] is None else sums[t] + term
         for t in range(step):
             total[base + t] = sums[t].astype(total.dtype)
         return carry
 
-    lax.fori_loop(0, count // step, body, 0)
+    lax.fori_loop(0, total.shape[0] // step, body, 0)
+
+
+def load_left(block, base, left):
+    lines, count, _ = left.shape
+    for line in range(lines):
+        start = base + line * count
+        left[line] = block[start : start + count, :].astype(f32)
+
+
+def early_kernel(other_half, own, other, near, sums, left):
+    same = lax.axis_index("br") == lax.axis_index("res") // 2
+    mine = jnp.logical_not(same) if other_half else same
+    pl.when(mine)(lambda: load_left(own, 0, left))
+    pl.when(jnp.logical_not(mine))(lambda: load_left(other, 0, left))
+    accumulate_rows(left, near, None, sums)
+
+
+def late_kernel(other_half, came, passed, other_came, other_passed, far, sums, total, left):
+    same = lax.axis_index("br") == lax.axis_index("res") // 2
+    mine = jnp.logical_not(same) if other_half else same
+    turn = on_turn()
+    other, straight = jnp.logical_not(mine), jnp.logical_not(turn)
+    area = left.shape[0] * left.shape[1]
+    pl.when(mine & turn)(lambda: load_left(came, 0, left))
+    pl.when(mine & straight)(lambda: load_left(passed, 0, left))
+    pl.when(other & turn)(lambda: load_left(other_came, area, left))
+    pl.when(other & straight)(lambda: load_left(other_passed, 0, left))
+    accumulate_rows(left, far, sums, total)
 
 
 def finish_kernel(present, kept, own, gate, leave, *refs):
@@ -395,14 +410,28 @@
     return lax.ppermute(block, axis, [(i, i ^ bit) for i in range(lax.axis_size(axis))])
 
 
-def gather_side(block, ahead=()):
+def gather_side(block):
     if lax.axis_size("br") == 2 and lax.axis_size("aux") == 2:
         near = flip(block, "br")
         far = flip(block, "aux")
-        far = lax.optimization_barrier((far, *ahead))[0]
         return [block, far, near, flip(far, "br")], True
     whole = lax.all_gather(block, SIDE)
     return [whole[i] for i in range(whole.shape[0])], False
+
+
+def pair_up(block, other, out):
+    out[0] = block[...]
+    out[1] = other[...]
+
+
+def double(block, axis, bit, axis_after, ahead):
+    far = flip(block, axis, bit)
+    pair = call(pair_up, shape((2, *block.shape), block.dtype), after=ahead)(block, far)
+    return [pair, flip(pair, axis_after)]
+
+
+def double_side(block, ahead):
+    return double(block, "aux", 1, "br", ahead)
 
 
 def shape(dims, kind):
@@ -464,9 +493,12 @@
 def turn_pairs(pairs):
     index = lambda half, low, br, aux: ((half * 2 + low) * 2 + br) * 2 + aux
     every = [(h, low, br, aux) for h in (0, 1) for low in (0, 1) for br in (0, 1) for aux in (0, 1)]
-    return lax.ppermute(
-        pairs, ALL, [(index(h, l, br, a), index(h, a, br, l)) for h, l, br, a in every]
+    goes = lambda h, l, br, a: index(h, l, br, 1 - a) if a == l else index(h, 1 - l, br, a)
+    turned = lax.ppermute(pairs, ALL, [(index(*place), goes(*place)) for place in every])
+    crossed = lax.ppermute(
+        pairs, ALL, [(index(h, l, br, a), index(h, 1 - l, br, a)) for h, l, br, a in every if a == l]
     )
+    return turned, crossed
 
 
 def on_device(
@@ -509,15 +541,15 @@
         trimul_entry_matrix,
         couple_logit_matrix.T,
     )
-    embedded, payload, bundle, gate, terms, near = call(
+    embedded, payload, gate, terms, near, left = call(
         functools.partial(start_kernel, len(args)),
         (
             shape((rows, depth), f32),
             shape((rows + tail, depth), bf16),
-            shape((area + (rows + tail) * (depth // width), width), bf16),
             shape((area, width), f32),
             shape((3 * held, width), bf16),
             shape(couple_features.shape, f32),
+            shape((area, width), bf16),
         ),
         [pltpu.VMEM(x.shape, x.dtype) for x in args]
         + [pltpu.SemaphoreType.DMA((len(args),)), pltpu.VMEM((tail, depth), f32)],
@@ -526,29 +558,35 @@
     )(amino_present, *args)
     pending = ()
     if halves:
-        beside = flip(bundle, "res")
-        row_blocks = [payload, beside, flip(payload, "res", 2), flip(payload, "res", 3)]
-        row_relative = True
-        turned = call(turn_kernel, shape((area + 3 * held, width), bf16))(
-            turn_pairs(couple_features), trimul_entry_matrix, terms
-        )
-        terms, side_relative = gather_side(turned, (beside, *row_blocks[2:]))
-        far = call(
-            functools.partial(far_kernel, pair_rows),
-            shape(couple_features.shape, f32),
-            smem=1,
-            after=(turned,),
-        )(*presence, beside, trimul_entry_matrix)
-
-        def sums(other_half, kind, after):
-            return call(
-                functools.partial(partial_kernel, other_half),
-                shape(couple_features.shape, kind),
-                [pltpu.VMEM((2 * pair_rows, pair_cols, width), f32)],
-                after=after,
-            )(*terms, near, far)
-
-        sent = sums(True, bf16, ())
+        row_blocks, row_relative = gather(payload, "res")
+        turned, crossed = turn_pairs(couple_features)
+        turned, crossed = lax.optimization_barrier((turned, crossed))
+        held_left = call(hold_kernel, shape((area + 3 * held, width), bf16))(left, terms)
+        both, came = call(
+            turn_kernel,
+            (shape((2 * area + 3 * held, width), bf16), shape((area + 3 * held, width), bf16)),
+        )(turned, trimul_entry_matrix, held_left)
+        passed = flip(came, "aux")
+        other = flip(both, "br")
+        cube = shape(couple_features.shape, f32)
+        scratch = [pltpu.VMEM(couple_features.shape, f32)]
+        far = call(far_kernel, cube, smem=1)(*presence, turned, crossed, trimul_entry_matrix)
+        nearest = lax.optimization_barrier((near, far))[0]
+        early = lambda other_half, right: call(
+            functools.partial(early_kernel, other_half), cube, scratch
+        )(both, other, right)
+        sent = early(True, nearest)
+        ready = lax.optimization_barrier((passed, far, sent, *row_blocks[1:]))[0]
+        other_passed = flip(ready, "br")
+        operands = (came, passed, other, other_passed, far)
+        terms, side_relative = (came, passed, other, other_passed), True
+        late = lambda other_half, kind, sums, after: call(
+            functools.partial(late_kernel, other_half),
+            shape(couple_features.shape, kind),
+            scratch,
+            after=after,
+        )(*operands, sums)
+        sent = late(True, bf16, sent, ())
         received = flip(sent, "res", 2)
         pending = (sent,)
     else:
@@ -566,10 +604,13 @@
         ],
         after=pending,
     )(*terms, *row_blocks, payload, embedded, horizontal_entry_matrix, horizontal_exit_matrix)
-    column_blocks, _ = gather_side(payload)
     if halves:
-        kept = sums(False, f32, (payload,))
+        kept = early(False, lax.optimization_barrier((near, payload))[0])
+        column_blocks = double_side(payload, (kept,))
+        kept = late(False, f32, kept, ())
         pending = (kept,)
+    else:
+        column_blocks = gather_side(payload)[0]
     group = 8
     alignment_output = call(
         functools.partial(column_kernel, lines, positions, group, heads),

time: 47.1 us -> 44.8 us (0.951)
  starting transfers between devices: 15.2 us -> 12.6 us
  local copies, waits for them, and re-layouts: 0.86 us -> 1.82 us
  waiting for transfers between devices: 11.4 us -> 10.9 us
    ppermute x10 -> x9, starting transfers between devices: 13.6 us -> 7.59 us  [flip(): lax.ppermute(block, axis, [(i, i ^ bit) for i in range(lax.axis_size(axis...]
    ppermute x1 -> x2, starting transfers between devices: 1.61 us -> 5.01 us  [the longest x1 4.95 us: turn_pairs(): lax.ppermute(pairs, ALL, [(index(h, l, br, a), index(h, 1 - l, br, a)) fo...]
    ppermute x10 -> x9, waiting for transfers between devices: 11.4 us -> 8.65 us  [flip(): lax.ppermute(block, axis, [(i, i ^ bit) for i in range(lax.axis_size(axis...]
    ppermute x1 -> x2, waiting for transfers between devices: 0.01 us -> 2.27 us  [the longest x1 2.18 us: turn_pairs(): lax.ppermute(pairs, ALL, [(index(*place), goes(*place)) for place in every])]
    unnamed x30 -> x32, local copies, waits for them, and re-layouts: 0.86 us -> 1.82 us
    pallas_call x8 -> x12, Pallas kernels: 18.5 us -> 18.4 us  [run(): pl.pallas_call(ordered, out_shape=out_shape, in_specs=[pl.BlockSpec(memor...]
  transfers between devices with their start and end apart: 11 -> 11, of which waited for: 5 -> 6; matrix products, arithmetic and copies ran while one was open for 0% -> 0% of each run, Pallas kernels for 30% -> 33%
where the time goes in v2:
time: 44.8 us; the launch traced here: 44.6 us
  Pallas kernels  18.4 us (41%)
  starting transfers between devices  12.6 us (28%)
  waiting for transfers between devices  10.9 us (24%)
  local copies, waits for them, and re-layouts  1.82 us (4%)
  between operations  0.89 us (2%)
    pallas_call x12, Pallas kernels, run(): pl.pallas_call(ordered, out_shape=out_shape, in_specs=[pl.BlockSpec(memor...  18.4 us
    ppermute x9, waiting for transfers between devices, flip(): lax.ppermute(block, axis, [(i, i ^ bit) for i in range(lax.axis_size(axis...  8.65 us
    ppermute x9, starting transfers between devices, flip(): lax.ppermute(block, axis, [(i, i ^ bit) for i in range(lax.axis_size(axis...  7.59 us
    ppermute x1, starting transfers between devices, turn_pairs(): lax.ppermute(pairs, ALL, [(index(h, l, br, a), index(h, 1 - l, br, a)) fo...  4.95 us
    ppermute x1, waiting for transfers between devices, turn_pairs(): lax.ppermute(pairs, ALL, [(index(*place), goes(*place)) for place in every])  2.18 us
    unnamed x32, local copies, waits for them, and re-layouts  1.82 us
  transfers between devices with their start and end apart: 11, of which 6 were waited for; matrix products, arithmetic and copies ran while one was open for 0% of the time, Pallas kernels for 33%

profile of v2, /device:TPU:0, one launch (start us, length us, event | category | flops | bytes accessed | tf_op | source)
XLA Modules:
  0.0 44.6 jit_solution(11991207015318139019)
XLA Ops:
  0.6 4.9 %collective-permute-start.1 = (bf16[32,32,128]{2,1,0:T(8,128)(2,1)}, bf16[32,32,128]{2,1,0:T(8,128)(2,1)S(1)}, u32[]{:S(2)}, u32[]{:S(2)}) collective-permute-start(bf16[32,32,128]{2,1,0:T(8,128)(2,1)} %refs_2_.3), channel_id=1, source_target_pairs={{0,4},{2,6},{5,1},{7,3},{8,12},{10,14},{13,9},{15,11},{16,20},{18,... | collective-permute-start | bytes 786440 | tf_op jit(solution)/shard_map/ppermute | solution.py:498
  5.7 3.9 %shard_map.158 = (f32[128,256]{1,0:T(8,128)}, bf16[144,256]{1,0:T(8,128)(2,1)}, f32[1024,128]{1,0:T(8,128)}, bf16[192,128]{1,0:T(8,128)(2,1)}, f32[32,32,128]{2,1,0:T(8,128)}, /*index=5*/bf16[1024,128]{1,0:T(8,128)(2,1)}) custom-call(s32[128]{0:T(128)} %refs_0_.5, bf16[4,32,256]{2,1,0:T(8,128)(2,1)} %refs_1_.2, s32[4,32]{1,0:T(4,128)} %refs_2_.2, ...), custom_call_target="tpu_custom_call" | custom-call | flops 1 | bytes 1 | tf_op jit(solution)/shard_map/pallas_call | solution.py:448
  9.6 0.9 %copy-done.9 = bf16[1024,128]{1,0:T(8,128)(2,1)S(1)} copy-done((bf16[1024,128]{1,0:T(8,128)(2,1)S(1)}, bf16[1024,128]{1,0:T(8,128)(2,1)}, u32[]{:S(2)}) %copy-start.9) | copy-done | bytes 262168
  10.5 0.8 %copy-done.13 = bf16[192,128]{1,0:T(8,128)(2,1)S(1)} copy-done((bf16[192,128]{1,0:T(8,128)(2,1)S(1)}, bf16[192,128]{1,0:T(8,128)(2,1)}, u32[]{:S(2)}) %copy-start.13) | copy-done | bytes 49176
  11.3 0.1 collective-permute-done.1.refs_3_
  11.4 2.2 %collective-permute-done.refs_0_.refs_2_ = bf16[32,32,128]{2,1,0:T(8,128)(2,1)S(1)} collective-permute-done((bf16[32,32,128]{2,1,0:T(8,128)(2,1)}, bf16[32,32,128]{2,1,0:T(8,128)(2,1)S(1)}, u32[]{:S(2)}, u32[]{:S(2)}) %collective-permute-start) | collective-permute-done | bytes 262176 | tf_op jit(solution)/shard_map/ppermute | solution.py:497
  13.6 0.6 %shard_map.160 = (bf16[2240,128]{1,0:T(8,128)(2,1)S(1)}, bf16[1216,128]{1,0:T(8,128)(2,1)S(1)}) custom-call(bf16[32,32,128]{2,1,0:T(8,128)(2,1)S(1)} %collective-permute-done.refs_0_.refs_2_, bf16[128,640]{1,0:T(8,128)(2,1)S(1)} %copy-done.1, bf16[1216,128]{1,0:T(8,128)(2,1)S(1)} %shard_map.159.refs_2_), custom_call_target="tpu_custom_call" | custom-call | flops 1 | bytes 1 | tf_op jit(solution)/shard_map/pallas_call | solution.py:448
  14.3 0.6 %collective-permute-start.2 = (bf16[1216,128]{1,0:T(8,128)(2,1)S(1)}, bf16[1216,128]{1,0:T(8,128)(2,1)S(1)}, u32[]{:S(2)}, u32[]{:S(2)}) collective-permute-start(bf16[1216,128]{1,0:T(8,128)(2,1)S(1)} %get-tuple-element.20.refs_0_), channel_id=1, source_target_pairs={{0,1},{1,0},{2,3},{3,2},{4,5},{5,4},{6,7},{7,6},{8,9},{9,8},{10,11... | collective-permute-start | bytes 933896 | tf_op jit(solution)/shard_map/ppermute | solution.py:410
  14.9 3.4 %collective-permute-start.6 = (bf16[144,256]{1,0:T(8,128)(2,1)S(1)}, bf16[144,256]{1,0:T(8,128)(2,1)S(1)}, u32[]{:S(2)}, u32[]{:S(2)}) collective-permute-start(bf16[144,256]{1,0:T(8,128)(2,1)S(1)} %copy-done.8), channel_id=1, source_target_pairs={{0,12},{4,8},{8,4},{12,0},{1,13},{5,9},{9,5},{13,1},{2,14},{6,10},... | collective-permute-start | bytes 221192 | tf_op jit(solution)/shard_map/ppermute | solution.py:410
  18.3 0.9 %collective-permute-start.4 = (bf16[144,256]{1,0:T(8,128)(2,1)S(1)}, bf16[144,256]{1,0:T(8,128)(2,1)S(1)}, u32[]{:S(2)}, u32[]{:S(2)}) collective-permute-start(bf16[144,256]{1,0:T(8,128)(2,1)S(1)} %copy-done.8), channel_id=1, source_target_pairs={{0,4},{4,0},{8,12},{12,8},{1,5},{5,1},{9,13},{13,9},{2,6},{6,2},{1... | collective-permute-start | bytes 221192 | tf_op jit(solution)/shard_map/ppermute | solution.py:410
  19.3 1.1 %shard_map.161.refs_4_ = f32[32,32,128]{2,1,0:T(8,128)S(1)} custom-call(s32[128]{0:T(128)S(1)} %copy-done.15, s32[1,128]{1,0:T(1,128)S(1)} %bitcast.3, bf16[32,32,128]{2,1,0:T(8,128)(2,1)S(1)} %collective-permute-done.refs_0_.refs_2_, bf16[32,32,128]{2,1,0:T(8,128)(2,1)S(1)} %collective-permute-done.1.refs_3_, bf16[128,640]{1,0:T(8,128)(2,1)S(1)} %copy-done.1), custom_call_target="tpu_custom_call" | custom-call | flops 1 | bytes 1 | tf_op jit(solution)/shard_map/pallas_call | solution.py:448
  20.4 1.6 %shard_map.162.refs_5_ = f32[32,32,128]{2,1,0:T(8,128)S(1)} custom-call(bf16[2240,128]{1,0:T(8,128)(2,1)S(1)} %get-tuple-element.21.refs_0_, bf16[2240,128]{1,0:T(8,128)(2,1)S(1)} %collective-permute-done.3.refs_1_.refs_2_, f32[32,32,128]{2,1,0:T(8,128)S(1)} %copy-done), custom_call_target="tpu_custom_call" | custom-call | flops 1 | bytes 1 | tf_op jit(solution)/shard_map/pallas_call | solution.py:448
  22.0 2.8 %collective-permute-done.5.refs_6_ = bf16[144,256]{1,0:T(8,128)(2,1)S(1)} collective-permute-done((bf16[144,256]{1,0:T(8,128)(2,1)S(1)}, bf16[144,256]{1,0:T(8,128)(2,1)S(1)}, u32[]{:S(2)}, u32[]{:S(2)}) %collective-permute-start.5) | collective-permute-done | bytes 73760 | tf_op jit(solution)/shard_map/ppermute | solution.py:410
  24.8 1.6 %collective-permute-done.7.refs_3_ = bf16[1216,128]{1,0:T(8,128)(2,1)S(1)} collective-permute-done((bf16[1216,128]{1,0:T(8,128)(2,1)S(1)}, bf16[1216,128]{1,0:T(8,128)(2,1)S(1)}, u32[]{:S(2)}, u32[]{:S(2)}) %collective-permute-start.7) | collective-permute-done | bytes 311328 | tf_op jit(solution)/shard_map/ppermute | solution.py:410
  26.4 1.5 %shard_map.163.refs_12_ = bf16[32,32,128]{2,1,0:T(8,128)(2,1)S(1)} custom-call(bf16[1216,128]{1,0:T(8,128)(2,1)S(1)} %get-tuple-element.20.refs_0_, bf16[1216,128]{1,0:T(8,128)(2,1)S(1)} %collective-permute-done.2.refs_1_, bf16[2240,128]{1,0:T(8,128)(2,1)S(1)} %collective-permute-done.3.refs_1_.refs_2_, ...), custom_call_target="tpu_custom_call" | custom-call | flops 1 | bytes 1 | tf_op jit(solution)/shard_map/pallas_call | solution.py:448
  27.9 1.9 %collective-permute-start.10 = (bf16[32,32,128]{2,1,0:T(8,128)(2,1)S(1)}, bf16[32,32,128]{2,1,0:T(8,128)(2,1)S(1)}, u32[]{:S(2)}, u32[]{:S(2)}) collective-permute-start(bf16[32,32,128]{2,1,0:T(8,128)(2,1)S(1)} %shard_map.163.refs_12_), channel_id=1, source_target_pairs={{0,8},{4,12},{8,0},{12,4},{1,9},{5,13},{9,1},{13,5},{2,10},{6,14},... | collective-permute-start | bytes 786440 | tf_op jit(solution)/shard_map/ppermute | solution.py:410
  29.8 1.6 %shard_map.164 = (f32[128,256]{1,0:T(8,128)S(1)}, bf16[144,256]{1,0:T(8,128)(2,1)S(1)}) custom-call(bf16[1216,128]{1,0:T(8,128)(2,1)S(1)} %get-tuple-element.20.refs_0_, bf16[1216,128]{1,0:T(8,128)(2,1)S(1)} %collective-permute-done.2.refs_1_, bf16[2240,128]{1,0:T(8,128)(2,1)S(1)} %collective-permute-done.3.refs_1_.refs_2_, ...), custom_call_target="tpu_custom_call" | custom-call | flops 1 | bytes 1 | tf_op jit(solution)/shard_map/pallas_call | solution.py:448
  31.4 0.6 %collective-permute-start.8 = (bf16[144,256]{1,0:T(8,128)(2,1)S(1)}, bf16[144,256]{1,0:T(8,128)(2,1)S(1)}, u32[]{:S(2)}, u32[]{:S(2)}) collective-permute-start(bf16[144,256]{1,0:T(8,128)(2,1)S(1)} %get-tuple-element.28.refs_0_.refs_2_), channel_id=1, source_target_pairs={{0,1},{1,0},{2,3},{3,2},{4,5},{5,4},{6,7},{7,6},{8,9},{9,8},{10,11... | collective-permute-start | bytes 221192 | tf_op jit(solution)/shard_map/ppermute | solution.py:410
  32.0 1.5 %shard_map.165.refs_2_.refs_5_ = f32[32,32,128]{2,1,0:T(8,128)S(1)} custom-call(bf16[2240,128]{1,0:T(8,128)(2,1)S(1)} %get-tuple-element.21.refs_0_, bf16[2240,128]{1,0:T(8,128)(2,1)S(1)} %collective-permute-done.3.refs_1_.refs_2_, f32[32,32,128]{2,1,0:T(8,128)S(1)} %copy-done), custom_call_target="tpu_custom_call" | custom-call | flops 1 | bytes 1 | tf_op jit(solution)/shard_map/pallas_call | solution.py:448
  33.5 2.3 %collective-permute-done.8.refs_1_ = bf16[144,256]{1,0:T(8,128)(2,1)S(1)} collective-permute-done((bf16[144,256]{1,0:T(8,128)(2,1)S(1)}, bf16[144,256]{1,0:T(8,128)(2,1)S(1)}, u32[]{:S(2)}, u32[]{:S(2)}) %collective-permute-start.8) | collective-permute-done | bytes 73760 | tf_op jit(solution)/shard_map/ppermute | solution.py:410
  35.9 1.6 %shard_map.167.refs_8_.refs_1_ = f32[32,32,128]{2,1,0:T(8,128)S(1)} custom-call(bf16[1216,128]{1,0:T(8,128)(2,1)S(1)} %get-tuple-element.20.refs_0_, bf16[1216,128]{1,0:T(8,128)(2,1)S(1)} %collective-permute-done.2.refs_1_, bf16[2240,128]{1,0:T(8,128)(2,1)S(1)} %collective-permute-done.3.refs_1_.refs_2_, ...), custom_call_target="tpu_custom_call" | custom-call | flops 1 | bytes 1 | tf_op jit(solution)/shard_map/pallas_call | solution.py:448
  37.5 3.3 %shard_map.168 = bf16[4,32,256]{2,1,0:T(8,128)(2,1)} custom-call(bf16[2,144,256]{2,1,0:T(8,128)(2,1)S(1)} %shard_map.166.refs_0_, bf16[2,144,256]{2,1,0:T(8,128)(2,1)S(1)} %collective-permute-done.9.refs_1_, bf16[144,256]{1,0:T(8,128)(2,1)S(1)} %get-tuple-element.28.refs_0_.refs_2_, f32[128,256]{1,0:T(8,128)S(1)} %get-tuple-element.30.refs_3_, ...), custom_call_target="tpu_custom_call" | custom-call | flops 1 | bytes 1 | tf_op jit(solution)/shard_map/pallas_call | solution.py:448
  40.8 2.0 %collective-permute-done.10.refs_5_ = bf16[32,32,128]{2,1,0:T(8,128)(2,1)S(1)} collective-permute-done((bf16[32,32,128]{2,1,0:T(8,128)(2,1)S(1)}, bf16[32,32,128]{2,1,0:T(8,128)(2,1)S(1)}, u32[]{:S(2)}, u32[]{:S(2)}) %collective-permute-start.10) | collective-permute-done | bytes 262176 | tf_op jit(solution)/shard_map/ppermute | solution.py:410
  42.9 1.7 %shard_map.169 = bf16[32,32,128]{2,1,0:T(8,128)(2,1)} custom-call(s32[128]{0:T(128)S(1)} %copy-done.15, f32[32,32,128]{2,1,0:T(8,128)S(1)} %shard_map.167.refs_8_.refs_1_, bf16[32,32,128]{2,1,0:T(8,128)(2,1)S(1)} %copy-done.2, f32[1024,128]{1,0:T(8,128)S(1)} %copy-done.7, bf16[128,128]{1,0:T(8,128)(2,1)S(1)} %copy-done.14, ...), custom_call_target="tpu_custom_call" | custom-call | flops 1 | bytes 1 | tf_op jit(solution)/shard_map/pallas_call | solution.py:448
  (42 shorter events, 0.3 us)
Async XLA Ops:
  0.6 10.8 %collective-permute-start.1 = (bf16[32,32,128]{2,1,0:T(8,128)(2,1)}, bf16[32,32,128]{2,1,0:T(8,128)(2,1)S(1)}, u32[]{:S(2)}, u32[]{:S(2)}) collective-permute-start(bf16[32,32,128]{2,1,0:T(8,128)(2,1)} %refs_2_.3), channel_id=1, source_target_pairs={{0,4},{2,6},{5,1},{7,3},{8,12},{10,14},{13,9},{15,11},{16,20},{18,... | collective-permute-start | bytes 786440 | tf_op jit(solution)/shard_map/ppermute | solution.py:498
  5.6 8.0 %collective-permute-start = (bf16[32,32,128]{2,1,0:T(8,128)(2,1)}, bf16[32,32,128]{2,1,0:T(8,128)(2,1)S(1)}, u32[]{:S(2)}, u32[]{:S(2)}) collective-permute-start(bf16[32,32,128]{2,1,0:T(8,128)(2,1)} %refs_2_.3), channel_id=1, source_target_pairs={{0,1},{1,5},{2,3},{3,7},{4,0},{5,4},{6,2},{7,6},{8,9},{9,13},{10,1... | collective-permute-start | bytes 786440 | tf_op jit(solution)/shard_map/ppermute | solution.py:497
  11.3 2.3 %copy-start.1 = (bf16[128,640]{1,0:T(8,128)(2,1)S(1)}, bf16[128,640]{1,0:T(8,128)(2,1)}, u32[]{:S(2)}) copy-start(bf16[128,640]{1,0:T(8,128)(2,1)} %refs_4_.5) | copy-start | bytes 491524
  11.3 3.5 %copy-start.8 = (bf16[144,256]{1,0:T(8,128)(2,1)S(1)}, bf16[144,256]{1,0:T(8,128)(2,1)}, u32[]{:S(2)}) copy-start(bf16[144,256]{1,0:T(8,128)(2,1)} %get-tuple-element.25.refs_4_.refs_8_) | copy-start | bytes 221188
  14.2 6.2 %collective-permute-start.3 = (bf16[2240,128]{1,0:T(8,128)(2,1)S(1)}, bf16[2240,128]{1,0:T(8,128)(2,1)S(1)}, u32[]{:S(2)}, u32[]{:S(2)}) collective-permute-start(bf16[2240,128]{1,0:T(8,128)(2,1)S(1)} %get-tuple-element.21.refs_0_), channel_id=1, source_target_pairs={{0,2},{2,0},{1,3},{3,1},{4,6},{6,4},{5,7},{7,5},{8,10},{10,8},{9,1... | collective-permute-start | bytes 1720328 | tf_op jit(solution)/shard_map/ppermute | solution.py:410
  14.3 5.0 %copy-start.15 = (s32[128]{0:T(128)S(1)}, s32[128]{0:T(128)}, u32[]{:S(2)}) copy-start(s32[128]{0:T(128)} %refs_0_.5) | copy-start | bytes 1540
  14.3 10.5 %collective-permute-start.2 = (bf16[1216,128]{1,0:T(8,128)(2,1)S(1)}, bf16[1216,128]{1,0:T(8,128)(2,1)S(1)}, u32[]{:S(2)}, u32[]{:S(2)}) collective-permute-start(bf16[1216,128]{1,0:T(8,128)(2,1)S(1)} %get-tuple-element.20.refs_0_), channel_id=1, source_target_pairs={{0,1},{1,0},{2,3},{3,2},{4,5},{5,4},{6,7},{7,6},{8,9},{9,8},{10,11... | collective-permute-start | bytes 933896 | tf_op jit(solution)/shard_map/ppermute | solution.py:410
  14.9 5.6 %copy-start = (f32[32,32,128]{2,1,0:T(8,128)S(1)}, f32[32,32,128]{2,1,0:T(8,128)}, u32[]{:S(2)}) copy-start(f32[32,32,128]{2,1,0:T(8,128)} %get-tuple-element.29.refs_2_) | copy-start | bytes 1572868
  14.9 7.1 %collective-permute-start.6 = (bf16[144,256]{1,0:T(8,128)(2,1)S(1)}, bf16[144,256]{1,0:T(8,128)(2,1)S(1)}, u32[]{:S(2)}, u32[]{:S(2)}) collective-permute-start(bf16[144,256]{1,0:T(8,128)(2,1)S(1)} %copy-done.8), channel_id=1, source_target_pairs={{0,12},{4,8},{8,4},{12,0},{1,13},{5,9},{9,5},{13,1},{2,14},{6,10},... | collective-permute-start | bytes 221192 | tf_op jit(solution)/shard_map/ppermute | solution.py:410
  18.3 6.5 %collective-permute-start.5 = (bf16[144,256]{1,0:T(8,128)(2,1)S(1)}, bf16[144,256]{1,0:T(8,128)(2,1)S(1)}, u32[]{:S(2)}, u32[]{:S(2)}) collective-permute-start(bf16[144,256]{1,0:T(8,128)(2,1)S(1)} %copy-done.8), channel_id=1, source_target_pairs={{0,8},{4,12},{8,0},{12,4},{1,9},{5,13},{9,1},{13,5},{2,10},{6,14},... | collective-permute-start | bytes 221192 | tf_op jit(solution)/shard_map/ppermute | solution.py:410
  18.3 6.5 %collective-permute-start.4 = (bf16[144,256]{1,0:T(8,128)(2,1)S(1)}, bf16[144,256]{1,0:T(8,128)(2,1)S(1)}, u32[]{:S(2)}, u32[]{:S(2)}) collective-permute-start(bf16[144,256]{1,0:T(8,128)(2,1)S(1)} %copy-done.8), channel_id=1, source_target_pairs={{0,4},{4,0},{8,12},{12,8},{1,5},{5,1},{9,13},{13,9},{2,6},{6,2},{1... | collective-permute-start | bytes 221192 | tf_op jit(solution)/shard_map/ppermute | solution.py:410
  22.0 7.8 %copy-start.3 = (bf16[256,1024]{1,0:T(8,128)(2,1)S(1)}, bf16[256,1024]{1,0:T(8,128)(2,1)}, u32[]{:S(2)}) copy-start(bf16[256,1024]{1,0:T(8,128)(2,1)} %refs_10_.1) | copy-start | bytes 1572868
  22.0 7.8 %copy-start.10 = (bf16[256,256]{1,0:T(8,128)(2,1)S(1)}, bf16[256,256]{1,0:T(8,128)(2,1)}, u32[]{:S(2)}) copy-start(bf16[256,256]{1,0:T(8,128)(2,1)} %refs_11_.1) | copy-start | bytes 393220
  22.0 7.8 %copy-start.12 = (f32[128,256]{1,0:T(8,128)S(1)}, f32[128,256]{1,0:T(8,128)}, u32[]{:S(2)}) copy-start(f32[128,256]{1,0:T(8,128)} %get-tuple-element.27.refs_9_) | copy-start | bytes 393220
  24.8 1.6 %collective-permute-start.7 = (bf16[1216,128]{1,0:T(8,128)(2,1)S(1)}, bf16[1216,128]{1,0:T(8,128)(2,1)S(1)}, u32[]{:S(2)}, u32[]{:S(2)}) collective-permute-start(bf16[1216,128]{1,0:T(8,128)(2,1)S(1)} %collective-permute-done.2.refs_1_), channel_id=1, source_target_pairs={{0,2},{2,0},{1,3},{3,1},{4,6},{6,4},{5,7},{7,5},{8,10},{10,8},{9,1... | collective-permute-start | bytes 933896 | tf_op jit(solution)/shard_map/ppermute | solution.py:410
  27.9 14.9 %collective-permute-start.10 = (bf16[32,32,128]{2,1,0:T(8,128)(2,1)S(1)}, bf16[32,32,128]{2,1,0:T(8,128)(2,1)S(1)}, u32[]{:S(2)}, u32[]{:S(2)}) collective-permute-start(bf16[32,32,128]{2,1,0:T(8,128)(2,1)S(1)} %shard_map.163.refs_12_), channel_id=1, source_target_pairs={{0,8},{4,12},{8,0},{12,4},{1,9},{5,13},{9,1},{13,5},{2,10},{6,14},... | collective-permute-start | bytes 786440 | tf_op jit(solution)/shard_map/ppermute | solution.py:410
  31.4 4.4 %collective-permute-start.8 = (bf16[144,256]{1,0:T(8,128)(2,1)S(1)}, bf16[144,256]{1,0:T(8,128)(2,1)S(1)}, u32[]{:S(2)}, u32[]{:S(2)}) collective-permute-start(bf16[144,256]{1,0:T(8,128)(2,1)S(1)} %get-tuple-element.28.refs_0_.refs_2_), channel_id=1, source_target_pairs={{0,1},{1,0},{2,3},{3,2},{4,5},{5,4},{6,7},{7,6},{8,9},{9,8},{10,11... | collective-permute-start | bytes 221192 | tf_op jit(solution)/shard_map/ppermute | solution.py:410
  35.8 1.7 %copy-start.4 = (bf16[256,1024]{1,0:T(8,128)(2,1)S(1)}, bf16[256,1024]{1,0:T(8,128)(2,1)}, u32[]{:S(2)}) copy-start(bf16[256,1024]{1,0:T(8,128)(2,1)} %refs_4_.6) | copy-start | bytes 1572868
  35.8 1.7 %copy-start.5 = (bf16[256,1024]{1,0:T(8,128)(2,1)S(1)}, bf16[256,1024]{1,0:T(8,128)(2,1)}, u32[]{:S(2)}) copy-start(bf16[256,1024]{1,0:T(8,128)(2,1)} %refs_6_.3) | copy-start | bytes 1572868
  35.8 1.7 %copy-start.6 = (bf16[1024,256]{1,0:T(8,128)(2,1)S(1)}, bf16[1024,256]{1,0:T(8,128)(2,1)}, u32[]{:S(2)}) copy-start(bf16[1024,256]{1,0:T(8,128)(2,1)} %refs_7_.3) | copy-start | bytes 1572868
  35.8 1.7 %collective-permute-start.9 = (bf16[2,144,256]{2,1,0:T(8,128)(2,1)S(1)}, bf16[2,144,256]{2,1,0:T(8,128)(2,1)S(1)}, u32[]{:S(2)}, u32[]{:S(2)}) collective-permute-start(bf16[2,144,256]{2,1,0:T(8,128)(2,1)S(1)} %shard_map.166.refs_0_), channel_id=1, source_target_pairs={{0,2},{2,0},{1,3},{3,1},{4,6},{6,4},{5,7},{7,5},{8,10},{10,8},{9,1... | collective-permute-start | bytes 442376 | tf_op jit(solution)/shard_map/ppermute | solution.py:410
  37.5 5.3 %copy-start.2 = (bf16[32,32,128]{2,1,0:T(8,128)(2,1)S(1)}, bf16[32,32,128]{2,1,0:T(8,128)(2,1)}, u32[]{:S(2)}) copy-start(bf16[32,32,128]{2,1,0:T(8,128)(2,1)} %refs_2_.3) | copy-start | bytes 786436
  37.5 5.3 %copy-start.7 = (f32[1024,128]{1,0:T(8,128)S(1)}, f32[1024,128]{1,0:T(8,128)}, u32[]{:S(2)}) copy-start(f32[1024,128]{1,0:T(8,128)} %get-tuple-element.31.refs_3_) | copy-start | bytes 1572868
  37.5 5.3 %copy-start.14 = (bf16[128,128]{1,0:T(8,128)(2,1)S(1)}, bf16[128,128]{1,0:T(8,128)(2,1)}, u32[]{:S(2)}) copy-start(bf16[128,128]{1,0:T(8,128)(2,1)} %refs_4_.7) | copy-start | bytes 98308
  (3 other events, 3.5 us)

commit v3 on v2

--- a/solution.py
+++ b/solution.py
@@ -73,8 +73,9 @@
     return jnp.sum(mixed * own[None], axis=1)
 
 
-def row_kernel(relative, side_relative, sides, lines, positions, *refs):
-    terms, refs = refs[:sides], refs[sides:]
+def row_kernel(relative, side_relative, places, lines, positions, *refs):
+    used = 1 + max(max(index, index if other is None else other) for index, _, other in places)
+    terms, refs = refs[:used], refs[used:]
     blocks = refs[: len(refs) - 10]
     own, embedded, entry, leave, after, payload, bias, keys, values, mix = refs[len(refs) - 10 :]
     depth = leave.shape[0]
@@ -86,14 +87,18 @@
     per = lanes // positions
     side = side_index()
     sums = []
-    for term in terms:
-        held = positions * heads // per
-        base = term.shape[0] - 3 * held
-        sums.append(
-            term[base : base + held, :].astype(f32)
-            + term[base + held : base + 2 * held, :].astype(f32)
-            + term[base + 2 * held :, :].astype(f32)
-        )
+    held = positions * heads // per
+    sums = []
+    for source, start, other in places:
+        parts = []
+        for index in range(3):
+            first = index * held
+            part = terms[source][start + first : start + first + held, :].astype(f32)
+            if other is not None:
+                choice = terms[other][first : first + held, :].astype(f32)
+                part = jnp.where(on_turn(), choice, part)
+            parts.append(part)
+        sums.append(parts[0] + parts[1] + parts[2])
     place = iota((heads, key_count), 1) // positions
     for line in range(positions):
         total = jnp.zeros((heads, key_count), f32)
@@ -200,6 +205,15 @@
     return high, middle, (rest - middle.astype(f32)).astype(bf16)
 
 
+def store_terms(logit, out, start):
+    heads, count = logit.shape
+    lanes = out.shape[1]
+    for index, term in enumerate(split(logit)):
+        for part in range(count // lanes):
+            base = start + (index * (count // lanes) + part) * heads
+            out[base : base + heads, :] = term[:, part * lanes : (part + 1) * lanes]
+
+
 def start_kernel(count, present, *refs):
     sources, outputs, rest = refs[:count], refs[count : count + 6], refs[count + 6 :]
     buffers, semaphores, tail = rest[:count], rest[count], rest[count + 1]
@@ -211,11 +225,7 @@
     heads = logits.shape[0]
     normed = normalize(pairs[...].astype(f32).reshape(lines * positions, width)).astype(bf16)
     logit = lax.dot_general(logits[...], normed, NT, preferred_element_type=f32)
-    held = terms.shape[0] // 3
-    for index, term in enumerate(split(logit)):
-        for part in range(held // heads):
-            base = index * held + part * heads
-            terms[base : base + heads, :] = term[:, part * width : (part + 1) * width]
+    store_terms(logit, terms, 0)
     projected = dot(normed, entry[...])
     gate[...] = sigmoid(projected[:, 4 * width :])
     left[...] = (sigmoid(projected[:, width : 2 * width]) * projected[:, :width]).astype(bf16)
@@ -224,26 +234,26 @@
     mask_right(lax.axis_index("res"), operand, present, present_row, near)
 
 
-def hold_kernel(left, terms, out):
-    out[: left.shape[0], :] = left[...]
-    out[left.shape[0] :, :] = terms[...]
-
-
 def on_turn():
     return lax.axis_index("res") % 2 == lax.axis_index("aux")
 
 
-def turn_kernel(pairs, entry, own, both, out):
-    width = pairs.shape[2]
-    operand = gated(pairs, entry[:, : 2 * width])
-    area = operand.shape[0]
-    both[:area, :] = jnp.where(on_turn(), own[:area, :].astype(f32), operand.astype(f32)).astype(
-        bf16
-    )
-    both[area : 2 * area, :] = operand
-    both[2 * area :, :] = own[area:, :]
-    out[:area, :] = operand
-    out[area:, :] = own[area:, :]
+def turn_kernel(pairs, entry, logits, terms, came, given, both):
+    lines, positions, width = pairs.shape
+    held = terms.shape[0]
+    normed = normalize(pairs[...].astype(f32).reshape(lines * positions, width)).astype(bf16)
+    projected = dot(normed, entry[:, : 2 * width])
+    operand = (sigmoid(projected[:, width:]) * projected[:, :width]).astype(bf16)
+    came[...] = operand
+    given[...] = operand
+
+    @pl.when(jnp.logical_not(on_turn()))
+    def _():
+        given[:held, :] = terms[...]
+
+    both[:held, :] = terms[...]
+    logit = lax.dot_general(logits[...], normed, NT, preferred_element_type=f32)
+    store_terms(logit, both, held)
 
 
 def gated(pairs, weight):
@@ -364,11 +374,15 @@
         left[line] = block[start : start + count, :].astype(f32)
 
 
-def early_kernel(other_half, own, other, near, sums, left):
+def early_kernel(other_half, own, came, other_own, other_came, near, sums, left):
     same = lax.axis_index("br") == lax.axis_index("res") // 2
     mine = jnp.logical_not(same) if other_half else same
-    pl.when(mine)(lambda: load_left(own, 0, left))
-    pl.when(jnp.logical_not(mine))(lambda: load_left(other, 0, left))
+    turn = on_turn()
+    other, straight = jnp.logical_not(mine), jnp.logical_not(turn)
+    pl.when(mine & turn)(lambda: load_left(own, 0, left))
+    pl.when(mine & straight)(lambda: load_left(came, 0, left))
+    pl.when(other & turn)(lambda: load_left(other_own, 0, left))
+    pl.when(other & straight)(lambda: load_left(other_came, 0, left))
     accumulate_rows(left, near, None, sums)
 
 
@@ -377,10 +391,9 @@
     mine = jnp.logical_not(same) if other_half else same
     turn = on_turn()
     other, straight = jnp.logical_not(mine), jnp.logical_not(turn)
-    area = left.shape[0] * left.shape[1]
     pl.when(mine & turn)(lambda: load_left(came, 0, left))
     pl.when(mine & straight)(lambda: load_left(passed, 0, left))
-    pl.when(other & turn)(lambda: load_left(other_came, area, left))
+    pl.when(other & turn)(lambda: load_left(other_came, 0, left))
     pl.when(other & straight)(lambda: load_left(other_passed, 0, left))
     accumulate_rows(left, far, sums, total)
 
@@ -560,26 +573,25 @@
     if halves:
         row_blocks, row_relative = gather(payload, "res")
         turned, crossed = turn_pairs(couple_features)
-        turned, crossed = lax.optimization_barrier((turned, crossed))
-        held_left = call(hold_kernel, shape((area + 3 * held, width), bf16))(left, terms)
-        both, came = call(
-            turn_kernel,
-            (shape((2 * area + 3 * held, width), bf16), shape((area + 3 * held, width), bf16)),
-        )(turned, trimul_entry_matrix, held_left)
-        passed = flip(came, "aux")
-        other = flip(both, "br")
+        flat = shape((area, width), bf16)
+        came, given, terms = call(turn_kernel, (flat, flat, shape((6 * held, width), bf16)))(
+            turned, trimul_entry_matrix, couple_logit_matrix.T, terms
+        )
+        passed = flip(given, "aux")
+        other_left, other_came = flip(left, "br"), flip(came, "br")
         cube = shape(couple_features.shape, f32)
         scratch = [pltpu.VMEM(couple_features.shape, f32)]
         far = call(far_kernel, cube, smem=1)(*presence, turned, crossed, trimul_entry_matrix)
         nearest = lax.optimization_barrier((near, far))[0]
         early = lambda other_half, right: call(
             functools.partial(early_kernel, other_half), cube, scratch
-        )(both, other, right)
+        )(left, came, other_left, other_came, right)
         sent = early(True, nearest)
-        ready = lax.optimization_barrier((passed, far, sent, *row_blocks[1:]))[0]
+        ready = lax.optimization_barrier((passed, far, sent, row_blocks[2], row_blocks[3], row_blocks[1]))[0]
         other_passed = flip(ready, "br")
-        operands = (came, passed, other, other_passed, far)
-        terms, side_relative = (came, passed, other, other_passed), True
+        operands = (came, passed, other_came, other_passed, far)
+        terms, side_relative = (terms, flip(terms, "br"), passed, other_passed), True
+        places = [(0, 0, None), (0, 3 * held, 2), (1, 0, None), (1, 3 * held, 3)]
         late = lambda other_half, kind, sums, after: call(
             functools.partial(late_kernel, other_half),
             shape(couple_features.shape, kind),
@@ -592,9 +604,10 @@
     else:
         row_blocks, row_relative = gather(payload, "res")
         terms, side_relative = gather_side(terms)
+        places = [(index, 0, None) for index in range(side)]
 
     after, payload = call(
-        functools.partial(row_kernel, row_relative, side_relative, side, lines, positions),
+        functools.partial(row_kernel, row_relative, side_relative, places, lines, positions),
         (shape((rows, depth), f32), shape((rows + tail, depth), bf16)),
         [
             pltpu.VMEM((pair_rows * heads, residues), f32),

time: 44.8 us -> 43.5 us (0.971)
  waiting for transfers between devices: 10.9 us -> 6.92 us
  starting transfers between devices: 12.6 us -> 15.7 us
  local copies, waits for them, and re-layouts: 1.82 us -> 1.04 us
    ppermute x9 -> x11, starting transfers between devices: 7.59 us -> 10.7 us  [flip(): lax.ppermute(block, axis, [(i, i ^ bit) for i in range(lax.axis_size(axis...]
    ppermute x1, starting transfers between devices: 0.06 us -> 2.99 us  [turn_pairs(): lax.ppermute(pairs, ALL, [(index(*place), goes(*place)) for place in every])]
    ppermute x1, starting transfers between devices: 4.95 us -> 2.02 us  [turn_pairs(): lax.ppermute(pairs, ALL, [(index(h, l, br, a), index(h, 1 - l, br, a)) fo...]
    ppermute x9 -> x11, waiting for transfers between devices: 8.65 us -> 6.48 us  [flip(): lax.ppermute(block, axis, [(i, i ^ bit) for i in range(lax.axis_size(axis...]
    ppermute x1, waiting for transfers between devices: 2.18 us -> 0.43 us  [turn_pairs(): lax.ppermute(pairs, ALL, [(index(*place), goes(*place)) for place in every])]
    unnamed x32 -> x34, local copies, waits for them, and re-layouts: 1.82 us -> 1.04 us
    pallas_call x12 -> x11, Pallas kernels: 18.4 us -> 18.7 us  [run(): pl.pallas_call(ordered, out_shape=out_shape, in_specs=[pl.BlockSpec(memor...]
  transfers between devices with their start and end apart: 11 -> 13, of which waited for: 6 -> 6; matrix products, arithmetic and copies ran while one was open for 0% -> 0% of each run, Pallas kernels for 33% -> 39%
where the time goes in v3:
time: 43.5 us; the launch traced here: 43.3 us
  Pallas kernels  18.7 us (43%)
  starting transfers between devices  15.7 us (36%)
  waiting for transfers between devices  6.92 us (16%)
  local copies, waits for them, and re-layouts  1.04 us (2%)
  between operations  0.89 us (2%)
    pallas_call x11, Pallas kernels, run(): pl.pallas_call(ordered, out_shape=out_shape, in_specs=[pl.BlockSpec(memor...  18.7 us
    ppermute x11, starting transfers between devices, flip(): lax.ppermute(block, axis, [(i, i ^ bit) for i in range(lax.axis_size(axis...  10.7 us
    ppermute x11, waiting for transfers between devices, flip(): lax.ppermute(block, axis, [(i, i ^ bit) for i in range(lax.axis_size(axis...  6.48 us
    ppermute x1, starting transfers between devices, turn_pairs(): lax.ppermute(pairs, ALL, [(index(*place), goes(*place)) for place in every])  2.99 us
    ppermute x1, starting transfers between devices, turn_pairs(): lax.ppermute(pairs, ALL, [(index(h, l, br, a), index(h, 1 - l, br, a)) fo...  2.02 us
    unnamed x34, local copies, waits for them, and re-layouts  1.04 us
  transfers between devices with their start and end apart: 13, of which 6 were waited for; matrix products, arithmetic and copies ran while one was open for 0% of the time, Pallas kernels for 39%

profile of v3, /device:TPU:0, one launch (start us, length us, event | category | flops | bytes accessed | tf_op | source)
XLA Modules:
  0.0 43.3 jit_solution(16185475004671649462)
XLA Ops:
  0.6 3.0 %collective-permute-start = (bf16[32,32,128]{2,1,0:T(8,128)(2,1)}, bf16[32,32,128]{2,1,0:T(8,128)(2,1)S(1)}, u32[]{:S(2)}, u32[]{:S(2)}) collective-permute-start(bf16[32,32,128]{2,1,0:T(8,128)(2,1)} %refs_2_.3), channel_id=1, source_target_pairs={{0,1},{1,5},{2,3},{3,7},{4,0},{5,4},{6,2},{7,6},{8,9},{9,13},{10,1... | collective-permute-start | bytes 786440 | tf_op jit(solution)/shard_map/ppermute | solution.py:510
  3.6 2.0 %collective-permute-start.3 = (bf16[32,32,128]{2,1,0:T(8,128)(2,1)}, bf16[32,32,128]{2,1,0:T(8,128)(2,1)S(1)}, u32[]{:S(2)}, u32[]{:S(2)}) collective-permute-start(bf16[32,32,128]{2,1,0:T(8,128)(2,1)} %refs_2_.3), channel_id=1, source_target_pairs={{0,4},{2,6},{5,1},{7,3},{8,12},{10,14},{13,9},{15,11},{16,20},{18,... | collective-permute-start | bytes 786440 | tf_op jit(solution)/shard_map/ppermute | solution.py:511
  5.7 4.0 %shard_map.158 = (f32[128,256]{1,0:T(8,128)}, bf16[144,256]{1,0:T(8,128)(2,1)}, f32[1024,128]{1,0:T(8,128)}, bf16[192,128]{1,0:T(8,128)(2,1)}, f32[32,32,128]{2,1,0:T(8,128)}, /*index=5*/bf16[1024,128]{1,0:T(8,128)(2,1)}) custom-call(s32[128]{0:T(128)} %refs_0_.5, bf16[4,32,256]{2,1,0:T(8,128)(2,1)} %refs_1_.2, s32[4,32]{1,0:T(4,128)} %refs_2_.2, ...), custom_call_target="tpu_custom_call" | custom-call | flops 1 | bytes 1 | tf_op jit(solution)/shard_map/pallas_call | solution.py:461
  10.4 0.8 %copy-done.13 = bf16[192,128]{1,0:T(8,128)(2,1)S(1)} copy-done((bf16[192,128]{1,0:T(8,128)(2,1)S(1)}, bf16[192,128]{1,0:T(8,128)(2,1)}, u32[]{:S(2)}) %copy-start.13) | copy-done | bytes 49176
  11.2 0.8 %shard_map.159 = (bf16[1024,128]{1,0:T(8,128)(2,1)S(1)}, bf16[1024,128]{1,0:T(8,128)(2,1)S(1)}, bf16[384,128]{1,0:T(8,128)(2,1)S(1)}) custom-call(bf16[32,32,128]{2,1,0:T(8,128)(2,1)S(1)} %collective-permute-done.refs_0_.refs_2_, bf16[128,640]{1,0:T(8,128)(2,1)S(1)} %copy-done.1, bf16[8,128]{1,0:T(8,128)(2,1)S(1)} %bitcast.5, bf16[192,128]{1,0:T(8,128)(2,1)S(1)} %copy-done.13), custom_call_target="tpu_custom_call" | custom-call | flops 1 | bytes 1 | tf_op jit(solution)/shard_map/pallas_call | solution.py:461
  12.1 1.6 %collective-permute-start.2 = (bf16[1024,128]{1,0:T(8,128)(2,1)S(1)}, bf16[1024,128]{1,0:T(8,128)(2,1)S(1)}, u32[]{:S(2)}, u32[]{:S(2)}) collective-permute-start(bf16[1024,128]{1,0:T(8,128)(2,1)S(1)} %get-tuple-element.18), channel_id=1, source_target_pairs={{0,1},{1,0},{2,3},{3,2},{4,5},{5,4},{6,7},{7,6},{8,9},{9,8},{10,11... | collective-permute-start | bytes 786440 | tf_op jit(solution)/shard_map/ppermute | solution.py:423
  13.7 2.6 %collective-permute-start.6 = (bf16[144,256]{1,0:T(8,128)(2,1)S(1)}, bf16[144,256]{1,0:T(8,128)(2,1)S(1)}, u32[]{:S(2)}, u32[]{:S(2)}) collective-permute-start(bf16[144,256]{1,0:T(8,128)(2,1)S(1)} %copy-done.9), channel_id=1, source_target_pairs={{0,8},{4,12},{8,0},{12,4},{1,9},{5,13},{9,1},{13,5},{2,10},{6,14},... | collective-permute-start | bytes 221192 | tf_op jit(solution)/shard_map/ppermute | solution.py:423
  16.3 1.8 %collective-permute-start.7 = (bf16[144,256]{1,0:T(8,128)(2,1)S(1)}, bf16[144,256]{1,0:T(8,128)(2,1)S(1)}, u32[]{:S(2)}, u32[]{:S(2)}) collective-permute-start(bf16[144,256]{1,0:T(8,128)(2,1)S(1)} %copy-done.9), channel_id=1, source_target_pairs={{0,12},{4,8},{8,4},{12,0},{1,13},{5,9},{9,5},{13,1},{2,14},{6,10},... | collective-permute-start | bytes 221192 | tf_op jit(solution)/shard_map/ppermute | solution.py:423
  18.3 1.1 %shard_map.160.refs_4_ = f32[32,32,128]{2,1,0:T(8,128)S(1)} custom-call(s32[128]{0:T(128)S(1)} %copy-done.15, s32[1,128]{1,0:T(1,128)S(1)} %bitcast.3, bf16[32,32,128]{2,1,0:T(8,128)(2,1)S(1)} %collective-permute-done.refs_0_.refs_2_, bf16[32,32,128]{2,1,0:T(8,128)(2,1)S(1)} %collective-permute-done.3.refs_3_, bf16[128,640]{1,0:T(8,128)(2,1)S(1)} %copy-done.1), custom_call_target="tpu_custom_call" | custom-call | flops 1 | bytes 1 | tf_op jit(solution)/shard_map/pallas_call | solution.py:461
  19.5 1.6 %shard_map.161.refs_5_ = f32[32,32,128]{2,1,0:T(8,128)S(1)} custom-call(bf16[1024,128]{1,0:T(8,128)(2,1)S(1)} %copy-done.3, bf16[1024,128]{1,0:T(8,128)(2,1)S(1)} %get-tuple-element.20.refs_1_.refs_0_, bf16[1024,128]{1,0:T(8,128)(2,1)S(1)} %collective-permute-done.4.refs_2_, bf16[1024,128]{1,0:T(8,128)(2,1)S(1)} %collective-permute-done.5.refs_3_.refs_2_, ...), custom_call_target="tpu_custom_call" | custom-call | flops 1 | bytes 1 | tf_op jit(solution)/shard_map/pallas_call | solution.py:461
  21.1 1.9 %collective-permute-done.7.refs_7_ = bf16[144,256]{1,0:T(8,128)(2,1)S(1)} collective-permute-done((bf16[144,256]{1,0:T(8,128)(2,1)S(1)}, bf16[144,256]{1,0:T(8,128)(2,1)S(1)}, u32[]{:S(2)}, u32[]{:S(2)}) %collective-permute-start.7) | collective-permute-done | bytes 73760 | tf_op jit(solution)/shard_map/ppermute | solution.py:423
  23.0 0.5 %collective-permute-done.8.refs_5_ = bf16[144,256]{1,0:T(8,128)(2,1)S(1)} collective-permute-done((bf16[144,256]{1,0:T(8,128)(2,1)S(1)}, bf16[144,256]{1,0:T(8,128)(2,1)S(1)}, u32[]{:S(2)}, u32[]{:S(2)}) %collective-permute-start.8) | collective-permute-done | bytes 73760 | tf_op jit(solution)/shard_map/ppermute | solution.py:423
  23.5 0.5 %collective-permute-start.1 = (bf16[384,128]{1,0:T(8,128)(2,1)S(1)}, bf16[384,128]{1,0:T(8,128)(2,1)S(1)}, u32[]{:S(2)}, u32[]{:S(2)}) collective-permute-start(bf16[384,128]{1,0:T(8,128)(2,1)S(1)} %get-tuple-element.17.refs_0_), channel_id=1, source_target_pairs={{0,2},{2,0},{1,3},{3,1},{4,6},{6,4},{5,7},{7,5},{8,10},{10,8},{9,1... | collective-permute-start | bytes 294920 | tf_op jit(solution)/shard_map/ppermute | solution.py:423
  24.0 1.0 %collective-permute-done.9.refs_3_ = bf16[1024,128]{1,0:T(8,128)(2,1)S(1)} collective-permute-done((bf16[1024,128]{1,0:T(8,128)(2,1)S(1)}, bf16[1024,128]{1,0:T(8,128)(2,1)S(1)}, u32[]{:S(2)}, u32[]{:S(2)}) %collective-permute-start.9) | collective-permute-done | bytes 262176 | tf_op jit(solution)/shard_map/ppermute | solution.py:423
  25.0 1.5 %shard_map.162.refs_12_ = bf16[32,32,128]{2,1,0:T(8,128)(2,1)S(1)} custom-call(bf16[1024,128]{1,0:T(8,128)(2,1)S(1)} %get-tuple-element.20.refs_1_.refs_0_, bf16[1024,128]{1,0:T(8,128)(2,1)S(1)} %collective-permute-done.2.refs_1_.refs_2_, bf16[1024,128]{1,0:T(8,128)(2,1)S(1)} %collective-permute-done.5.refs_3_.refs_2_, ...), custom_call_target="tpu_custom_call" | custom-call | flops 1 | bytes 1 | tf_op jit(solution)/shard_map/pallas_call | solution.py:461
  26.5 2.8 %collective-permute-start.12 = (bf16[32,32,128]{2,1,0:T(8,128)(2,1)S(1)}, bf16[32,32,128]{2,1,0:T(8,128)(2,1)S(1)}, u32[]{:S(2)}, u32[]{:S(2)}) collective-permute-start(bf16[32,32,128]{2,1,0:T(8,128)(2,1)S(1)} %shard_map.162.refs_12_), channel_id=1, source_target_pairs={{0,8},{4,12},{8,0},{12,4},{1,9},{5,13},{9,1},{13,5},{2,10},{6,14},... | collective-permute-start | bytes 786440 | tf_op jit(solution)/shard_map/ppermute | solution.py:423
  29.3 1.6 %shard_map.163 = (f32[128,256]{1,0:T(8,128)S(1)}, bf16[144,256]{1,0:T(8,128)(2,1)S(1)}) custom-call(bf16[384,128]{1,0:T(8,128)(2,1)S(1)} %get-tuple-element.17.refs_0_, bf16[384,128]{1,0:T(8,128)(2,1)S(1)} %collective-permute-done.1.refs_1_, bf16[1024,128]{1,0:T(8,128)(2,1)S(1)} %collective-permute-done.2.refs_1_.refs_2_, ...), custom_call_target="tpu_custom_call" | custom-call | flops 1 | bytes 1 | tf_op jit(solution)/shard_map/pallas_call | solution.py:461
  30.9 0.9 %collective-permute-start.10 = (bf16[144,256]{1,0:T(8,128)(2,1)S(1)}, bf16[144,256]{1,0:T(8,128)(2,1)S(1)}, u32[]{:S(2)}, u32[]{:S(2)}) collective-permute-start(bf16[144,256]{1,0:T(8,128)(2,1)S(1)} %get-tuple-element.26.refs_0_.refs_2_), channel_id=1, source_target_pairs={{0,1},{1,0},{2,3},{3,2},{4,5},{5,4},{6,7},{7,6},{8,9},{9,8},{10,11... | collective-permute-start | bytes 221192 | tf_op jit(solution)/shard_map/ppermute | solution.py:423
  31.8 1.5 %shard_map.164.refs_2_.refs_5_ = f32[32,32,128]{2,1,0:T(8,128)S(1)} custom-call(bf16[1024,128]{1,0:T(8,128)(2,1)S(1)} %copy-done.3, bf16[1024,128]{1,0:T(8,128)(2,1)S(1)} %get-tuple-element.20.refs_1_.refs_0_, bf16[1024,128]{1,0:T(8,128)(2,1)S(1)} %collective-permute-done.4.refs_2_, bf16[1024,128]{1,0:T(8,128)(2,1)S(1)} %collective-permute-done.5.refs_3_.refs_2_, ...), custom_call_target="tpu_custom_call" | custom-call | flops 1 | bytes 1 | tf_op jit(solution)/shard_map/pallas_call | solution.py:461
  33.4 1.9 %collective-permute-done.10.refs_1_ = bf16[144,256]{1,0:T(8,128)(2,1)S(1)} collective-permute-done((bf16[144,256]{1,0:T(8,128)(2,1)S(1)}, bf16[144,256]{1,0:T(8,128)(2,1)S(1)}, u32[]{:S(2)}, u32[]{:S(2)}) %collective-permute-start.10) | collective-permute-done | bytes 73760 | tf_op jit(solution)/shard_map/ppermute | solution.py:423
  35.4 1.6 %shard_map.166.refs_8_.refs_1_ = f32[32,32,128]{2,1,0:T(8,128)S(1)} custom-call(bf16[1024,128]{1,0:T(8,128)(2,1)S(1)} %get-tuple-element.20.refs_1_.refs_0_, bf16[1024,128]{1,0:T(8,128)(2,1)S(1)} %collective-permute-done.2.refs_1_.refs_2_, bf16[1024,128]{1,0:T(8,128)(2,1)S(1)} %collective-permute-done.5.refs_3_.refs_2_, ...), custom_call_target="tpu_custom_call" | custom-call | flops 1 | bytes 1 | tf_op jit(solution)/shard_map/pallas_call | solution.py:461
  37.1 3.3 %shard_map.167 = bf16[4,32,256]{2,1,0:T(8,128)(2,1)} custom-call(bf16[2,144,256]{2,1,0:T(8,128)(2,1)S(1)} %shard_map.165.refs_0_, bf16[2,144,256]{2,1,0:T(8,128)(2,1)S(1)} %collective-permute-done.11.refs_1_, bf16[144,256]{1,0:T(8,128)(2,1)S(1)} %get-tuple-element.26.refs_0_.refs_2_, f32[128,256]{1,0:T(8,128)S(1)} %get-tuple-element.28.refs_3_, ...), custom_call_target="tpu_custom_call" | custom-call | flops 1 | bytes 1 | tf_op jit(solution)/shard_map/pallas_call | solution.py:461
  40.4 1.1 %collective-permute-done.12.refs_5_ = bf16[32,32,128]{2,1,0:T(8,128)(2,1)S(1)} collective-permute-done((bf16[32,32,128]{2,1,0:T(8,128)(2,1)S(1)}, bf16[32,32,128]{2,1,0:T(8,128)(2,1)S(1)}, u32[]{:S(2)}, u32[]{:S(2)}) %collective-permute-start.12) | collective-permute-done | bytes 262176 | tf_op jit(solution)/shard_map/ppermute | solution.py:423
  41.5 1.7 %shard_map.168 = bf16[32,32,128]{2,1,0:T(8,128)(2,1)} custom-call(s32[128]{0:T(128)S(1)} %copy-done.15, f32[32,32,128]{2,1,0:T(8,128)S(1)} %shard_map.166.refs_8_.refs_1_, bf16[32,32,128]{2,1,0:T(8,128)(2,1)S(1)} %copy-done.2, f32[1024,128]{1,0:T(8,128)S(1)} %copy-done.8, bf16[128,128]{1,0:T(8,128)(2,1)S(1)} %copy-done.14, ...), custom_call_target="tpu_custom_call" | custom-call | flops 1 | bytes 1 | tf_op jit(solution)/shard_map/pallas_call | solution.py:461
  (47 shorter events, 1.2 us)
Async XLA Ops:
  0.6 9.6 %collective-permute-start = (bf16[32,32,128]{2,1,0:T(8,128)(2,1)}, bf16[32,32,128]{2,1,0:T(8,128)(2,1)S(1)}, u32[]{:S(2)}, u32[]{:S(2)}) collective-permute-start(bf16[32,32,128]{2,1,0:T(8,128)(2,1)} %refs_2_.3), channel_id=1, source_target_pairs={{0,1},{1,5},{2,3},{3,7},{4,0},{5,4},{6,2},{7,6},{8,9},{9,13},{10,1... | collective-permute-start | bytes 786440 | tf_op jit(solution)/shard_map/ppermute | solution.py:510
  3.6 12.6 %collective-permute-start.3 = (bf16[32,32,128]{2,1,0:T(8,128)(2,1)}, bf16[32,32,128]{2,1,0:T(8,128)(2,1)S(1)}, u32[]{:S(2)}, u32[]{:S(2)}) collective-permute-start(bf16[32,32,128]{2,1,0:T(8,128)(2,1)} %refs_2_.3), channel_id=1, source_target_pairs={{0,4},{2,6},{5,1},{7,3},{8,12},{10,14},{13,9},{15,11},{16,20},{18,... | collective-permute-start | bytes 786440 | tf_op jit(solution)/shard_map/ppermute | solution.py:511
  5.7 4.6 %copy-start.1 = (bf16[128,640]{1,0:T(8,128)(2,1)S(1)}, bf16[128,640]{1,0:T(8,128)(2,1)}, u32[]{:S(2)}) copy-start(bf16[128,640]{1,0:T(8,128)(2,1)} %refs_4_.5) | copy-start | bytes 491524
  9.7 8.3 %collective-permute-start.4 = (bf16[1024,128]{1,0:T(8,128)(2,1)}, bf16[1024,128]{1,0:T(8,128)(2,1)S(1)}, u32[]{:S(2)}, u32[]{:S(2)}) collective-permute-start(bf16[1024,128]{1,0:T(8,128)(2,1)} %get-tuple-element.19.refs_0_), channel_id=1, source_target_pairs={{0,2},{2,0},{1,3},{3,1},{4,6},{6,4},{5,7},{7,5},{8,10},{10,8},{9,1... | collective-permute-start | bytes 786440 | tf_op jit(solution)/shard_map/ppermute | solution.py:423
  11.2 2.5 %copy-start.9 = (bf16[144,256]{1,0:T(8,128)(2,1)S(1)}, bf16[144,256]{1,0:T(8,128)(2,1)}, u32[]{:S(2)}) copy-start(bf16[144,256]{1,0:T(8,128)(2,1)} %get-tuple-element.23.refs_4_.refs_8_) | copy-start | bytes 221188
  12.0 7.5 %collective-permute-start.5 = (bf16[1024,128]{1,0:T(8,128)(2,1)S(1)}, bf16[1024,128]{1,0:T(8,128)(2,1)S(1)}, u32[]{:S(2)}, u32[]{:S(2)}) collective-permute-start(bf16[1024,128]{1,0:T(8,128)(2,1)S(1)} %get-tuple-element.20.refs_1_.refs_0_), channel_id=1, source_target_pairs={{0,2},{2,0},{1,3},{3,1},{4,6},{6,4},{5,7},{7,5},{8,10},{10,8},{9,1... | collective-permute-start | bytes 786440 | tf_op jit(solution)/shard_map/ppermute | solution.py:423
  12.1 6.2 %copy-start.15 = (s32[128]{0:T(128)S(1)}, s32[128]{0:T(128)}, u32[]{:S(2)}) copy-start(s32[128]{0:T(128)} %refs_0_.5) | copy-start | bytes 1540
  12.1 11.4 %collective-permute-start.2 = (bf16[1024,128]{1,0:T(8,128)(2,1)S(1)}, bf16[1024,128]{1,0:T(8,128)(2,1)S(1)}, u32[]{:S(2)}, u32[]{:S(2)}) collective-permute-start(bf16[1024,128]{1,0:T(8,128)(2,1)S(1)} %get-tuple-element.18), channel_id=1, source_target_pairs={{0,1},{1,0},{2,3},{3,2},{4,5},{5,4},{6,7},{7,6},{8,9},{9,8},{10,11... | collective-permute-start | bytes 786440 | tf_op jit(solution)/shard_map/ppermute | solution.py:423
  13.7 5.8 %copy-start = (f32[32,32,128]{2,1,0:T(8,128)S(1)}, f32[32,32,128]{2,1,0:T(8,128)}, u32[]{:S(2)}) copy-start(f32[32,32,128]{2,1,0:T(8,128)} %get-tuple-element.27.refs_4_) | copy-start | bytes 1572868
  13.7 5.8 %copy-start.3 = (bf16[1024,128]{1,0:T(8,128)(2,1)S(1)}, bf16[1024,128]{1,0:T(8,128)(2,1)}, u32[]{:S(2)}) copy-start(bf16[1024,128]{1,0:T(8,128)(2,1)} %get-tuple-element.19.refs_0_) | copy-start | bytes 786436
  13.7 7.4 %collective-permute-start.6 = (bf16[144,256]{1,0:T(8,128)(2,1)S(1)}, bf16[144,256]{1,0:T(8,128)(2,1)S(1)}, u32[]{:S(2)}, u32[]{:S(2)}) collective-permute-start(bf16[144,256]{1,0:T(8,128)(2,1)S(1)} %copy-done.9), channel_id=1, source_target_pairs={{0,8},{4,12},{8,0},{12,4},{1,9},{5,13},{9,1},{13,5},{2,10},{6,14},... | collective-permute-start | bytes 221192 | tf_op jit(solution)/shard_map/ppermute | solution.py:423
  16.3 6.7 %collective-permute-start.7 = (bf16[144,256]{1,0:T(8,128)(2,1)S(1)}, bf16[144,256]{1,0:T(8,128)(2,1)S(1)}, u32[]{:S(2)}, u32[]{:S(2)}) collective-permute-start(bf16[144,256]{1,0:T(8,128)(2,1)S(1)} %copy-done.9), channel_id=1, source_target_pairs={{0,12},{4,8},{8,4},{12,0},{1,13},{5,9},{9,5},{13,1},{2,14},{6,10},... | collective-permute-start | bytes 221192 | tf_op jit(solution)/shard_map/ppermute | solution.py:423
  18.0 5.5 %collective-permute-start.8 = (bf16[144,256]{1,0:T(8,128)(2,1)S(1)}, bf16[144,256]{1,0:T(8,128)(2,1)S(1)}, u32[]{:S(2)}, u32[]{:S(2)}) collective-permute-start(bf16[144,256]{1,0:T(8,128)(2,1)S(1)} %copy-done.9), channel_id=1, source_target_pairs={{0,4},{4,0},{8,12},{12,8},{1,5},{5,1},{9,13},{13,9},{2,6},{6,2},{1... | collective-permute-start | bytes 221192 | tf_op jit(solution)/shard_map/ppermute | solution.py:423
  23.5 1.5 %collective-permute-start.9 = (bf16[1024,128]{1,0:T(8,128)(2,1)S(1)}, bf16[1024,128]{1,0:T(8,128)(2,1)S(1)}, u32[]{:S(2)}, u32[]{:S(2)}) collective-permute-start(bf16[1024,128]{1,0:T(8,128)(2,1)S(1)} %collective-permute-done.2.refs_1_.refs_2_), channel_id=1, source_target_pairs={{0,2},{2,0},{1,3},{3,1},{4,6},{6,4},{5,7},{7,5},{8,10},{10,8},{9,1... | collective-permute-start | bytes 786440 | tf_op jit(solution)/shard_map/ppermute | solution.py:423
  23.5 5.8 %copy-start.4 = (bf16[256,1024]{1,0:T(8,128)(2,1)S(1)}, bf16[256,1024]{1,0:T(8,128)(2,1)}, u32[]{:S(2)}) copy-start(bf16[256,1024]{1,0:T(8,128)(2,1)} %refs_10_.1) | copy-start | bytes 1572868
  23.5 5.8 %copy-start.10 = (bf16[256,256]{1,0:T(8,128)(2,1)S(1)}, bf16[256,256]{1,0:T(8,128)(2,1)}, u32[]{:S(2)}) copy-start(bf16[256,256]{1,0:T(8,128)(2,1)} %refs_11_.1) | copy-start | bytes 393220
  23.5 5.8 %copy-start.12 = (f32[128,256]{1,0:T(8,128)S(1)}, f32[128,256]{1,0:T(8,128)}, u32[]{:S(2)}) copy-start(f32[128,256]{1,0:T(8,128)} %get-tuple-element.25.refs_9_) | copy-start | bytes 393220
  23.5 5.8 %collective-permute-start.1 = (bf16[384,128]{1,0:T(8,128)(2,1)S(1)}, bf16[384,128]{1,0:T(8,128)(2,1)S(1)}, u32[]{:S(2)}, u32[]{:S(2)}) collective-permute-start(bf16[384,128]{1,0:T(8,128)(2,1)S(1)} %get-tuple-element.17.refs_0_), channel_id=1, source_target_pairs={{0,2},{2,0},{1,3},{3,1},{4,6},{6,4},{5,7},{7,5},{8,10},{10,8},{9,1... | collective-permute-start | bytes 294920 | tf_op jit(solution)/shard_map/ppermute | solution.py:423
  26.5 15.0 %collective-permute-start.12 = (bf16[32,32,128]{2,1,0:T(8,128)(2,1)S(1)}, bf16[32,32,128]{2,1,0:T(8,128)(2,1)S(1)}, u32[]{:S(2)}, u32[]{:S(2)}) collective-permute-start(bf16[32,32,128]{2,1,0:T(8,128)(2,1)S(1)} %shard_map.162.refs_12_), channel_id=1, source_target_pairs={{0,8},{4,12},{8,0},{12,4},{1,9},{5,13},{9,1},{13,5},{2,10},{6,14},... | collective-permute-start | bytes 786440 | tf_op jit(solution)/shard_map/ppermute | solution.py:423
  30.9 4.4 %collective-permute-start.10 = (bf16[144,256]{1,0:T(8,128)(2,1)S(1)}, bf16[144,256]{1,0:T(8,128)(2,1)S(1)}, u32[]{:S(2)}, u32[]{:S(2)}) collective-permute-start(bf16[144,256]{1,0:T(8,128)(2,1)S(1)} %get-tuple-element.26.refs_0_.refs_2_), channel_id=1, source_target_pairs={{0,1},{1,0},{2,3},{3,2},{4,5},{5,4},{6,7},{7,6},{8,9},{9,8},{10,11... | collective-permute-start | bytes 221192 | tf_op jit(solution)/shard_map/ppermute | solution.py:423
  35.3 1.7 %collective-permute-start.11 = (bf16[2,144,256]{2,1,0:T(8,128)(2,1)S(1)}, bf16[2,144,256]{2,1,0:T(8,128)(2,1)S(1)}, u32[]{:S(2)}, u32[]{:S(2)}) collective-permute-start(bf16[2,144,256]{2,1,0:T(8,128)(2,1)S(1)} %shard_map.165.refs_0_), channel_id=1, source_target_pairs={{0,2},{2,0},{1,3},{3,1},{4,6},{6,4},{5,7},{7,5},{8,10},{10,8},{9,1... | collective-permute-start | bytes 442376 | tf_op jit(solution)/shard_map/ppermute | solution.py:423
  37.0 4.5 %copy-start.2 = (bf16[32,32,128]{2,1,0:T(8,128)(2,1)S(1)}, bf16[32,32,128]{2,1,0:T(8,128)(2,1)}, u32[]{:S(2)}) copy-start(bf16[32,32,128]{2,1,0:T(8,128)(2,1)} %refs_2_.3) | copy-start | bytes 786436
  37.1 4.5 %copy-start.8 = (f32[1024,128]{1,0:T(8,128)S(1)}, f32[1024,128]{1,0:T(8,128)}, u32[]{:S(2)}) copy-start(f32[1024,128]{1,0:T(8,128)} %get-tuple-element.29.refs_3_) | copy-start | bytes 1572868
  37.1 4.5 %copy-start.14 = (bf16[128,128]{1,0:T(8,128)(2,1)S(1)}, bf16[128,128]{1,0:T(8,128)(2,1)}, u32[]{:S(2)}) copy-start(bf16[128,128]{1,0:T(8,128)(2,1)} %refs_4_.7) | copy-start | bytes 98308
  (6 other events, 8.3 us)

commit v4 on v3

--- a/solution.py
+++ b/solution.py
@@ -214,28 +214,35 @@
             out[base : base + heads, :] = term[:, part * lanes : (part + 1) * lanes]
 
 
-def start_kernel(count, present, *refs):
-    sources, outputs, rest = refs[:count], refs[count : count + 6], refs[count + 6 :]
+def first_kernel(count, *refs):
+    sources, outputs, rest = refs[:count], refs[count : count + 3], refs[count + 3 :]
     buffers, semaphores, tail = rest[:count], rest[count], rest[count + 1]
     fetch(sources, buffers, semaphores)
-    embedded, payload, gate, terms, near, left = outputs
+    embedded, payload, terms = outputs
     embed_kernel(*buffers[:4], embedded, payload, tail)
-    present_row, pairs, entry, logits = buffers[4:]
+    pairs, logits = buffers[4:]
     lines, positions, width = pairs.shape
-    heads = logits.shape[0]
     normed = normalize(pairs[...].astype(f32).reshape(lines * positions, width)).astype(bf16)
     logit = lax.dot_general(logits[...], normed, NT, preferred_element_type=f32)
     store_terms(logit, terms, 0)
+
+
+def pair_kernel(present, present_row, pairs, entry, gate, near, left):
+    lines, positions, width = pairs.shape
+    normed = normalize(pairs[...].astype(f32).reshape(lines * positions, width)).astype(bf16)
     projected = dot(normed, entry[...])
     gate[...] = sigmoid(projected[:, 4 * width :])
     left[...] = (sigmoid(projected[:, width : 2 * width]) * projected[:, :width]).astype(bf16)
     operand = sigmoid(projected[:, 3 * width : 4 * width]) * projected[:, 2 * width : 3 * width]
-    operand = operand.astype(bf16)
-    mask_right(lax.axis_index("res"), operand, present, present_row, near)
+    mask_right(lax.axis_index("res"), operand.astype(bf16), present, present_row, near)
 
 
 def on_turn():
     return lax.axis_index("res") % 2 == lax.axis_index("aux")
+
+
+def hold_kernel(terms, present_row, out):
+    out[...] = terms[...]
 
 
 def turn_kernel(pairs, entry, logits, terms, came, given, both):
@@ -549,46 +556,45 @@
         symbol_ids,
         entry_present,
         symbol_lookup_matrix,
-        amino_present[None, :],
         couple_features,
-        trimul_entry_matrix,
         couple_logit_matrix.T,
     )
-    embedded, payload, gate, terms, near, left = call(
-        functools.partial(start_kernel, len(args)),
+    embedded, payload, terms = call(
+        functools.partial(first_kernel, len(args)),
         (
             shape((rows, depth), f32),
             shape((rows + tail, depth), bf16),
-            shape((area, width), f32),
             shape((3 * held, width), bf16),
-            shape(couple_features.shape, f32),
-            shape((area, width), bf16),
         ),
         [pltpu.VMEM(x.shape, x.dtype) for x in args]
         + [pltpu.SemaphoreType.DMA((len(args),)), pltpu.VMEM((tail, depth), f32)],
-        smem=1,
         hbm=True,
-    )(amino_present, *args)
+    )(*args)
+    flat = shape((area, width), bf16)
+    of_pairs = lambda pairs: call(
+        pair_kernel, (shape((area, width), f32), shape(pairs.shape, f32), flat), smem=1
+    )(*presence, pairs, trimul_entry_matrix)
     pending = ()
     if halves:
         row_blocks, row_relative = gather(payload, "res")
         turned, crossed = turn_pairs(couple_features)
-        flat = shape((area, width), bf16)
+        terms = call(hold_kernel, shape(terms.shape, bf16))(terms, presence[1])
         came, given, terms = call(turn_kernel, (flat, flat, shape((6 * held, width), bf16)))(
             turned, trimul_entry_matrix, couple_logit_matrix.T, terms
         )
         passed = flip(given, "aux")
+        gate, near, left = of_pairs(lax.optimization_barrier((couple_features, came))[0])
         other_left, other_came = flip(left, "br"), flip(came, "br")
         cube = shape(couple_features.shape, f32)
         scratch = [pltpu.VMEM(couple_features.shape, f32)]
         far = call(far_kernel, cube, smem=1)(*presence, turned, crossed, trimul_entry_matrix)
-        nearest = lax.optimization_barrier((near, far))[0]
+        ready = lax.optimization_barrier((passed, far, row_blocks[2], row_blocks[3], row_blocks[1]))[0]
+        other_passed = flip(ready, "br")
+        nearest = lax.optimization_barrier((near, passed, far))[0]
         early = lambda other_half, right: call(
             functools.partial(early_kernel, other_half), cube, scratch
         )(left, came, other_left, other_came, right)
         sent = early(True, nearest)
-        ready = lax.optimization_barrier((passed, far, sent, row_blocks[2], row_blocks[3], row_blocks[1]))[0]
-        other_passed = flip(ready, "br")
         operands = (came, passed, other_came, other_passed, far)
         terms, side_relative = (terms, flip(terms, "br"), passed, other_passed), True
         places = [(0, 0, None), (0, 3 * held, 2), (1, 0, None), (1, 3 * held, 3)]
@@ -603,6 +609,7 @@
         pending = (sent,)
     else:
         row_blocks, row_relative = gather(payload, "res")
+        gate = of_pairs(couple_features)[0]
         terms, side_relative = gather_side(terms)
         places = [(index, 0, None) for index in range(side)]
 

time: 43.5 us -> 42.4 us (0.975)
  waiting for transfers between devices: 6.92 us -> 6.13 us
  starting transfers between devices: 15.7 us -> 15.2 us
  local copies, waits for them, and re-layouts: 1.04 us -> 1.52 us
    ppermute x11, waiting for transfers between devices: 6.48 us -> 5.38 us  [flip(): lax.ppermute(block, axis, [(i, i ^ bit) for i in range(lax.axis_size(axis...]
    ppermute x11, starting transfers between devices: 10.7 us -> 10.2 us  [flip(): lax.ppermute(block, axis, [(i, i ^ bit) for i in range(lax.axis_size(axis...]
    unnamed x34 -> x28, local copies, waits for them, and re-layouts: 1.04 us -> 1.52 us
    pallas_call x11 -> x13, Pallas kernels: 18.7 us -> 18.5 us  [run(): pl.pallas_call(ordered, out_shape=out_shape, in_specs=[pl.BlockSpec(memor...]
  transfers between devices with their start and end apart: 13 -> 13, of which waited for: 6 -> 5; matrix products, arithmetic and copies ran while one was open for 0% -> 0% of each run, Pallas kernels for 39% -> 40%
where the time goes in v4:
time: 42.4 us; the launch traced here: 42.2 us
  Pallas kernels  18.5 us (44%)
  starting transfers between devices  15.2 us (36%)
  waiting for transfers between devices  6.13 us (14%)
  local copies, waits for them, and re-layouts  1.52 us (4%)
  between operations  0.87 us (2%)
    pallas_call x13, Pallas kernels, run(): pl.pallas_call(ordered, out_shape=out_shape, in_specs=[pl.BlockSpec(memor...  18.5 us
    ppermute x11, starting transfers between devices, flip(): lax.ppermute(block, axis, [(i, i ^ bit) for i in range(lax.axis_size(axis...  10.2 us
    ppermute x11, waiting for transfers between devices, flip(): lax.ppermute(block, axis, [(i, i ^ bit) for i in range(lax.axis_size(axis...  5.38 us
    ppermute x1, starting transfers between devices, turn_pairs(): lax.ppermute(pairs, ALL, [(index(*place), goes(*place)) for place in every])  2.99 us
    ppermute x1, starting transfers between devices, turn_pairs(): lax.ppermute(pairs, ALL, [(index(h, l, br, a), index(h, 1 - l, br, a)) fo...  2.02 us
    unnamed x28, local copies, waits for them, and re-layouts  1.52 us
  transfers between devices with their start and end apart: 13, of which 5 were waited for; matrix products, arithmetic and copies ran while one was open for 0% of the time, Pallas kernels for 40%

profile of v4, /device:TPU:0, one launch (start us, length us, event | category | flops | bytes accessed | tf_op | source)
XLA Modules:
  0.0 42.2 jit_solution(12398214047270002201)
XLA Ops:
  0.6 3.0 %collective-permute-start = (bf16[32,32,128]{2,1,0:T(8,128)(2,1)}, bf16[32,32,128]{2,1,0:T(8,128)(2,1)S(1)}, u32[]{:S(2)}, u32[]{:S(2)}) collective-permute-start(bf16[32,32,128]{2,1,0:T(8,128)(2,1)} %refs_2_.4), channel_id=1, source_target_pairs={{0,1},{1,5},{2,3},{3,7},{4,0},{5,4},{6,2},{7,6},{8,9},{9,13},{10,1... | collective-permute-start | bytes 786440 | tf_op jit(solution)/shard_map/ppermute | solution.py:517
  3.6 2.0 %collective-permute-start.3 = (bf16[32,32,128]{2,1,0:T(8,128)(2,1)}, bf16[32,32,128]{2,1,0:T(8,128)(2,1)S(1)}, u32[]{:S(2)}, u32[]{:S(2)}) collective-permute-start(bf16[32,32,128]{2,1,0:T(8,128)(2,1)} %refs_2_.4), channel_id=1, source_target_pairs={{0,4},{2,6},{5,1},{7,3},{8,12},{10,14},{13,9},{15,11},{16,20},{18,... | collective-permute-start | bytes 786440 | tf_op jit(solution)/shard_map/ppermute | solution.py:518
  5.7 2.3 %shard_map.158 = (f32[128,256]{1,0:T(8,128)}, bf16[144,256]{1,0:T(8,128)(2,1)}, bf16[192,128]{1,0:T(8,128)(2,1)}) custom-call(bf16[4,32,256]{2,1,0:T(8,128)(2,1)} %refs_0_.4, s32[4,32]{1,0:T(4,128)} %refs_1_.2, s32[4,32]{1,0:T(4,128)} %refs_2_.2, bf16[23,256]{1,0:T(8,128)(2,1)} %refs_3_.2, bf16[32,32,128]{2,1,0:T(8,128)(2,1)} %refs_2_.4, bf16[8,128]{1,0:T(8,128)(2,1)} %bitcast.5), custom_call_target="tpu_custom_call" | custom-call | flops 1 | bytes 1 | tf_op jit(solution)/shard_map/pallas_call | solution.py:468
  8.0 0.6 %copy-done.12 = s32[128]{0:T(128)S(1)} copy-done((s32[128]{0:T(128)S(1)}, s32[128]{0:T(128)}, u32[]{:S(2)}) %copy-start.12) | copy-done | bytes 536
  8.7 0.8 %copy-done.10 = bf16[192,128]{1,0:T(8,128)(2,1)S(1)} copy-done((bf16[192,128]{1,0:T(8,128)(2,1)S(1)}, bf16[192,128]{1,0:T(8,128)(2,1)}, u32[]{:S(2)}) %copy-start.10) | copy-done | bytes 49176
  9.5 0.7 %collective-permute-done.refs_0_.refs_2_ = bf16[32,32,128]{2,1,0:T(8,128)(2,1)S(1)} collective-permute-done((bf16[32,32,128]{2,1,0:T(8,128)(2,1)}, bf16[32,32,128]{2,1,0:T(8,128)(2,1)S(1)}, u32[]{:S(2)}, u32[]{:S(2)}) %collective-permute-start) | collective-permute-done | bytes 262176 | tf_op jit(solution)/shard_map/ppermute | solution.py:517
  10.2 0.8 %shard_map.160 = (bf16[1024,128]{1,0:T(8,128)(2,1)S(1)}, bf16[1024,128]{1,0:T(8,128)(2,1)S(1)}, bf16[384,128]{1,0:T(8,128)(2,1)S(1)}) custom-call(bf16[32,32,128]{2,1,0:T(8,128)(2,1)S(1)} %collective-permute-done.refs_0_.refs_2_, bf16[128,640]{1,0:T(8,128)(2,1)S(1)} %copy-done.1, bf16[8,128]{1,0:T(8,128)(2,1)S(1)} %bitcast.6, ...), custom_call_target="tpu_custom_call" | custom-call | flops 1 | bytes 1 | tf_op jit(solution)/shard_map/pallas_call | solution.py:468
  11.0 1.7 %collective-permute-start.2 = (bf16[1024,128]{1,0:T(8,128)(2,1)S(1)}, bf16[1024,128]{1,0:T(8,128)(2,1)S(1)}, u32[]{:S(2)}, u32[]{:S(2)}) collective-permute-start(bf16[1024,128]{1,0:T(8,128)(2,1)S(1)} %get-tuple-element.19), channel_id=1, source_target_pairs={{0,1},{1,0},{2,3},{3,2},{4,5},{5,4},{6,7},{7,6},{8,9},{9,8},{10,11... | collective-permute-start | bytes 786440 | tf_op jit(solution)/shard_map/ppermute | solution.py:430
  12.8 2.6 %collective-permute-start.4 = (bf16[144,256]{1,0:T(8,128)(2,1)S(1)}, bf16[144,256]{1,0:T(8,128)(2,1)S(1)}, u32[]{:S(2)}, u32[]{:S(2)}) collective-permute-start(bf16[144,256]{1,0:T(8,128)(2,1)S(1)} %copy-done.6), channel_id=1, source_target_pairs={{0,8},{4,12},{8,0},{12,4},{1,9},{5,13},{9,1},{13,5},{2,10},{6,14},... | collective-permute-start | bytes 221192 | tf_op jit(solution)/shard_map/ppermute | solution.py:430
  15.4 1.5 %collective-permute-start.5 = (bf16[144,256]{1,0:T(8,128)(2,1)S(1)}, bf16[144,256]{1,0:T(8,128)(2,1)S(1)}, u32[]{:S(2)}, u32[]{:S(2)}) collective-permute-start(bf16[144,256]{1,0:T(8,128)(2,1)S(1)} %copy-done.6), channel_id=1, source_target_pairs={{0,12},{4,8},{8,4},{12,0},{1,13},{5,9},{9,5},{13,1},{2,14},{6,10},... | collective-permute-start | bytes 221192 | tf_op jit(solution)/shard_map/ppermute | solution.py:430
  17.1 1.5 %shard_map.162 = (f32[1024,128]{1,0:T(8,128)S(1)}, f32[32,32,128]{2,1,0:T(8,128)S(1)}, bf16[1024,128]{1,0:T(8,128)(2,1)S(1)}) custom-call(s32[128]{0:T(128)S(1)} %copy-done.12, s32[1,128]{1,0:T(1,128)S(1)} %bitcast.3, bf16[32,32,128]{2,1,0:T(8,128)(2,1)S(1)} %copy-done, bf16[128,640]{1,0:T(8,128)(2,1)S(1)} %copy-done.1), custom_call_target="tpu_custom_call" | custom-call | flops 1 | bytes 1 | tf_op jit(solution)/shard_map/pallas_call | solution.py:468
  18.7 1.1 %shard_map.161.refs_4_ = f32[32,32,128]{2,1,0:T(8,128)S(1)} custom-call(s32[128]{0:T(128)S(1)} %copy-done.12, s32[1,128]{1,0:T(1,128)S(1)} %bitcast.4, bf16[32,32,128]{2,1,0:T(8,128)(2,1)S(1)} %collective-permute-done.refs_0_.refs_2_, bf16[32,32,128]{2,1,0:T(8,128)(2,1)S(1)} %collective-permute-done.3.refs_3_, bf16[128,640]{1,0:T(8,128)(2,1)S(1)} %copy-done.1), custom_call_target="tpu_custom_call" | custom-call | flops 1 | bytes 1 | tf_op jit(solution)/shard_map/pallas_call | solution.py:468
  20.4 1.3 %collective-permute-done.5.refs_7_ = bf16[144,256]{1,0:T(8,128)(2,1)S(1)} collective-permute-done((bf16[144,256]{1,0:T(8,128)(2,1)S(1)}, bf16[144,256]{1,0:T(8,128)(2,1)S(1)}, u32[]{:S(2)}, u32[]{:S(2)}) %collective-permute-start.5) | collective-permute-done | bytes 73760 | tf_op jit(solution)/shard_map/ppermute | solution.py:430
  22.5 1.5 %shard_map.163.refs_5_ = f32[32,32,128]{2,1,0:T(8,128)S(1)} custom-call(bf16[1024,128]{1,0:T(8,128)(2,1)S(1)} %get-tuple-element.25.refs_0_, bf16[1024,128]{1,0:T(8,128)(2,1)S(1)} %get-tuple-element.23.refs_1_.refs_0_, bf16[1024,128]{1,0:T(8,128)(2,1)S(1)} %collective-permute-done.9.refs_2_, bf16[1024,128]{1,0:T(8,128)(2,1)S(1)} %collective-permute-done.8.refs_3_.refs_2_, ...), custom_call_target="tpu_custom_call" | custom-call | flops 1 | bytes 1 | tf_op jit(solution)/shard_map/pallas_call | solution.py:468
  24.1 1.5 %shard_map.164.refs_12_ = bf16[32,32,128]{2,1,0:T(8,128)(2,1)S(1)} custom-call(bf16[1024,128]{1,0:T(8,128)(2,1)S(1)} %get-tuple-element.23.refs_1_.refs_0_, bf16[1024,128]{1,0:T(8,128)(2,1)S(1)} %collective-permute-done.2.refs_1_.refs_2_, bf16[1024,128]{1,0:T(8,128)(2,1)S(1)} %collective-permute-done.8.refs_3_.refs_2_, ...), custom_call_target="tpu_custom_call" | custom-call | flops 1 | bytes 1 | tf_op jit(solution)/shard_map/pallas_call | solution.py:468
  25.6 1.9 %collective-permute-start.12 = (bf16[32,32,128]{2,1,0:T(8,128)(2,1)S(1)}, bf16[32,32,128]{2,1,0:T(8,128)(2,1)S(1)}, u32[]{:S(2)}, u32[]{:S(2)}) collective-permute-start(bf16[32,32,128]{2,1,0:T(8,128)(2,1)S(1)} %shard_map.164.refs_12_), channel_id=1, source_target_pairs={{0,8},{4,12},{8,0},{12,4},{1,9},{5,13},{9,1},{13,5},{2,10},{6,14},... | collective-permute-start | bytes 786440 | tf_op jit(solution)/shard_map/ppermute | solution.py:430
  27.6 1.6 %shard_map.165 = (f32[128,256]{1,0:T(8,128)S(1)}, bf16[144,256]{1,0:T(8,128)(2,1)S(1)}) custom-call(bf16[384,128]{1,0:T(8,128)(2,1)S(1)} %get-tuple-element.18.refs_0_, bf16[384,128]{1,0:T(8,128)(2,1)S(1)} %collective-permute-done.1.refs_1_, bf16[1024,128]{1,0:T(8,128)(2,1)S(1)} %collective-permute-done.2.refs_1_.refs_2_, ...), custom_call_target="tpu_custom_call" | custom-call | flops 1 | bytes 1 | tf_op jit(solution)/shard_map/pallas_call | solution.py:468
  29.1 1.0 %collective-permute-start.10 = (bf16[144,256]{1,0:T(8,128)(2,1)S(1)}, bf16[144,256]{1,0:T(8,128)(2,1)S(1)}, u32[]{:S(2)}, u32[]{:S(2)}) collective-permute-start(bf16[144,256]{1,0:T(8,128)(2,1)S(1)} %get-tuple-element.28.refs_0_.refs_2_), channel_id=1, source_target_pairs={{0,1},{1,0},{2,3},{3,2},{4,5},{5,4},{6,7},{7,6},{8,9},{9,8},{10,11... | collective-permute-start | bytes 221192 | tf_op jit(solution)/shard_map/ppermute | solution.py:430
  30.1 1.5 %shard_map.166.refs_2_.refs_5_ = f32[32,32,128]{2,1,0:T(8,128)S(1)} custom-call(bf16[1024,128]{1,0:T(8,128)(2,1)S(1)} %get-tuple-element.25.refs_0_, bf16[1024,128]{1,0:T(8,128)(2,1)S(1)} %get-tuple-element.23.refs_1_.refs_0_, bf16[1024,128]{1,0:T(8,128)(2,1)S(1)} %collective-permute-done.9.refs_2_, ...), custom_call_target="tpu_custom_call" | custom-call | flops 1 | bytes 1 | tf_op jit(solution)/shard_map/pallas_call | solution.py:468
  31.6 1.9 %collective-permute-done.10.refs_1_ = bf16[144,256]{1,0:T(8,128)(2,1)S(1)} collective-permute-done((bf16[144,256]{1,0:T(8,128)(2,1)S(1)}, bf16[144,256]{1,0:T(8,128)(2,1)S(1)}, u32[]{:S(2)}, u32[]{:S(2)}) %collective-permute-start.10) | collective-permute-done | bytes 73760 | tf_op jit(solution)/shard_map/ppermute | solution.py:430
  33.7 1.6 %shard_map.168.refs_8_.refs_1_ = f32[32,32,128]{2,1,0:T(8,128)S(1)} custom-call(bf16[1024,128]{1,0:T(8,128)(2,1)S(1)} %get-tuple-element.23.refs_1_.refs_0_, bf16[1024,128]{1,0:T(8,128)(2,1)S(1)} %collective-permute-done.2.refs_1_.refs_2_, bf16[1024,128]{1,0:T(8,128)(2,1)S(1)} %collective-permute-done.8.refs_3_.refs_2_, ...), custom_call_target="tpu_custom_call" | custom-call | flops 1 | bytes 1 | tf_op jit(solution)/shard_map/pallas_call | solution.py:468
  35.3 3.3 %shard_map.169 = bf16[4,32,256]{2,1,0:T(8,128)(2,1)} custom-call(bf16[2,144,256]{2,1,0:T(8,128)(2,1)S(1)} %shard_map.167.refs_0_, bf16[2,144,256]{2,1,0:T(8,128)(2,1)S(1)} %collective-permute-done.11.refs_1_, bf16[144,256]{1,0:T(8,128)(2,1)S(1)} %get-tuple-element.28.refs_0_.refs_2_, f32[128,256]{1,0:T(8,128)S(1)} %get-tuple-element.30.refs_3_, ...), custom_call_target="tpu_custom_call" | custom-call | flops 1 | bytes 1 | tf_op jit(solution)/shard_map/pallas_call | solution.py:468
  38.6 1.9 %collective-permute-done.12.refs_5_ = bf16[32,32,128]{2,1,0:T(8,128)(2,1)S(1)} collective-permute-done((bf16[32,32,128]{2,1,0:T(8,128)(2,1)S(1)}, bf16[32,32,128]{2,1,0:T(8,128)(2,1)S(1)}, u32[]{:S(2)}, u32[]{:S(2)}) %collective-permute-start.12) | collective-permute-done | bytes 262176 | tf_op jit(solution)/shard_map/ppermute | solution.py:430
  40.5 1.7 %shard_map.170 = bf16[32,32,128]{2,1,0:T(8,128)(2,1)} custom-call(s32[128]{0:T(128)S(1)} %copy-done.12, f32[32,32,128]{2,1,0:T(8,128)S(1)} %shard_map.168.refs_8_.refs_1_, bf16[32,32,128]{2,1,0:T(8,128)(2,1)S(1)} %copy-done, f32[1024,128]{1,0:T(8,128)S(1)} %get-tuple-element.31.refs_3_, bf16[128,128]{1,0:T(8,128)(2,1)S(1)} %copy-done.11, ...), custom_call_target="tpu_custom_call" | custom-call | flops 1 | bytes 1 | tf_op jit(solution)/shard_map/pallas_call | solution.py:468
  (43 shorter events, 1.9 us)
Async XLA Ops:
  0.6 9.6 %collective-permute-start = (bf16[32,32,128]{2,1,0:T(8,128)(2,1)}, bf16[32,32,128]{2,1,0:T(8,128)(2,1)S(1)}, u32[]{:S(2)}, u32[]{:S(2)}) collective-permute-start(bf16[32,32,128]{2,1,0:T(8,128)(2,1)} %refs_2_.4), channel_id=1, source_target_pairs={{0,1},{1,5},{2,3},{3,7},{4,0},{5,4},{6,2},{7,6},{8,9},{9,13},{10,1... | collective-permute-start | bytes 786440 | tf_op jit(solution)/shard_map/ppermute | solution.py:517
  3.6 15.0 %collective-permute-start.3 = (bf16[32,32,128]{2,1,0:T(8,128)(2,1)}, bf16[32,32,128]{2,1,0:T(8,128)(2,1)S(1)}, u32[]{:S(2)}, u32[]{:S(2)}) collective-permute-start(bf16[32,32,128]{2,1,0:T(8,128)(2,1)} %refs_2_.4), channel_id=1, source_target_pairs={{0,4},{2,6},{5,1},{7,3},{8,12},{10,14},{13,9},{15,11},{16,20},{18,... | collective-permute-start | bytes 786440 | tf_op jit(solution)/shard_map/ppermute | solution.py:518
  5.7 4.6 %copy-start.1 = (bf16[128,640]{1,0:T(8,128)(2,1)S(1)}, bf16[128,640]{1,0:T(8,128)(2,1)}, u32[]{:S(2)}) copy-start(bf16[128,640]{1,0:T(8,128)(2,1)} %refs_3_.3) | copy-start | bytes 491524
  9.5 3.3 %copy-start.6 = (bf16[144,256]{1,0:T(8,128)(2,1)S(1)}, bf16[144,256]{1,0:T(8,128)(2,1)}, u32[]{:S(2)}) copy-start(bf16[144,256]{1,0:T(8,128)(2,1)} %get-tuple-element.20.refs_4_.refs_8_) | copy-start | bytes 221188
  9.5 7.6 %copy-start = (bf16[32,32,128]{2,1,0:T(8,128)(2,1)S(1)}, bf16[32,32,128]{2,1,0:T(8,128)(2,1)}, u32[]{:S(2)}) copy-start(bf16[32,32,128]{2,1,0:T(8,128)(2,1)} %refs_2_.4) | copy-start | bytes 786436
  11.0 11.0 %collective-permute-start.2 = (bf16[1024,128]{1,0:T(8,128)(2,1)S(1)}, bf16[1024,128]{1,0:T(8,128)(2,1)S(1)}, u32[]{:S(2)}, u32[]{:S(2)}) collective-permute-start(bf16[1024,128]{1,0:T(8,128)(2,1)S(1)} %get-tuple-element.19), channel_id=1, source_target_pairs={{0,1},{1,0},{2,3},{3,2},{4,5},{5,4},{6,7},{7,6},{8,9},{9,8},{10,11... | collective-permute-start | bytes 786440 | tf_op jit(solution)/shard_map/ppermute | solution.py:430
  12.8 7.0 %collective-permute-start.4 = (bf16[144,256]{1,0:T(8,128)(2,1)S(1)}, bf16[144,256]{1,0:T(8,128)(2,1)S(1)}, u32[]{:S(2)}, u32[]{:S(2)}) collective-permute-start(bf16[144,256]{1,0:T(8,128)(2,1)S(1)} %copy-done.6), channel_id=1, source_target_pairs={{0,8},{4,12},{8,0},{12,4},{1,9},{5,13},{9,1},{13,5},{2,10},{6,14},... | collective-permute-start | bytes 221192 | tf_op jit(solution)/shard_map/ppermute | solution.py:430
  15.4 6.3 %collective-permute-start.5 = (bf16[144,256]{1,0:T(8,128)(2,1)S(1)}, bf16[144,256]{1,0:T(8,128)(2,1)S(1)}, u32[]{:S(2)}, u32[]{:S(2)}) collective-permute-start(bf16[144,256]{1,0:T(8,128)(2,1)S(1)} %copy-done.6), channel_id=1, source_target_pairs={{0,12},{4,8},{8,4},{12,0},{1,13},{5,9},{9,5},{13,1},{2,14},{6,10},... | collective-permute-start | bytes 221192 | tf_op jit(solution)/shard_map/ppermute | solution.py:430
  16.9 5.1 %collective-permute-start.6 = (bf16[144,256]{1,0:T(8,128)(2,1)S(1)}, bf16[144,256]{1,0:T(8,128)(2,1)S(1)}, u32[]{:S(2)}, u32[]{:S(2)}) collective-permute-start(bf16[144,256]{1,0:T(8,128)(2,1)S(1)} %copy-done.6), channel_id=1, source_target_pairs={{0,4},{4,0},{8,12},{12,8},{1,5},{5,1},{9,13},{13,9},{2,6},{6,2},{1... | collective-permute-start | bytes 221192 | tf_op jit(solution)/shard_map/ppermute | solution.py:430
  18.6 4.0 %collective-permute-start.8 = (bf16[1024,128]{1,0:T(8,128)(2,1)S(1)}, bf16[1024,128]{1,0:T(8,128)(2,1)S(1)}, u32[]{:S(2)}, u32[]{:S(2)}) collective-permute-start(bf16[1024,128]{1,0:T(8,128)(2,1)S(1)} %get-tuple-element.23.refs_1_.refs_0_), channel_id=1, source_target_pairs={{0,2},{2,0},{1,3},{3,1},{4,6},{6,4},{5,7},{7,5},{8,10},{10,8},{9,1... | collective-permute-start | bytes 786440 | tf_op jit(solution)/shard_map/ppermute | solution.py:430
  19.8 2.7 %collective-permute-start.9 = (bf16[1024,128]{1,0:T(8,128)(2,1)S(1)}, bf16[1024,128]{1,0:T(8,128)(2,1)S(1)}, u32[]{:S(2)}, u32[]{:S(2)}) collective-permute-start(bf16[1024,128]{1,0:T(8,128)(2,1)S(1)} %get-tuple-element.25.refs_0_), channel_id=1, source_target_pairs={{0,2},{2,0},{1,3},{3,1},{4,6},{6,4},{5,7},{7,5},{8,10},{10,8},{9,1... | collective-permute-start | bytes 786440 | tf_op jit(solution)/shard_map/ppermute | solution.py:430
  22.0 2.1 %collective-permute-start.7 = (bf16[1024,128]{1,0:T(8,128)(2,1)S(1)}, bf16[1024,128]{1,0:T(8,128)(2,1)S(1)}, u32[]{:S(2)}, u32[]{:S(2)}) collective-permute-start(bf16[1024,128]{1,0:T(8,128)(2,1)S(1)} %collective-permute-done.2.refs_1_.refs_2_), channel_id=1, source_target_pairs={{0,2},{2,0},{1,3},{3,1},{4,6},{6,4},{5,7},{7,5},{8,10},{10,8},{9,1... | collective-permute-start | bytes 786440 | tf_op jit(solution)/shard_map/ppermute | solution.py:430
  22.0 5.5 %collective-permute-start.1 = (bf16[384,128]{1,0:T(8,128)(2,1)S(1)}, bf16[384,128]{1,0:T(8,128)(2,1)S(1)}, u32[]{:S(2)}, u32[]{:S(2)}) collective-permute-start(bf16[384,128]{1,0:T(8,128)(2,1)S(1)} %get-tuple-element.18.refs_0_), channel_id=1, source_target_pairs={{0,2},{2,0},{1,3},{3,1},{4,6},{6,4},{5,7},{7,5},{8,10},{10,8},{9,1... | collective-permute-start | bytes 294920 | tf_op jit(solution)/shard_map/ppermute | solution.py:430
  24.1 3.5 %copy-start.2 = (bf16[256,1024]{1,0:T(8,128)(2,1)S(1)}, bf16[256,1024]{1,0:T(8,128)(2,1)}, u32[]{:S(2)}) copy-start(bf16[256,1024]{1,0:T(8,128)(2,1)} %refs_10_.1) | copy-start | bytes 1572868
  24.1 3.5 %copy-start.7 = (bf16[256,256]{1,0:T(8,128)(2,1)S(1)}, bf16[256,256]{1,0:T(8,128)(2,1)}, u32[]{:S(2)}) copy-start(bf16[256,256]{1,0:T(8,128)(2,1)} %refs_11_.1) | copy-start | bytes 393220
  24.1 3.5 %copy-start.9 = (f32[128,256]{1,0:T(8,128)S(1)}, f32[128,256]{1,0:T(8,128)}, u32[]{:S(2)}) copy-start(f32[128,256]{1,0:T(8,128)} %get-tuple-element.22.refs_9_) | copy-start | bytes 393220
  25.6 14.8 %collective-permute-start.12 = (bf16[32,32,128]{2,1,0:T(8,128)(2,1)S(1)}, bf16[32,32,128]{2,1,0:T(8,128)(2,1)S(1)}, u32[]{:S(2)}, u32[]{:S(2)}) collective-permute-start(bf16[32,32,128]{2,1,0:T(8,128)(2,1)S(1)} %shard_map.164.refs_12_), channel_id=1, source_target_pairs={{0,8},{4,12},{8,0},{12,4},{1,9},{5,13},{9,1},{13,5},{2,10},{6,14},... | collective-permute-start | bytes 786440 | tf_op jit(solution)/shard_map/ppermute | solution.py:430
  29.1 4.4 %collective-permute-start.10 = (bf16[144,256]{1,0:T(8,128)(2,1)S(1)}, bf16[144,256]{1,0:T(8,128)(2,1)S(1)}, u32[]{:S(2)}, u32[]{:S(2)}) collective-permute-start(bf16[144,256]{1,0:T(8,128)(2,1)S(1)} %get-tuple-element.28.refs_0_.refs_2_), channel_id=1, source_target_pairs={{0,1},{1,0},{2,3},{3,2},{4,5},{5,4},{6,7},{7,6},{8,9},{9,8},{10,11... | collective-permute-start | bytes 221192 | tf_op jit(solution)/shard_map/ppermute | solution.py:430
  33.5 1.7 %copy-start.3 = (bf16[256,1024]{1,0:T(8,128)(2,1)S(1)}, bf16[256,1024]{1,0:T(8,128)(2,1)}, u32[]{:S(2)}) copy-start(bf16[256,1024]{1,0:T(8,128)(2,1)} %refs_4_.6) | copy-start | bytes 1572868
  33.5 1.7 %copy-start.4 = (bf16[256,1024]{1,0:T(8,128)(2,1)S(1)}, bf16[256,1024]{1,0:T(8,128)(2,1)}, u32[]{:S(2)}) copy-start(bf16[256,1024]{1,0:T(8,128)(2,1)} %refs_6_.1) | copy-start | bytes 1572868
  33.5 1.7 %copy-start.5 = (bf16[1024,256]{1,0:T(8,128)(2,1)S(1)}, bf16[1024,256]{1,0:T(8,128)(2,1)}, u32[]{:S(2)}) copy-start(bf16[1024,256]{1,0:T(8,128)(2,1)} %refs_7_.1) | copy-start | bytes 1572868
  33.6 1.7 %copy-start.8 = (bf16[256,256]{1,0:T(8,128)(2,1)S(1)}, bf16[256,256]{1,0:T(8,128)(2,1)}, u32[]{:S(2)}) copy-start(bf16[256,256]{1,0:T(8,128)(2,1)} %refs_5_.1) | copy-start | bytes 393220
  33.6 1.7 %collective-permute-start.11 = (bf16[2,144,256]{2,1,0:T(8,128)(2,1)S(1)}, bf16[2,144,256]{2,1,0:T(8,128)(2,1)S(1)}, u32[]{:S(2)}, u32[]{:S(2)}) collective-permute-start(bf16[2,144,256]{2,1,0:T(8,128)(2,1)S(1)} %shard_map.167.refs_0_), channel_id=1, source_target_pairs={{0,2},{2,0},{1,3},{3,1},{4,6},{6,4},{5,7},{7,5},{8,10},{10,8},{9,1... | collective-permute-start | bytes 442376 | tf_op jit(solution)/shard_map/ppermute | solution.py:430
  35.3 5.2 %copy-start.11 = (bf16[128,128]{1,0:T(8,128)(2,1)S(1)}, bf16[128,128]{1,0:T(8,128)(2,1)}, u32[]{:S(2)}) copy-start(bf16[128,128]{1,0:T(8,128)(2,1)} %refs_4_.7) | copy-start | bytes 98308
  (3 other events, 2.2 us)

commit v5 on v4

--- a/solution.py
+++ b/solution.py
@@ -206,12 +206,12 @@
 
 
 def store_terms(logit, out, start):
-    heads, count = logit.shape
     lanes = out.shape[1]
-    for index, term in enumerate(split(logit)):
-        for part in range(count // lanes):
-            base = start + (index * (count // lanes) + part) * heads
-            out[base : base + heads, :] = term[:, part * lanes : (part + 1) * lanes]
+    parts = [logit[:, first : first + lanes] for first in range(0, logit.shape[1], lanes)]
+    values = jnp.concatenate(parts, axis=0)
+    held = values.shape[0]
+    for index, term in enumerate(split(values)):
+        out[start + index * held : start + (index + 1) * held, :] = term
 
 
 def first_kernel(count, *refs):

time: 42.4 us -> 42.4 us (level)
  no operation moved by 1% of the time
where the time goes in v5:
time: 42.4 us; the launch traced here: 42.2 us
  Pallas kernels  18.5 us (44%)
  starting transfers between devices  15.2 us (36%)
  waiting for transfers between devices  6.13 us (14%)
  local copies, waits for them, and re-layouts  1.52 us (4%)
  between operations  0.88 us (2%)
    pallas_call x13, Pallas kernels, run(): pl.pallas_call(ordered, out_shape=out_shape, in_specs=[pl.BlockSpec(memor...  18.5 us
    ppermute x11, starting transfers between devices, flip(): lax.ppermute(block, axis, [(i, i ^ bit) for i in range(lax.axis_size(axis...  10.2 us
    ppermute x11, waiting for transfers between devices, flip(): lax.ppermute(block, axis, [(i, i ^ bit) for i in range(lax.axis_size(axis...  5.39 us
    ppermute x1, starting transfers between devices, turn_pairs(): lax.ppermute(pairs, ALL, [(index(*place), goes(*place)) for place in every])  2.99 us
    ppermute x1, starting transfers between devices, turn_pairs(): lax.ppermute(pairs, ALL, [(index(h, l, br, a), index(h, 1 - l, br, a)) fo...  2.02 us
    unnamed x28, local copies, waits for them, and re-layouts  1.52 us
  transfers between devices with their start and end apart: 13, of which 5 were waited for; matrix products, arithmetic and copies ran while one was open for 0% of the time, Pallas kernels for 40%

profile of v5, /device:TPU:0, one launch (start us, length us, event | category | flops | bytes accessed | tf_op | source)
XLA Modules:
  0.0 42.2 jit_solution(4510142480671639856)
XLA Ops:
  0.6 3.0 %collective-permute-start = (bf16[32,32,128]{2,1,0:T(8,128)(2,1)}, bf16[32,32,128]{2,1,0:T(8,128)(2,1)S(1)}, u32[]{:S(2)}, u32[]{:S(2)}) collective-permute-start(bf16[32,32,128]{2,1,0:T(8,128)(2,1)} %refs_2_.4), channel_id=1, source_target_pairs={{0,1},{1,5},{2,3},{3,7},{4,0},{5,4},{6,2},{7,6},{8,9},{9,13},{10,1... | collective-permute-start | bytes 786440 | tf_op jit(solution)/shard_map/ppermute | solution.py:517
  3.6 2.0 %collective-permute-start.3 = (bf16[32,32,128]{2,1,0:T(8,128)(2,1)}, bf16[32,32,128]{2,1,0:T(8,128)(2,1)S(1)}, u32[]{:S(2)}, u32[]{:S(2)}) collective-permute-start(bf16[32,32,128]{2,1,0:T(8,128)(2,1)} %refs_2_.4), channel_id=1, source_target_pairs={{0,4},{2,6},{5,1},{7,3},{8,12},{10,14},{13,9},{15,11},{16,20},{18,... | collective-permute-start | bytes 786440 | tf_op jit(solution)/shard_map/ppermute | solution.py:518
  5.7 2.3 %shard_map.158 = (f32[128,256]{1,0:T(8,128)}, bf16[144,256]{1,0:T(8,128)(2,1)}, bf16[192,128]{1,0:T(8,128)(2,1)}) custom-call(bf16[4,32,256]{2,1,0:T(8,128)(2,1)} %refs_0_.4, s32[4,32]{1,0:T(4,128)} %refs_1_.2, s32[4,32]{1,0:T(4,128)} %refs_2_.2, bf16[23,256]{1,0:T(8,128)(2,1)} %refs_3_.2, bf16[32,32,128]{2,1,0:T(8,128)(2,1)} %refs_2_.4, bf16[8,128]{1,0:T(8,128)(2,1)} %bitcast.5), custom_call_target="tpu_custom_call" | custom-call | flops 1 | bytes 1 | tf_op jit(solution)/shard_map/pallas_call | solution.py:468
  8.0 0.6 %copy-done.12 = s32[128]{0:T(128)S(1)} copy-done((s32[128]{0:T(128)S(1)}, s32[128]{0:T(128)}, u32[]{:S(2)}) %copy-start.12) | copy-done | bytes 536
  8.7 0.8 %copy-done.10 = bf16[192,128]{1,0:T(8,128)(2,1)S(1)} copy-done((bf16[192,128]{1,0:T(8,128)(2,1)S(1)}, bf16[192,128]{1,0:T(8,128)(2,1)}, u32[]{:S(2)}) %copy-start.10) | copy-done | bytes 49176
  9.5 0.7 %collective-permute-done.refs_0_.refs_2_ = bf16[32,32,128]{2,1,0:T(8,128)(2,1)S(1)} collective-permute-done((bf16[32,32,128]{2,1,0:T(8,128)(2,1)}, bf16[32,32,128]{2,1,0:T(8,128)(2,1)S(1)}, u32[]{:S(2)}, u32[]{:S(2)}) %collective-permute-start) | collective-permute-done | bytes 262176 | tf_op jit(solution)/shard_map/ppermute | solution.py:517
  10.2 0.8 %shard_map.160 = (bf16[1024,128]{1,0:T(8,128)(2,1)S(1)}, bf16[1024,128]{1,0:T(8,128)(2,1)S(1)}, bf16[384,128]{1,0:T(8,128)(2,1)S(1)}) custom-call(bf16[32,32,128]{2,1,0:T(8,128)(2,1)S(1)} %collective-permute-done.refs_0_.refs_2_, bf16[128,640]{1,0:T(8,128)(2,1)S(1)} %copy-done.1, bf16[8,128]{1,0:T(8,128)(2,1)S(1)} %bitcast.6, ...), custom_call_target="tpu_custom_call" | custom-call | flops 1 | bytes 1 | tf_op jit(solution)/shard_map/pallas_call | solution.py:468
  11.0 1.7 %collective-permute-start.2 = (bf16[1024,128]{1,0:T(8,128)(2,1)S(1)}, bf16[1024,128]{1,0:T(8,128)(2,1)S(1)}, u32[]{:S(2)}, u32[]{:S(2)}) collective-permute-start(bf16[1024,128]{1,0:T(8,128)(2,1)S(1)} %get-tuple-element.19), channel_id=1, source_target_pairs={{0,1},{1,0},{2,3},{3,2},{4,5},{5,4},{6,7},{7,6},{8,9},{9,8},{10,11... | collective-permute-start | bytes 786440 | tf_op jit(solution)/shard_map/ppermute | solution.py:430
  12.8 2.6 %collective-permute-start.4 = (bf16[144,256]{1,0:T(8,128)(2,1)S(1)}, bf16[144,256]{1,0:T(8,128)(2,1)S(1)}, u32[]{:S(2)}, u32[]{:S(2)}) collective-permute-start(bf16[144,256]{1,0:T(8,128)(2,1)S(1)} %copy-done.6), channel_id=1, source_target_pairs={{0,8},{4,12},{8,0},{12,4},{1,9},{5,13},{9,1},{13,5},{2,10},{6,14},... | collective-permute-start | bytes 221192 | tf_op jit(solution)/shard_map/ppermute | solution.py:430
  15.4 1.5 %collective-permute-start.5 = (bf16[144,256]{1,0:T(8,128)(2,1)S(1)}, bf16[144,256]{1,0:T(8,128)(2,1)S(1)}, u32[]{:S(2)}, u32[]{:S(2)}) collective-permute-start(bf16[144,256]{1,0:T(8,128)(2,1)S(1)} %copy-done.6), channel_id=1, source_target_pairs={{0,12},{4,8},{8,4},{12,0},{1,13},{5,9},{9,5},{13,1},{2,14},{6,10},... | collective-permute-start | bytes 221192 | tf_op jit(solution)/shard_map/ppermute | solution.py:430
  17.1 1.4 %shard_map.162 = (f32[1024,128]{1,0:T(8,128)S(1)}, f32[32,32,128]{2,1,0:T(8,128)S(1)}, bf16[1024,128]{1,0:T(8,128)(2,1)S(1)}) custom-call(s32[128]{0:T(128)S(1)} %copy-done.12, s32[1,128]{1,0:T(1,128)S(1)} %bitcast.3, bf16[32,32,128]{2,1,0:T(8,128)(2,1)S(1)} %copy-done, bf16[128,640]{1,0:T(8,128)(2,1)S(1)} %copy-done.1), custom_call_target="tpu_custom_call" | custom-call | flops 1 | bytes 1 | tf_op jit(solution)/shard_map/pallas_call | solution.py:468
  18.7 1.1 %shard_map.161.refs_4_ = f32[32,32,128]{2,1,0:T(8,128)S(1)} custom-call(s32[128]{0:T(128)S(1)} %copy-done.12, s32[1,128]{1,0:T(1,128)S(1)} %bitcast.4, bf16[32,32,128]{2,1,0:T(8,128)(2,1)S(1)} %collective-permute-done.refs_0_.refs_2_, bf16[32,32,128]{2,1,0:T(8,128)(2,1)S(1)} %collective-permute-done.3.refs_3_, bf16[128,640]{1,0:T(8,128)(2,1)S(1)} %copy-done.1), custom_call_target="tpu_custom_call" | custom-call | flops 1 | bytes 1 | tf_op jit(solution)/shard_map/pallas_call | solution.py:468
  20.4 1.3 %collective-permute-done.5.refs_7_ = bf16[144,256]{1,0:T(8,128)(2,1)S(1)} collective-permute-done((bf16[144,256]{1,0:T(8,128)(2,1)S(1)}, bf16[144,256]{1,0:T(8,128)(2,1)S(1)}, u32[]{:S(2)}, u32[]{:S(2)}) %collective-permute-start.5) | collective-permute-done | bytes 73760 | tf_op jit(solution)/shard_map/ppermute | solution.py:430
  22.5 1.5 %shard_map.163.refs_5_ = f32[32,32,128]{2,1,0:T(8,128)S(1)} custom-call(bf16[1024,128]{1,0:T(8,128)(2,1)S(1)} %get-tuple-element.25.refs_0_, bf16[1024,128]{1,0:T(8,128)(2,1)S(1)} %get-tuple-element.23.refs_1_.refs_0_, bf16[1024,128]{1,0:T(8,128)(2,1)S(1)} %collective-permute-done.9.refs_2_, bf16[1024,128]{1,0:T(8,128)(2,1)S(1)} %collective-permute-done.8.refs_3_.refs_2_, ...), custom_call_target="tpu_custom_call" | custom-call | flops 1 | bytes 1 | tf_op jit(solution)/shard_map/pallas_call | solution.py:468
  24.1 1.5 %shard_map.164.refs_12_ = bf16[32,32,128]{2,1,0:T(8,128)(2,1)S(1)} custom-call(bf16[1024,128]{1,0:T(8,128)(2,1)S(1)} %get-tuple-element.23.refs_1_.refs_0_, bf16[1024,128]{1,0:T(8,128)(2,1)S(1)} %collective-permute-done.2.refs_1_.refs_2_, bf16[1024,128]{1,0:T(8,128)(2,1)S(1)} %collective-permute-done.8.refs_3_.refs_2_, ...), custom_call_target="tpu_custom_call" | custom-call | flops 1 | bytes 1 | tf_op jit(solution)/shard_map/pallas_call | solution.py:468
  25.6 1.9 %collective-permute-start.12 = (bf16[32,32,128]{2,1,0:T(8,128)(2,1)S(1)}, bf16[32,32,128]{2,1,0:T(8,128)(2,1)S(1)}, u32[]{:S(2)}, u32[]{:S(2)}) collective-permute-start(bf16[32,32,128]{2,1,0:T(8,128)(2,1)S(1)} %shard_map.164.refs_12_), channel_id=1, source_target_pairs={{0,8},{4,12},{8,0},{12,4},{1,9},{5,13},{9,1},{13,5},{2,10},{6,14},... | collective-permute-start | bytes 786440 | tf_op jit(solution)/shard_map/ppermute | solution.py:430
  27.6 1.6 %shard_map.165 = (f32[128,256]{1,0:T(8,128)S(1)}, bf16[144,256]{1,0:T(8,128)(2,1)S(1)}) custom-call(bf16[384,128]{1,0:T(8,128)(2,1)S(1)} %get-tuple-element.18.refs_0_, bf16[384,128]{1,0:T(8,128)(2,1)S(1)} %collective-permute-done.1.refs_1_, bf16[1024,128]{1,0:T(8,128)(2,1)S(1)} %collective-permute-done.2.refs_1_.refs_2_, ...), custom_call_target="tpu_custom_call" | custom-call | flops 1 | bytes 1 | tf_op jit(solution)/shard_map/pallas_call | solution.py:468
  29.1 1.0 %collective-permute-start.10 = (bf16[144,256]{1,0:T(8,128)(2,1)S(1)}, bf16[144,256]{1,0:T(8,128)(2,1)S(1)}, u32[]{:S(2)}, u32[]{:S(2)}) collective-permute-start(bf16[144,256]{1,0:T(8,128)(2,1)S(1)} %get-tuple-element.28.refs_0_.refs_2_), channel_id=1, source_target_pairs={{0,1},{1,0},{2,3},{3,2},{4,5},{5,4},{6,7},{7,6},{8,9},{9,8},{10,11... | collective-permute-start | bytes 221192 | tf_op jit(solution)/shard_map/ppermute | solution.py:430
  30.1 1.5 %shard_map.166.refs_2_.refs_5_ = f32[32,32,128]{2,1,0:T(8,128)S(1)} custom-call(bf16[1024,128]{1,0:T(8,128)(2,1)S(1)} %get-tuple-element.25.refs_0_, bf16[1024,128]{1,0:T(8,128)(2,1)S(1)} %get-tuple-element.23.refs_1_.refs_0_, bf16[1024,128]{1,0:T(8,128)(2,1)S(1)} %collective-permute-done.9.refs_2_, ...), custom_call_target="tpu_custom_call" | custom-call | flops 1 | bytes 1 | tf_op jit(solution)/shard_map/pallas_call | solution.py:468
  31.6 1.9 %collective-permute-done.10.refs_1_ = bf16[144,256]{1,0:T(8,128)(2,1)S(1)} collective-permute-done((bf16[144,256]{1,0:T(8,128)(2,1)S(1)}, bf16[144,256]{1,0:T(8,128)(2,1)S(1)}, u32[]{:S(2)}, u32[]{:S(2)}) %collective-permute-start.10) | collective-permute-done | bytes 73760 | tf_op jit(solution)/shard_map/ppermute | solution.py:430
  33.6 1.6 %shard_map.168.refs_8_.refs_1_ = f32[32,32,128]{2,1,0:T(8,128)S(1)} custom-call(bf16[1024,128]{1,0:T(8,128)(2,1)S(1)} %get-tuple-element.23.refs_1_.refs_0_, bf16[1024,128]{1,0:T(8,128)(2,1)S(1)} %collective-permute-done.2.refs_1_.refs_2_, bf16[1024,128]{1,0:T(8,128)(2,1)S(1)} %collective-permute-done.8.refs_3_.refs_2_, ...), custom_call_target="tpu_custom_call" | custom-call | flops 1 | bytes 1 | tf_op jit(solution)/shard_map/pallas_call | solution.py:468
  35.3 3.3 %shard_map.169 = bf16[4,32,256]{2,1,0:T(8,128)(2,1)} custom-call(bf16[2,144,256]{2,1,0:T(8,128)(2,1)S(1)} %shard_map.167.refs_0_, bf16[2,144,256]{2,1,0:T(8,128)(2,1)S(1)} %collective-permute-done.11.refs_1_, bf16[144,256]{1,0:T(8,128)(2,1)S(1)} %get-tuple-element.28.refs_0_.refs_2_, f32[128,256]{1,0:T(8,128)S(1)} %get-tuple-element.30.refs_3_, ...), custom_call_target="tpu_custom_call" | custom-call | flops 1 | bytes 1 | tf_op jit(solution)/shard_map/pallas_call | solution.py:468
  38.6 1.9 %collective-permute-done.12.refs_5_ = bf16[32,32,128]{2,1,0:T(8,128)(2,1)S(1)} collective-permute-done((bf16[32,32,128]{2,1,0:T(8,128)(2,1)S(1)}, bf16[32,32,128]{2,1,0:T(8,128)(2,1)S(1)}, u32[]{:S(2)}, u32[]{:S(2)}) %collective-permute-start.12) | collective-permute-done | bytes 262176 | tf_op jit(solution)/shard_map/ppermute | solution.py:430
  40.5 1.7 %shard_map.170 = bf16[32,32,128]{2,1,0:T(8,128)(2,1)} custom-call(s32[128]{0:T(128)S(1)} %copy-done.12, f32[32,32,128]{2,1,0:T(8,128)S(1)} %shard_map.168.refs_8_.refs_1_, bf16[32,32,128]{2,1,0:T(8,128)(2,1)S(1)} %copy-done, f32[1024,128]{1,0:T(8,128)S(1)} %get-tuple-element.31.refs_3_, bf16[128,128]{1,0:T(8,128)(2,1)S(1)} %copy-done.11, ...), custom_call_target="tpu_custom_call" | custom-call | flops 1 | bytes 1 | tf_op jit(solution)/shard_map/pallas_call | solution.py:468
  (43 shorter events, 1.9 us)
Async XLA Ops:
  0.6 9.6 %collective-permute-start = (bf16[32,32,128]{2,1,0:T(8,128)(2,1)}, bf16[32,32,128]{2,1,0:T(8,128)(2,1)S(1)}, u32[]{:S(2)}, u32[]{:S(2)}) collective-permute-start(bf16[32,32,128]{2,1,0:T(8,128)(2,1)} %refs_2_.4), channel_id=1, source_target_pairs={{0,1},{1,5},{2,3},{3,7},{4,0},{5,4},{6,2},{7,6},{8,9},{9,13},{10,1... | collective-permute-start | bytes 786440 | tf_op jit(solution)/shard_map/ppermute | solution.py:517
  3.6 14.9 %collective-permute-start.3 = (bf16[32,32,128]{2,1,0:T(8,128)(2,1)}, bf16[32,32,128]{2,1,0:T(8,128)(2,1)S(1)}, u32[]{:S(2)}, u32[]{:S(2)}) collective-permute-start(bf16[32,32,128]{2,1,0:T(8,128)(2,1)} %refs_2_.4), channel_id=1, source_target_pairs={{0,4},{2,6},{5,1},{7,3},{8,12},{10,14},{13,9},{15,11},{16,20},{18,... | collective-permute-start | bytes 786440 | tf_op jit(solution)/shard_map/ppermute | solution.py:518
  5.7 4.6 %copy-start.1 = (bf16[128,640]{1,0:T(8,128)(2,1)S(1)}, bf16[128,640]{1,0:T(8,128)(2,1)}, u32[]{:S(2)}) copy-start(bf16[128,640]{1,0:T(8,128)(2,1)} %refs_3_.3) | copy-start | bytes 491524
  9.5 3.3 %copy-start.6 = (bf16[144,256]{1,0:T(8,128)(2,1)S(1)}, bf16[144,256]{1,0:T(8,128)(2,1)}, u32[]{:S(2)}) copy-start(bf16[144,256]{1,0:T(8,128)(2,1)} %get-tuple-element.20.refs_4_.refs_8_) | copy-start | bytes 221188
  9.5 7.6 %copy-start = (bf16[32,32,128]{2,1,0:T(8,128)(2,1)S(1)}, bf16[32,32,128]{2,1,0:T(8,128)(2,1)}, u32[]{:S(2)}) copy-start(bf16[32,32,128]{2,1,0:T(8,128)(2,1)} %refs_2_.4) | copy-start | bytes 786436
  11.0 11.0 %collective-permute-start.2 = (bf16[1024,128]{1,0:T(8,128)(2,1)S(1)}, bf16[1024,128]{1,0:T(8,128)(2,1)S(1)}, u32[]{:S(2)}, u32[]{:S(2)}) collective-permute-start(bf16[1024,128]{1,0:T(8,128)(2,1)S(1)} %get-tuple-element.19), channel_id=1, source_target_pairs={{0,1},{1,0},{2,3},{3,2},{4,5},{5,4},{6,7},{7,6},{8,9},{9,8},{10,11... | collective-permute-start | bytes 786440 | tf_op jit(solution)/shard_map/ppermute | solution.py:430
  12.8 7.0 %collective-permute-start.4 = (bf16[144,256]{1,0:T(8,128)(2,1)S(1)}, bf16[144,256]{1,0:T(8,128)(2,1)S(1)}, u32[]{:S(2)}, u32[]{:S(2)}) collective-permute-start(bf16[144,256]{1,0:T(8,128)(2,1)S(1)} %copy-done.6), channel_id=1, source_target_pairs={{0,8},{4,12},{8,0},{12,4},{1,9},{5,13},{9,1},{13,5},{2,10},{6,14},... | collective-permute-start | bytes 221192 | tf_op jit(solution)/shard_map/ppermute | solution.py:430
  15.4 6.3 %collective-permute-start.5 = (bf16[144,256]{1,0:T(8,128)(2,1)S(1)}, bf16[144,256]{1,0:T(8,128)(2,1)S(1)}, u32[]{:S(2)}, u32[]{:S(2)}) collective-permute-start(bf16[144,256]{1,0:T(8,128)(2,1)S(1)} %copy-done.6), channel_id=1, source_target_pairs={{0,12},{4,8},{8,4},{12,0},{1,13},{5,9},{9,5},{13,1},{2,14},{6,10},... | collective-permute-start | bytes 221192 | tf_op jit(solution)/shard_map/ppermute | solution.py:430
  16.9 5.1 %collective-permute-start.6 = (bf16[144,256]{1,0:T(8,128)(2,1)S(1)}, bf16[144,256]{1,0:T(8,128)(2,1)S(1)}, u32[]{:S(2)}, u32[]{:S(2)}) collective-permute-start(bf16[144,256]{1,0:T(8,128)(2,1)S(1)} %copy-done.6), channel_id=1, source_target_pairs={{0,4},{4,0},{8,12},{12,8},{1,5},{5,1},{9,13},{13,9},{2,6},{6,2},{1... | collective-permute-start | bytes 221192 | tf_op jit(solution)/shard_map/ppermute | solution.py:430
  18.6 4.0 %collective-permute-start.8 = (bf16[1024,128]{1,0:T(8,128)(2,1)S(1)}, bf16[1024,128]{1,0:T(8,128)(2,1)S(1)}, u32[]{:S(2)}, u32[]{:S(2)}) collective-permute-start(bf16[1024,128]{1,0:T(8,128)(2,1)S(1)} %get-tuple-element.23.refs_1_.refs_0_), channel_id=1, source_target_pairs={{0,2},{2,0},{1,3},{3,1},{4,6},{6,4},{5,7},{7,5},{8,10},{10,8},{9,1... | collective-permute-start | bytes 786440 | tf_op jit(solution)/shard_map/ppermute | solution.py:430
  19.8 2.7 %collective-permute-start.9 = (bf16[1024,128]{1,0:T(8,128)(2,1)S(1)}, bf16[1024,128]{1,0:T(8,128)(2,1)S(1)}, u32[]{:S(2)}, u32[]{:S(2)}) collective-permute-start(bf16[1024,128]{1,0:T(8,128)(2,1)S(1)} %get-tuple-element.25.refs_0_), channel_id=1, source_target_pairs={{0,2},{2,0},{1,3},{3,1},{4,6},{6,4},{5,7},{7,5},{8,10},{10,8},{9,1... | collective-permute-start | bytes 786440 | tf_op jit(solution)/shard_map/ppermute | solution.py:430
  22.0 2.1 %collective-permute-start.7 = (bf16[1024,128]{1,0:T(8,128)(2,1)S(1)}, bf16[1024,128]{1,0:T(8,128)(2,1)S(1)}, u32[]{:S(2)}, u32[]{:S(2)}) collective-permute-start(bf16[1024,128]{1,0:T(8,128)(2,1)S(1)} %collective-permute-done.2.refs_1_.refs_2_), channel_id=1, source_target_pairs={{0,2},{2,0},{1,3},{3,1},{4,6},{6,4},{5,7},{7,5},{8,10},{10,8},{9,1... | collective-permute-start | bytes 786440 | tf_op jit(solution)/shard_map/ppermute | solution.py:430
  22.0 5.5 %collective-permute-start.1 = (bf16[384,128]{1,0:T(8,128)(2,1)S(1)}, bf16[384,128]{1,0:T(8,128)(2,1)S(1)}, u32[]{:S(2)}, u32[]{:S(2)}) collective-permute-start(bf16[384,128]{1,0:T(8,128)(2,1)S(1)} %get-tuple-element.18.refs_0_), channel_id=1, source_target_pairs={{0,2},{2,0},{1,3},{3,1},{4,6},{6,4},{5,7},{7,5},{8,10},{10,8},{9,1... | collective-permute-start | bytes 294920 | tf_op jit(solution)/shard_map/ppermute | solution.py:430
  24.1 3.5 %copy-start.2 = (bf16[256,1024]{1,0:T(8,128)(2,1)S(1)}, bf16[256,1024]{1,0:T(8,128)(2,1)}, u32[]{:S(2)}) copy-start(bf16[256,1024]{1,0:T(8,128)(2,1)} %refs_10_.1) | copy-start | bytes 1572868
  24.1 3.5 %copy-start.7 = (bf16[256,256]{1,0:T(8,128)(2,1)S(1)}, bf16[256,256]{1,0:T(8,128)(2,1)}, u32[]{:S(2)}) copy-start(bf16[256,256]{1,0:T(8,128)(2,1)} %refs_11_.1) | copy-start | bytes 393220
  24.1 3.5 %copy-start.9 = (f32[128,256]{1,0:T(8,128)S(1)}, f32[128,256]{1,0:T(8,128)}, u32[]{:S(2)}) copy-start(f32[128,256]{1,0:T(8,128)} %get-tuple-element.22.refs_9_) | copy-start | bytes 393220
  25.6 14.8 %collective-permute-start.12 = (bf16[32,32,128]{2,1,0:T(8,128)(2,1)S(1)}, bf16[32,32,128]{2,1,0:T(8,128)(2,1)S(1)}, u32[]{:S(2)}, u32[]{:S(2)}) collective-permute-start(bf16[32,32,128]{2,1,0:T(8,128)(2,1)S(1)} %shard_map.164.refs_12_), channel_id=1, source_target_pairs={{0,8},{4,12},{8,0},{12,4},{1,9},{5,13},{9,1},{13,5},{2,10},{6,14},... | collective-permute-start | bytes 786440 | tf_op jit(solution)/shard_map/ppermute | solution.py:430
  29.1 4.4 %collective-permute-start.10 = (bf16[144,256]{1,0:T(8,128)(2,1)S(1)}, bf16[144,256]{1,0:T(8,128)(2,1)S(1)}, u32[]{:S(2)}, u32[]{:S(2)}) collective-permute-start(bf16[144,256]{1,0:T(8,128)(2,1)S(1)} %get-tuple-element.28.refs_0_.refs_2_), channel_id=1, source_target_pairs={{0,1},{1,0},{2,3},{3,2},{4,5},{5,4},{6,7},{7,6},{8,9},{9,8},{10,11... | collective-permute-start | bytes 221192 | tf_op jit(solution)/shard_map/ppermute | solution.py:430
  33.5 1.7 %copy-start.3 = (bf16[256,1024]{1,0:T(8,128)(2,1)S(1)}, bf16[256,1024]{1,0:T(8,128)(2,1)}, u32[]{:S(2)}) copy-start(bf16[256,1024]{1,0:T(8,128)(2,1)} %refs_4_.6) | copy-start | bytes 1572868
  33.5 1.7 %copy-start.4 = (bf16[256,1024]{1,0:T(8,128)(2,1)S(1)}, bf16[256,1024]{1,0:T(8,128)(2,1)}, u32[]{:S(2)}) copy-start(bf16[256,1024]{1,0:T(8,128)(2,1)} %refs_6_.1) | copy-start | bytes 1572868
  33.5 1.7 %copy-start.5 = (bf16[1024,256]{1,0:T(8,128)(2,1)S(1)}, bf16[1024,256]{1,0:T(8,128)(2,1)}, u32[]{:S(2)}) copy-start(bf16[1024,256]{1,0:T(8,128)(2,1)} %refs_7_.1) | copy-start | bytes 1572868
  33.6 1.7 %copy-start.8 = (bf16[256,256]{1,0:T(8,128)(2,1)S(1)}, bf16[256,256]{1,0:T(8,128)(2,1)}, u32[]{:S(2)}) copy-start(bf16[256,256]{1,0:T(8,128)(2,1)} %refs_5_.1) | copy-start | bytes 393220
  33.6 1.7 %collective-permute-start.11 = (bf16[2,144,256]{2,1,0:T(8,128)(2,1)S(1)}, bf16[2,144,256]{2,1,0:T(8,128)(2,1)S(1)}, u32[]{:S(2)}, u32[]{:S(2)}) collective-permute-start(bf16[2,144,256]{2,1,0:T(8,128)(2,1)S(1)} %shard_map.167.refs_0_), channel_id=1, source_target_pairs={{0,2},{2,0},{1,3},{3,1},{4,6},{6,4},{5,7},{7,5},{8,10},{10,8},{9,1... | collective-permute-start | bytes 442376 | tf_op jit(solution)/shard_map/ppermute | solution.py:430
  35.3 5.2 %copy-start.11 = (bf16[128,128]{1,0:T(8,128)(2,1)S(1)}, bf16[128,128]{1,0:T(8,128)(2,1)}, u32[]{:S(2)}) copy-start(bf16[128,128]{1,0:T(8,128)(2,1)} %refs_4_.7) | copy-start | bytes 98308
  (3 other events, 2.2 us)

commit v6 on v5

--- a/solution.py
+++ b/solution.py
@@ -588,7 +588,7 @@
         cube = shape(couple_features.shape, f32)
         scratch = [pltpu.VMEM(couple_features.shape, f32)]
         far = call(far_kernel, cube, smem=1)(*presence, turned, crossed, trimul_entry_matrix)
-        ready = lax.optimization_barrier((passed, far, row_blocks[2], row_blocks[3], row_blocks[1]))[0]
+        ready = lax.optimization_barrier((passed, row_blocks[2], row_blocks[3], row_blocks[1]))[0]
         other_passed = flip(ready, "br")
         nearest = lax.optimization_barrier((near, passed, far))[0]
         early = lambda other_half, right: call(

time: 42.4 us -> 45.4 us (1.071)
  starting transfers between devices: 15.2 us -> 17.8 us
    ppermute x11, waiting for transfers between devices: 5.39 us -> 1.75 us  [flip(): lax.ppermute(block, axis, [(i, i ^ bit) for i in range(lax.axis_size(axis...]
    ppermute x1, waiting for transfers between devices: 0.74 us -> 2.78 us  [turn_pairs(): lax.ppermute(pairs, ALL, [(index(*place), goes(*place)) for place in every])]
    ppermute x1, waiting for transfers between devices: 0.01 us -> 1.76 us  [turn_pairs(): lax.ppermute(pairs, ALL, [(index(h, l, br, a), index(h, 1 - l, br, a)) fo...]
    ppermute x1, starting transfers between devices: 2.02 us -> 3.7 us  [turn_pairs(): lax.ppermute(pairs, ALL, [(index(h, l, br, a), index(h, 1 - l, br, a)) fo...]
    ppermute x11, starting transfers between devices: 10.2 us -> 11.1 us  [flip(): lax.ppermute(block, axis, [(i, i ^ bit) for i in range(lax.axis_size(axis...]
  transfers between devices with their start and end apart: 13 -> 13, of which waited for: 5 -> 3; matrix products, arithmetic and copies ran while one was open for 0% -> 0% of each run, Pallas kernels for 40% -> 35%
where the time goes in v6:
time: 45.4 us; the launch traced here: 45.1 us
  Pallas kernels  18.5 us (41%)
  starting transfers between devices  17.8 us (39%)
  waiting for transfers between devices  6.3 us (14%)
  local copies, waits for them, and re-layouts  1.51 us (3%)
  between operations  0.89 us (2%)
    pallas_call x13, Pallas kernels, run(): pl.pallas_call(ordered, out_shape=out_shape, in_specs=[pl.BlockSpec(memor...  18.5 us
    ppermute x11, starting transfers between devices, flip(): lax.ppermute(block, axis, [(i, i ^ bit) for i in range(lax.axis_size(axis...  11.1 us
    ppermute x1, starting transfers between devices, turn_pairs(): lax.ppermute(pairs, ALL, [(index(h, l, br, a), index(h, 1 - l, br, a)) fo...  3.7 us
    ppermute x1, starting transfers between devices, turn_pairs(): lax.ppermute(pairs, ALL, [(index(*place), goes(*place)) for place in every])  2.99 us
    ppermute x1, waiting for transfers between devices, turn_pairs(): lax.ppermute(pairs, ALL, [(index(*place), goes(*place)) for place in every])  2.78 us
    ppermute x1, waiting for transfers between devices, turn_pairs(): lax.ppermute(pairs, ALL, [(index(h, l, br, a), index(h, 1 - l, br, a)) fo...  1.76 us
    ppermute x11, waiting for transfers between devices, flip(): lax.ppermute(block, axis, [(i, i ^ bit) for i in range(lax.axis_size(axis...  1.75 us
    unnamed x28, local copies, waits for them, and re-layouts  1.51 us
  transfers between devices with their start and end apart: 13, of which 3 were waited for; matrix products, arithmetic and copies ran while one was open for 0% of the time, Pallas kernels for 35%

profile of v6, /device:TPU:0, one launch (start us, length us, event | category | flops | bytes accessed | tf_op | source)
XLA Modules:
  0.0 45.1 jit_solution(7679297719073213550)
XLA Ops:
  0.6 3.0 %collective-permute-start = (bf16[32,32,128]{2,1,0:T(8,128)(2,1)}, bf16[32,32,128]{2,1,0:T(8,128)(2,1)S(1)}, u32[]{:S(2)}, u32[]{:S(2)}) collective-permute-start(bf16[32,32,128]{2,1,0:T(8,128)(2,1)} %refs_2_.4), channel_id=1, source_target_pairs={{0,1},{1,5},{2,3},{3,7},{4,0},{5,4},{6,2},{7,6},{8,9},{9,13},{10,1... | collective-permute-start | bytes 786440 | tf_op jit(solution)/shard_map/ppermute | solution.py:517
  3.6 2.3 %shard_map.158 = (f32[128,256]{1,0:T(8,128)}, bf16[144,256]{1,0:T(8,128)(2,1)}, bf16[192,128]{1,0:T(8,128)(2,1)}) custom-call(bf16[4,32,256]{2,1,0:T(8,128)(2,1)} %refs_0_.4, s32[4,32]{1,0:T(4,128)} %refs_1_.2, s32[4,32]{1,0:T(4,128)} %refs_2_.2, bf16[23,256]{1,0:T(8,128)(2,1)} %refs_3_.2, bf16[32,32,128]{2,1,0:T(8,128)(2,1)} %refs_2_.4, bf16[8,128]{1,0:T(8,128)(2,1)} %bitcast.5), custom_call_target="tpu_custom_call" | custom-call | flops 1 | bytes 1 | tf_op jit(solution)/shard_map/pallas_call | solution.py:468
  6.0 0.6 %copy-done.12 = s32[128]{0:T(128)S(1)} copy-done((s32[128]{0:T(128)S(1)}, s32[128]{0:T(128)}, u32[]{:S(2)}) %copy-start.12) | copy-done | bytes 536
  6.6 0.8 %copy-done.10 = bf16[192,128]{1,0:T(8,128)(2,1)S(1)} copy-done((bf16[192,128]{1,0:T(8,128)(2,1)S(1)}, bf16[192,128]{1,0:T(8,128)(2,1)}, u32[]{:S(2)}) %copy-start.10) | copy-done | bytes 49176
  7.4 2.8 %collective-permute-done.refs_0_.refs_2_ = bf16[32,32,128]{2,1,0:T(8,128)(2,1)S(1)} collective-permute-done((bf16[32,32,128]{2,1,0:T(8,128)(2,1)}, bf16[32,32,128]{2,1,0:T(8,128)(2,1)S(1)}, u32[]{:S(2)}, u32[]{:S(2)}) %collective-permute-start) | collective-permute-done | bytes 262176 | tf_op jit(solution)/shard_map/ppermute | solution.py:517
  10.2 0.8 %shard_map.160 = (bf16[1024,128]{1,0:T(8,128)(2,1)S(1)}, bf16[1024,128]{1,0:T(8,128)(2,1)S(1)}, bf16[384,128]{1,0:T(8,128)(2,1)S(1)}) custom-call(bf16[32,32,128]{2,1,0:T(8,128)(2,1)S(1)} %collective-permute-done.refs_0_.refs_2_, bf16[128,640]{1,0:T(8,128)(2,1)S(1)} %copy-done.1, bf16[8,128]{1,0:T(8,128)(2,1)S(1)} %bitcast.6, ...), custom_call_target="tpu_custom_call" | custom-call | flops 1 | bytes 1 | tf_op jit(solution)/shard_map/pallas_call | solution.py:468
  11.0 1.7 %collective-permute-start.2 = (bf16[1024,128]{1,0:T(8,128)(2,1)S(1)}, bf16[1024,128]{1,0:T(8,128)(2,1)S(1)}, u32[]{:S(2)}, u32[]{:S(2)}) collective-permute-start(bf16[1024,128]{1,0:T(8,128)(2,1)S(1)} %get-tuple-element.19), channel_id=1, source_target_pairs={{0,1},{1,0},{2,3},{3,2},{4,5},{5,4},{6,7},{7,6},{8,9},{9,8},{10,11... | collective-permute-start | bytes 786440 | tf_op jit(solution)/shard_map/ppermute | solution.py:430
  12.8 2.6 %collective-permute-start.3 = (bf16[144,256]{1,0:T(8,128)(2,1)S(1)}, bf16[144,256]{1,0:T(8,128)(2,1)S(1)}, u32[]{:S(2)}, u32[]{:S(2)}) collective-permute-start(bf16[144,256]{1,0:T(8,128)(2,1)S(1)} %copy-done.6), channel_id=1, source_target_pairs={{0,8},{4,12},{8,0},{12,4},{1,9},{5,13},{9,1},{13,5},{2,10},{6,14},... | collective-permute-start | bytes 221192 | tf_op jit(solution)/shard_map/ppermute | solution.py:430
  15.4 1.3 %collective-permute-start.4 = (bf16[144,256]{1,0:T(8,128)(2,1)S(1)}, bf16[144,256]{1,0:T(8,128)(2,1)S(1)}, u32[]{:S(2)}, u32[]{:S(2)}) collective-permute-start(bf16[144,256]{1,0:T(8,128)(2,1)S(1)} %copy-done.6), channel_id=1, source_target_pairs={{0,12},{4,8},{8,4},{12,0},{1,13},{5,9},{9,5},{13,1},{2,14},{6,10},... | collective-permute-start | bytes 221192 | tf_op jit(solution)/shard_map/ppermute | solution.py:430
  16.9 3.7 %collective-permute-start.8 = (bf16[32,32,128]{2,1,0:T(8,128)(2,1)S(1)}, bf16[32,32,128]{2,1,0:T(8,128)(2,1)S(1)}, u32[]{:S(2)}, u32[]{:S(2)}) collective-permute-start(bf16[32,32,128]{2,1,0:T(8,128)(2,1)S(1)} %copy-done), channel_id=1, source_target_pairs={{0,4},{2,6},{5,1},{7,3},{8,12},{10,14},{13,9},{15,11},{16,20},{18,... | collective-permute-start | bytes 786440 | tf_op jit(solution)/shard_map/ppermute | solution.py:518
  20.6 1.5 %shard_map.162 = (f32[1024,128]{1,0:T(8,128)S(1)}, f32[32,32,128]{2,1,0:T(8,128)S(1)}, bf16[1024,128]{1,0:T(8,128)(2,1)S(1)}) custom-call(s32[128]{0:T(128)S(1)} %copy-done.12, s32[1,128]{1,0:T(1,128)S(1)} %bitcast.3, bf16[32,32,128]{2,1,0:T(8,128)(2,1)S(1)} %copy-done, bf16[128,640]{1,0:T(8,128)(2,1)S(1)} %copy-done.1), custom_call_target="tpu_custom_call" | custom-call | flops 1 | bytes 1 | tf_op jit(solution)/shard_map/pallas_call | solution.py:468
  22.2 0.5 %collective-permute-start.9 = (bf16[1024,128]{1,0:T(8,128)(2,1)S(1)}, bf16[1024,128]{1,0:T(8,128)(2,1)S(1)}, u32[]{:S(2)}, u32[]{:S(2)}) collective-permute-start(bf16[1024,128]{1,0:T(8,128)(2,1)S(1)} %get-tuple-element.25.refs_0_), channel_id=1, source_target_pairs={{0,2},{2,0},{1,3},{3,1},{4,6},{6,4},{5,7},{7,5},{8,10},{10,8},{9,1... | collective-permute-start | bytes 786440 | tf_op jit(solution)/shard_map/ppermute | solution.py:430
  23.2 1.8 %collective-permute-done.8.refs_3_ = bf16[32,32,128]{2,1,0:T(8,128)(2,1)S(1)} collective-permute-done((bf16[32,32,128]{2,1,0:T(8,128)(2,1)S(1)}, bf16[32,32,128]{2,1,0:T(8,128)(2,1)S(1)}, u32[]{:S(2)}, u32[]{:S(2)}) %collective-permute-start.8) | collective-permute-done | bytes 262176 | tf_op jit(solution)/shard_map/ppermute | solution.py:518
  25.0 1.1 %shard_map.161.refs_4_ = f32[32,32,128]{2,1,0:T(8,128)S(1)} custom-call(s32[128]{0:T(128)S(1)} %copy-done.12, s32[1,128]{1,0:T(1,128)S(1)} %bitcast.4, bf16[32,32,128]{2,1,0:T(8,128)(2,1)S(1)} %collective-permute-done.refs_0_.refs_2_, bf16[32,32,128]{2,1,0:T(8,128)(2,1)S(1)} %collective-permute-done.8.refs_3_, bf16[128,640]{1,0:T(8,128)(2,1)S(1)} %copy-done.1), custom_call_target="tpu_custom_call" | custom-call | flops 1 | bytes 1 | tf_op jit(solution)/shard_map/pallas_call | solution.py:468
  26.2 1.6 %shard_map.163.refs_5_ = f32[32,32,128]{2,1,0:T(8,128)S(1)} custom-call(bf16[1024,128]{1,0:T(8,128)(2,1)S(1)} %get-tuple-element.25.refs_0_, bf16[1024,128]{1,0:T(8,128)(2,1)S(1)} %get-tuple-element.23.refs_1_.refs_0_, bf16[1024,128]{1,0:T(8,128)(2,1)S(1)} %collective-permute-done.9.refs_2_, bf16[1024,128]{1,0:T(8,128)(2,1)S(1)} %collective-permute-done.7.refs_3_.refs_2_, ...), custom_call_target="tpu_custom_call" | custom-call | flops 1 | bytes 1 | tf_op jit(solution)/shard_map/pallas_call | solution.py:468
  27.8 1.5 %shard_map.164.refs_12_ = bf16[32,32,128]{2,1,0:T(8,128)(2,1)S(1)} custom-call(bf16[1024,128]{1,0:T(8,128)(2,1)S(1)} %get-tuple-element.23.refs_1_.refs_0_, bf16[1024,128]{1,0:T(8,128)(2,1)S(1)} %collective-permute-done.2.refs_1_.refs_2_, bf16[1024,128]{1,0:T(8,128)(2,1)S(1)} %collective-permute-done.7.refs_3_.refs_2_, ...), custom_call_target="tpu_custom_call" | custom-call | flops 1 | bytes 1 | tf_op jit(solution)/shard_map/pallas_call | solution.py:468
  29.3 3.0 %collective-permute-start.12 = (bf16[32,32,128]{2,1,0:T(8,128)(2,1)S(1)}, bf16[32,32,128]{2,1,0:T(8,128)(2,1)S(1)}, u32[]{:S(2)}, u32[]{:S(2)}) collective-permute-start(bf16[32,32,128]{2,1,0:T(8,128)(2,1)S(1)} %shard_map.164.refs_12_), channel_id=1, source_target_pairs={{0,8},{4,12},{8,0},{12,4},{1,9},{5,13},{9,1},{13,5},{2,10},{6,14},... | collective-permute-start | bytes 786440 | tf_op jit(solution)/shard_map/ppermute | solution.py:430
  32.3 1.6 %shard_map.165 = (f32[128,256]{1,0:T(8,128)S(1)}, bf16[144,256]{1,0:T(8,128)(2,1)S(1)}) custom-call(bf16[384,128]{1,0:T(8,128)(2,1)S(1)} %get-tuple-element.18.refs_0_, bf16[384,128]{1,0:T(8,128)(2,1)S(1)} %collective-permute-done.1.refs_1_, bf16[1024,128]{1,0:T(8,128)(2,1)S(1)} %collective-permute-done.2.refs_1_.refs_2_, ...), custom_call_target="tpu_custom_call" | custom-call | flops 1 | bytes 1 | tf_op jit(solution)/shard_map/pallas_call | solution.py:468
  33.9 1.1 %collective-permute-start.10 = (bf16[144,256]{1,0:T(8,128)(2,1)S(1)}, bf16[144,256]{1,0:T(8,128)(2,1)S(1)}, u32[]{:S(2)}, u32[]{:S(2)}) collective-permute-start(bf16[144,256]{1,0:T(8,128)(2,1)S(1)} %get-tuple-element.28.refs_0_.refs_2_), channel_id=1, source_target_pairs={{0,1},{1,0},{2,3},{3,2},{4,5},{5,4},{6,7},{7,6},{8,9},{9,8},{10,11... | collective-permute-start | bytes 221192 | tf_op jit(solution)/shard_map/ppermute | solution.py:430
  35.0 1.5 %shard_map.166.refs_2_.refs_5_ = f32[32,32,128]{2,1,0:T(8,128)S(1)} custom-call(bf16[1024,128]{1,0:T(8,128)(2,1)S(1)} %get-tuple-element.25.refs_0_, bf16[1024,128]{1,0:T(8,128)(2,1)S(1)} %get-tuple-element.23.refs_1_.refs_0_, bf16[1024,128]{1,0:T(8,128)(2,1)S(1)} %collective-permute-done.9.refs_2_, ...), custom_call_target="tpu_custom_call" | custom-call | flops 1 | bytes 1 | tf_op jit(solution)/shard_map/pallas_call | solution.py:468
  36.5 1.7 %collective-permute-done.10.refs_1_ = bf16[144,256]{1,0:T(8,128)(2,1)S(1)} collective-permute-done((bf16[144,256]{1,0:T(8,128)(2,1)S(1)}, bf16[144,256]{1,0:T(8,128)(2,1)S(1)}, u32[]{:S(2)}, u32[]{:S(2)}) %collective-permute-start.10) | collective-permute-done | bytes 73760 | tf_op jit(solution)/shard_map/ppermute | solution.py:430
  38.4 1.6 %shard_map.168.refs_8_.refs_1_ = f32[32,32,128]{2,1,0:T(8,128)S(1)} custom-call(bf16[1024,128]{1,0:T(8,128)(2,1)S(1)} %get-tuple-element.23.refs_1_.refs_0_, bf16[1024,128]{1,0:T(8,128)(2,1)S(1)} %collective-permute-done.2.refs_1_.refs_2_, bf16[1024,128]{1,0:T(8,128)(2,1)S(1)} %collective-permute-done.7.refs_3_.refs_2_, ...), custom_call_target="tpu_custom_call" | custom-call | flops 1 | bytes 1 | tf_op jit(solution)/shard_map/pallas_call | solution.py:468
  40.0 3.3 %shard_map.169 = bf16[4,32,256]{2,1,0:T(8,128)(2,1)} custom-call(bf16[2,144,256]{2,1,0:T(8,128)(2,1)S(1)} %shard_map.167.refs_0_, bf16[2,144,256]{2,1,0:T(8,128)(2,1)S(1)} %collective-permute-done.11.refs_1_, bf16[144,256]{1,0:T(8,128)(2,1)S(1)} %get-tuple-element.28.refs_0_.refs_2_, f32[128,256]{1,0:T(8,128)S(1)} %get-tuple-element.30.refs_3_, ...), custom_call_target="tpu_custom_call" | custom-call | flops 1 | bytes 1 | tf_op jit(solution)/shard_map/pallas_call | solution.py:468
  43.3 1.7 %shard_map.170 = bf16[32,32,128]{2,1,0:T(8,128)(2,1)} custom-call(s32[128]{0:T(128)S(1)} %copy-done.12, f32[32,32,128]{2,1,0:T(8,128)S(1)} %shard_map.168.refs_8_.refs_1_, bf16[32,32,128]{2,1,0:T(8,128)(2,1)S(1)} %copy-done, f32[1024,128]{1,0:T(8,128)S(1)} %get-tuple-element.31.refs_3_, bf16[128,128]{1,0:T(8,128)(2,1)S(1)} %copy-done.11, ...), custom_call_target="tpu_custom_call" | custom-call | flops 1 | bytes 1 | tf_op jit(solution)/shard_map/pallas_call | solution.py:468
  (43 shorter events, 1.0 us)
Async XLA Ops:
  0.6 9.6 %collective-permute-start = (bf16[32,32,128]{2,1,0:T(8,128)(2,1)}, bf16[32,32,128]{2,1,0:T(8,128)(2,1)S(1)}, u32[]{:S(2)}, u32[]{:S(2)}) collective-permute-start(bf16[32,32,128]{2,1,0:T(8,128)(2,1)} %refs_2_.4), channel_id=1, source_target_pairs={{0,1},{1,5},{2,3},{3,7},{4,0},{5,4},{6,2},{7,6},{8,9},{9,13},{10,1... | collective-permute-start | bytes 786440 | tf_op jit(solution)/shard_map/ppermute | solution.py:517
  3.6 6.6 %copy-start.1 = (bf16[128,640]{1,0:T(8,128)(2,1)S(1)}, bf16[128,640]{1,0:T(8,128)(2,1)}, u32[]{:S(2)}) copy-start(bf16[128,640]{1,0:T(8,128)(2,1)} %refs_3_.3) | copy-start | bytes 491524
  7.4 2.8 %copy-start.13 = (bf16[128,8]{0,1:T(8,128)(2,1)S(1)}, bf16[128,8]{0,1:T(8,128)(2,1)}, u32[]{:S(2)}) copy-start(bf16[128,8]{0,1:T(8,128)(2,1)} %param.22) | copy-start | bytes 6148
  7.4 5.3 %copy-start.6 = (bf16[144,256]{1,0:T(8,128)(2,1)S(1)}, bf16[144,256]{1,0:T(8,128)(2,1)}, u32[]{:S(2)}) copy-start(bf16[144,256]{1,0:T(8,128)(2,1)} %get-tuple-element.20.refs_4_.refs_8_) | copy-start | bytes 221188
  7.4 9.5 %copy-start = (bf16[32,32,128]{2,1,0:T(8,128)(2,1)S(1)}, bf16[32,32,128]{2,1,0:T(8,128)(2,1)}, u32[]{:S(2)}) copy-start(bf16[32,32,128]{2,1,0:T(8,128)(2,1)} %refs_2_.4) | copy-start | bytes 786436
  11.0 11.7 %collective-permute-start.2 = (bf16[1024,128]{1,0:T(8,128)(2,1)S(1)}, bf16[1024,128]{1,0:T(8,128)(2,1)S(1)}, u32[]{:S(2)}, u32[]{:S(2)}) collective-permute-start(bf16[1024,128]{1,0:T(8,128)(2,1)S(1)} %get-tuple-element.19), channel_id=1, source_target_pairs={{0,1},{1,0},{2,3},{3,2},{4,5},{5,4},{6,7},{7,6},{8,9},{9,8},{10,11... | collective-permute-start | bytes 786440 | tf_op jit(solution)/shard_map/ppermute | solution.py:430
  12.8 9.3 %collective-permute-start.3 = (bf16[144,256]{1,0:T(8,128)(2,1)S(1)}, bf16[144,256]{1,0:T(8,128)(2,1)S(1)}, u32[]{:S(2)}, u32[]{:S(2)}) collective-permute-start(bf16[144,256]{1,0:T(8,128)(2,1)S(1)} %copy-done.6), channel_id=1, source_target_pairs={{0,8},{4,12},{8,0},{12,4},{1,9},{5,13},{9,1},{13,5},{2,10},{6,14},... | collective-permute-start | bytes 221192 | tf_op jit(solution)/shard_map/ppermute | solution.py:430
  15.4 6.8 %collective-permute-start.4 = (bf16[144,256]{1,0:T(8,128)(2,1)S(1)}, bf16[144,256]{1,0:T(8,128)(2,1)S(1)}, u32[]{:S(2)}, u32[]{:S(2)}) collective-permute-start(bf16[144,256]{1,0:T(8,128)(2,1)S(1)} %copy-done.6), channel_id=1, source_target_pairs={{0,12},{4,8},{8,4},{12,0},{1,13},{5,9},{9,5},{13,1},{2,14},{6,10},... | collective-permute-start | bytes 221192 | tf_op jit(solution)/shard_map/ppermute | solution.py:430
  16.7 6.0 %collective-permute-start.5 = (bf16[144,256]{1,0:T(8,128)(2,1)S(1)}, bf16[144,256]{1,0:T(8,128)(2,1)S(1)}, u32[]{:S(2)}, u32[]{:S(2)}) collective-permute-start(bf16[144,256]{1,0:T(8,128)(2,1)S(1)} %copy-done.6), channel_id=1, source_target_pairs={{0,4},{4,0},{8,12},{12,8},{1,5},{5,1},{9,13},{13,9},{2,6},{6,2},{1... | collective-permute-start | bytes 221192 | tf_op jit(solution)/shard_map/ppermute | solution.py:430
  16.9 8.0 %collective-permute-start.8 = (bf16[32,32,128]{2,1,0:T(8,128)(2,1)S(1)}, bf16[32,32,128]{2,1,0:T(8,128)(2,1)S(1)}, u32[]{:S(2)}, u32[]{:S(2)}) collective-permute-start(bf16[32,32,128]{2,1,0:T(8,128)(2,1)S(1)} %copy-done), channel_id=1, source_target_pairs={{0,4},{2,6},{5,1},{7,3},{8,12},{10,14},{13,9},{15,11},{16,20},{18,... | collective-permute-start | bytes 786440 | tf_op jit(solution)/shard_map/ppermute | solution.py:518
  22.1 4.0 %collective-permute-start.7 = (bf16[1024,128]{1,0:T(8,128)(2,1)S(1)}, bf16[1024,128]{1,0:T(8,128)(2,1)S(1)}, u32[]{:S(2)}, u32[]{:S(2)}) collective-permute-start(bf16[1024,128]{1,0:T(8,128)(2,1)S(1)} %get-tuple-element.23.refs_1_.refs_0_), channel_id=1, source_target_pairs={{0,2},{2,0},{1,3},{3,1},{4,6},{6,4},{5,7},{7,5},{8,10},{10,8},{9,1... | collective-permute-start | bytes 786440 | tf_op jit(solution)/shard_map/ppermute | solution.py:430
  22.2 3.9 %collective-permute-start.9 = (bf16[1024,128]{1,0:T(8,128)(2,1)S(1)}, bf16[1024,128]{1,0:T(8,128)(2,1)S(1)}, u32[]{:S(2)}, u32[]{:S(2)}) collective-permute-start(bf16[1024,128]{1,0:T(8,128)(2,1)S(1)} %get-tuple-element.25.refs_0_), channel_id=1, source_target_pairs={{0,2},{2,0},{1,3},{3,1},{4,6},{6,4},{5,7},{7,5},{8,10},{10,8},{9,1... | collective-permute-start | bytes 786440 | tf_op jit(solution)/shard_map/ppermute | solution.py:430
  22.7 5.0 %collective-permute-start.6 = (bf16[1024,128]{1,0:T(8,128)(2,1)S(1)}, bf16[1024,128]{1,0:T(8,128)(2,1)S(1)}, u32[]{:S(2)}, u32[]{:S(2)}) collective-permute-start(bf16[1024,128]{1,0:T(8,128)(2,1)S(1)} %collective-permute-done.2.refs_1_.refs_2_), channel_id=1, source_target_pairs={{0,2},{2,0},{1,3},{3,1},{4,6},{6,4},{5,7},{7,5},{8,10},{10,8},{9,1... | collective-permute-start | bytes 786440 | tf_op jit(solution)/shard_map/ppermute | solution.py:430
  22.8 9.5 %collective-permute-start.1 = (bf16[384,128]{1,0:T(8,128)(2,1)S(1)}, bf16[384,128]{1,0:T(8,128)(2,1)S(1)}, u32[]{:S(2)}, u32[]{:S(2)}) collective-permute-start(bf16[384,128]{1,0:T(8,128)(2,1)S(1)} %get-tuple-element.18.refs_0_), channel_id=1, source_target_pairs={{0,2},{2,0},{1,3},{3,1},{4,6},{6,4},{5,7},{7,5},{8,10},{10,8},{9,1... | collective-permute-start | bytes 294920 | tf_op jit(solution)/shard_map/ppermute | solution.py:430
  27.7 4.6 %copy-start.2 = (bf16[256,1024]{1,0:T(8,128)(2,1)S(1)}, bf16[256,1024]{1,0:T(8,128)(2,1)}, u32[]{:S(2)}) copy-start(bf16[256,1024]{1,0:T(8,128)(2,1)} %refs_10_.1) | copy-start | bytes 1572868
  27.7 4.6 %copy-start.7 = (bf16[256,256]{1,0:T(8,128)(2,1)S(1)}, bf16[256,256]{1,0:T(8,128)(2,1)}, u32[]{:S(2)}) copy-start(bf16[256,256]{1,0:T(8,128)(2,1)} %refs_11_.1) | copy-start | bytes 393220
  27.7 4.5 %copy-start.9 = (f32[128,256]{1,0:T(8,128)S(1)}, f32[128,256]{1,0:T(8,128)}, u32[]{:S(2)}) copy-start(f32[128,256]{1,0:T(8,128)} %get-tuple-element.22.refs_9_) | copy-start | bytes 393220
  29.3 14.1 %collective-permute-start.12 = (bf16[32,32,128]{2,1,0:T(8,128)(2,1)S(1)}, bf16[32,32,128]{2,1,0:T(8,128)(2,1)S(1)}, u32[]{:S(2)}, u32[]{:S(2)}) collective-permute-start(bf16[32,32,128]{2,1,0:T(8,128)(2,1)S(1)} %shard_map.164.refs_12_), channel_id=1, source_target_pairs={{0,8},{4,12},{8,0},{12,4},{1,9},{5,13},{9,1},{13,5},{2,10},{6,14},... | collective-permute-start | bytes 786440 | tf_op jit(solution)/shard_map/ppermute | solution.py:430
  33.9 4.4 %collective-permute-start.10 = (bf16[144,256]{1,0:T(8,128)(2,1)S(1)}, bf16[144,256]{1,0:T(8,128)(2,1)S(1)}, u32[]{:S(2)}, u32[]{:S(2)}) collective-permute-start(bf16[144,256]{1,0:T(8,128)(2,1)S(1)} %get-tuple-element.28.refs_0_.refs_2_), channel_id=1, source_target_pairs={{0,1},{1,0},{2,3},{3,2},{4,5},{5,4},{6,7},{7,6},{8,9},{9,8},{10,11... | collective-permute-start | bytes 221192 | tf_op jit(solution)/shard_map/ppermute | solution.py:430
  38.2 1.7 %copy-start.3 = (bf16[256,1024]{1,0:T(8,128)(2,1)S(1)}, bf16[256,1024]{1,0:T(8,128)(2,1)}, u32[]{:S(2)}) copy-start(bf16[256,1024]{1,0:T(8,128)(2,1)} %refs_4_.6) | copy-start | bytes 1572868
  38.3 1.7 %copy-start.4 = (bf16[256,1024]{1,0:T(8,128)(2,1)S(1)}, bf16[256,1024]{1,0:T(8,128)(2,1)}, u32[]{:S(2)}) copy-start(bf16[256,1024]{1,0:T(8,128)(2,1)} %refs_6_.1) | copy-start | bytes 1572868
  38.3 1.7 %copy-start.5 = (bf16[1024,256]{1,0:T(8,128)(2,1)S(1)}, bf16[1024,256]{1,0:T(8,128)(2,1)}, u32[]{:S(2)}) copy-start(bf16[1024,256]{1,0:T(8,128)(2,1)} %refs_7_.1) | copy-start | bytes 1572868
  38.3 1.7 %collective-permute-start.11 = (bf16[2,144,256]{2,1,0:T(8,128)(2,1)S(1)}, bf16[2,144,256]{2,1,0:T(8,128)(2,1)S(1)}, u32[]{:S(2)}, u32[]{:S(2)}) collective-permute-start(bf16[2,144,256]{2,1,0:T(8,128)(2,1)S(1)} %shard_map.167.refs_0_), channel_id=1, source_target_pairs={{0,2},{2,0},{1,3},{3,1},{4,6},{6,4},{5,7},{7,5},{8,10},{10,8},{9,1... | collective-permute-start | bytes 442376 | tf_op jit(solution)/shard_map/ppermute | solution.py:430
  40.0 3.3 %copy-start.11 = (bf16[128,128]{1,0:T(8,128)(2,1)S(1)}, bf16[128,128]{1,0:T(8,128)(2,1)}, u32[]{:S(2)}) copy-start(bf16[128,128]{1,0:T(8,128)(2,1)} %refs_4_.7) | copy-start | bytes 98308
  (3 other events, 3.2 us)
